TPU v7x, 128 devices: a whole 4x4x4 slice. The times are simulated.
128 devices in a mesh: ctx: 8 (over y, core), dec: 16 (over z, x).
Axes of the slice: x: 4, y: 4, z: 4, core: 2. Of those that a mesh axis runs over, the one named last changes fastest.
Arguments:
- queries: bfloat16 [16, 1024, 16384], P('dec', 'ctx'), may hold values from -36 to 36
- keys: bfloat16 [16, 1024, 1024], P('dec', 'ctx'), may hold values from -3 to 3
- values: bfloat16 [16, 1024, 1024], P('dec', 'ctx'), may hold values from -4 to 4
- lengths: int32 [16, 4], P('dec'), may hold values from 1 to 512, 1024 in all within a row
- owners: int32 [16, 128, 1], P('dec', 'ctx'), may hold values from 0 to 15; in each aligned block of 16 rows (0 to 15, 16 to 31, ..., all dimensions but the last counted through in order) at most 2 rows name the same one
Outputs:
- attended: bfloat16 [16, 1024, 16384], P('dec', 'ctx')
- cache_keys: bfloat16 [128, 8, 32, 1024], P(None, 'ctx', 'dec')
- cache_values: bfloat16 [128, 8, 32, 1024], P(None, 'ctx', 'dec')
- cache_key_scales: bfloat16 [128, 8, 32, 8], P(None, 'ctx', 'dec')
- cache_value_scales: bfloat16 [128, 8, 32, 8], P(None, 'ctx', 'dec')
Inputs may be any that keep to these rules, and one draw needn't show every extreme that they name: `owners`: at most 2 of the 16 pages of one device go to one decode owner.
All inputs are finite; a program needn't handle non-finite values. Where the computation divides by a largest or mean magnitude, that divisor is 1e-20 or more.
Results may differ from a plain program's by a relative error of at most 0.013.
Values may be sent and summed in bfloat16 or wider, within the bound.
No kernel may reach another device: no remote copies, remote signals or barrier semaphores. Data moves between devices by JAX's collectives and lax.ppermute only.
A program may use at most 128 MiB of HBM per device.

v0:
```python
import math

import jax
import jax.numpy as jnp
from jax import lax
from jax.sharding import PartitionSpec as P

HD = 128
PAGE = 8
CAP = 2


def as_sent(shard):
    return jax.tree.map(lambda a: a.astype(jnp.bfloat16) if a.dtype == jnp.float32 else a, shard)


def hadamard_signs(width):
    row_index = lax.broadcasted_iota(jnp.int32, (width, width), 0)
    col_index = lax.broadcasted_iota(jnp.int32, (width, width), 1)
    common = row_index & col_index
    parity = jnp.zeros((width, width), jnp.int32)
    for bit_number in range(width.bit_length()):
        parity = parity + (common >> bit_number & 1)
    return (1 - 2 * (parity % 2)).astype(jnp.bfloat16)


def rotate_codes(rows_block, width):
    rotated = jnp.dot(rows_block, hadamard_signs(width), preferred_element_type=jnp.float32) * (
        1.0 / math.sqrt(width)
    )
    block_scale = (jnp.max(jnp.abs(rotated), axis=-1) + 1e-06).astype(jnp.bfloat16)
    codes = (rotated / block_scale.astype(jnp.float32)[:, None]).astype(jnp.bfloat16)
    return (codes, block_scale)


def request_of(positions, request_ends):
    return jnp.sum((positions[:, None] >= request_ends[None, :]).astype(jnp.int32), axis=1)


def body(queries, keys, values, lengths, owners):
    ctx_count = lax.axis_size("ctx")
    owner_count = lax.axis_size("dec")
    ctx_index = lax.axis_index("ctx")
    tokens = queries.shape[1]
    head_size = HD
    key_width = keys.shape[2]
    kv_heads = key_width // head_size
    group_size = queries.shape[2] // key_width
    heads_per = kv_heads // ctx_count
    inv_root = 1.0 / math.sqrt(head_size)
    query_heads = (
        queries[0]
        .reshape(tokens, kv_heads, group_size, head_size)
        .transpose(1, 2, 0, 3)
        .reshape(kv_heads, group_size * tokens, head_size)
    )
    query_pos = ctx_index * tokens + jnp.arange(tokens, dtype=jnp.int32)
    request_ends = jnp.cumsum(lengths[0])
    query_req = request_of(query_pos, request_ends)
    initial = (
        jnp.full((kv_heads, group_size * tokens), -1e30, jnp.float32),
        jnp.zeros((kv_heads, group_size * tokens), jnp.float32),
        jnp.zeros((kv_heads, group_size * tokens, head_size), jnp.float32),
    )
    key_piece = lax.all_gather(keys, "ctx", axis=1, tiled=True)
    key_count = key_piece.shape[1]
    key_pos = jnp.arange(key_count, dtype=jnp.int32)
    key_req = request_of(key_pos, request_ends)
    allowed = (
        (key_req[None, :] == query_req[:, None])
        & (key_pos[None, :] <= query_pos[:, None])
        & (key_pos[None, :] >= 0)
    )
    key_heads = key_piece[0].reshape(key_count, kv_heads, head_size).transpose(1, 0, 2)
    value_heads = (
        lax.all_gather(values, "ctx", axis=1, tiled=True)[0]
        .reshape(key_count, kv_heads, head_size)
        .transpose(1, 0, 2)
    )

    def head_pass(unused, head_items):
        query_block, key_block, value_block, row_top, row_total, row_accum = head_items
        scores = jnp.dot(query_block, key_block.T, preferred_element_type=jnp.float32) * inv_root
        scores = scores.reshape(group_size, tokens, key_count)
        masked = jnp.where(allowed[None], scores, -1e30)
        new_top = jnp.maximum(row_top, jnp.max(masked, axis=-1).reshape(group_size * tokens))
        weights = jnp.where(
            allowed[None], jnp.exp(scores - new_top.reshape(group_size, tokens, 1)), 0.0
        )
        decay = jnp.exp(row_top - new_top)
        new_total = row_total * decay + jnp.sum(weights, axis=-1).reshape(group_size * tokens)
        product = jnp.dot(
            weights.astype(jnp.bfloat16).reshape(group_size * tokens, key_count),
            value_block,
            preferred_element_type=jnp.float32,
        )
        new_accum = row_accum * decay[:, None] + product
        return (unused, (new_top, new_total, new_accum))

    running = lax.scan(head_pass, 0, (query_heads, key_heads, value_heads) + tuple(initial))[1]
    row_top, row_total, row_accum = running
    finished = row_accum / row_total[:, :, None]
    attended = (
        finished.reshape(kv_heads, group_size, tokens, head_size)
        .transpose(2, 0, 1, 3)
        .reshape(1, tokens, group_size * key_width)
        .astype(jnp.bfloat16)
    )
    pages_dev = tokens // PAGE
    key_codes, key_scale = rotate_codes(keys[0].reshape(tokens * kv_heads, head_size), head_size)
    value_codes, value_scale = rotate_codes(
        values[0].reshape(tokens * kv_heads, head_size), head_size
    )
    owner_ids = owners[0, :, 0]
    page_index = jnp.arange(pages_dev, dtype=jnp.int32)
    earlier = (owner_ids[:, None] == owner_ids[None, :]) & (
        page_index[None, :] < page_index[:, None]
    )
    rank = jnp.sum(earlier.astype(jnp.int32), axis=1)
    select = (
        (owner_ids[None, None, :] == jnp.arange(owner_count, dtype=jnp.int32)[:, None, None])
        & (rank[None, None, :] == jnp.arange(CAP, dtype=jnp.int32)[None, :, None])
    ).astype(jnp.bfloat16)

    def pack_codes(codes):
        paged = codes.reshape(pages_dev, PAGE, ctx_count, heads_per, head_size)
        packed = jnp.einsum("okj,jtchd->cohktd", select, paged, preferred_element_type=jnp.float32)
        return packed.astype(jnp.bfloat16).reshape(
            ctx_count, owner_count, heads_per, CAP, PAGE * head_size
        )

    def pack_scales(block_scale):
        paged = block_scale.reshape(pages_dev, PAGE, ctx_count, heads_per)
        packed = jnp.einsum("okj,jtch->cohkt", select, paged, preferred_element_type=jnp.float32)
        return packed.astype(jnp.bfloat16)

    outgoing = (
        pack_codes(key_codes),
        pack_codes(value_codes),
        pack_scales(key_scale),
        pack_scales(value_scale),
    )
    merged = tuple(
        (piece.reshape((ctx_count * owner_count,) + piece.shape[2:]) for piece in outgoing)
    )
    received = jax.tree.map(
        lambda part, own: part.astype(own.dtype),
        lax.all_to_all(as_sent(merged), ("ctx", "dec"), split_axis=0, concat_axis=0, tiled=True),
        merged,
    )
    return (attended, received[0], received[1], received[2], received[3])


def solution(mesh):
    placed = (
        P("dec", "ctx", None),
        P("dec", "ctx", None),
        P("dec", "ctx", None),
        P("dec", None),
        P("dec", "ctx", None),
    )
    return jax.shard_map(
        body,
        mesh=mesh,
        in_specs=placed,
        out_specs=(
            P("dec", "ctx", None),
            P(None, "ctx", "dec", None),
            P(None, "ctx", "dec", None),
            P(None, "ctx", "dec", None),
            P(None, "ctx", "dec", None),
        ),
        check_vma=False,
    )
```

profile of v0, /device:TPU:1, one launch (start us, length us, event | category | flops | bytes accessed | tf_op | source)
XLA Modules:
  0.0 249.2 jit_solution(13473669295457991847)
XLA Ops:
  7.2 1.8 copy.55
  9.1 1.8 copy.56
  14.9 11.5 %all-to-all-start.2 = ((bf16[128,1,2,8]{3,2,1,0:T(2,128)(2,1)}), bf16[128,1,2,8]{3,2,1,0:T(2,128)(2,1)S(1)}, u32[]{:S(2)}, u32[]{:S(2)}) async-start(bf16[128,1,2,8]{3,2,1,0:T(2,128)(2,1)} %bitcast.28), calls=%async_computation.2 | async-start | bytes 131072 | tf_op jit(solution)/shard_map/all_to_all | solution.py:148
  29.1 7.0 %all-to-all-done.2 = bf16[128,1,2,8]{3,2,1,0:T(2,128)(2,1)S(1)} async-done(((bf16[128,1,2,8]{3,2,1,0:T(2,128)(2,1)}), bf16[128,1,2,8]{3,2,1,0:T(2,128)(2,1)S(1)}, u32[]{:S(2)}, u32[]{:S(2)}) %all-to-all-start.2) | async-done | bytes 4128 | tf_op jit(solution)/shard_map/all_to_all | solution.py:148
  36.2 4.3 %all-to-all-start.3 = ((bf16[128,1,2,8]{3,2,1,0:T(2,128)(2,1)}), bf16[128,1,2,8]{3,2,1,0:T(2,128)(2,1)S(1)}, u32[]{:S(2)}, u32[]{:S(2)}) async-start(bf16[128,1,2,8]{3,2,1,0:T(2,128)(2,1)} %bitcast.32), calls=%async_computation.3 | async-start | bytes 131072 | tf_op jit(solution)/shard_map/all_to_all | solution.py:148
  42.0 8.2 %all-to-all-done.3 = bf16[128,1,2,8]{3,2,1,0:T(2,128)(2,1)S(1)} async-done(((bf16[128,1,2,8]{3,2,1,0:T(2,128)(2,1)}), bf16[128,1,2,8]{3,2,1,0:T(2,128)(2,1)S(1)}, u32[]{:S(2)}, u32[]{:S(2)}) %all-to-all-start.3) | async-done | bytes 4128 | tf_op jit(solution)/shard_map/all_to_all | solution.py:148
  50.2 4.3 %all-to-all-start = ((bf16[128,1,2,1024]{3,2,1,0:T(2,128)(2,1)}), bf16[128,1,2,1024]{3,2,1,0:T(2,128)(2,1)S(1)}, u32[]{:S(2)}, u32[]{:S(2)}) async-start(bf16[128,1,2,1024]{3,2,1,0:T(2,128)(2,1)} %reshape.232), calls=%async_computation | async-start | bytes 1048576 | tf_op jit(solution)/shard_map/all_to_all | solution.py:148
  56.3 12.4 %all-to-all-done = bf16[128,1,2,1024]{3,2,1,0:T(2,128)(2,1)S(1)} async-done(((bf16[128,1,2,1024]{3,2,1,0:T(2,128)(2,1)}), bf16[128,1,2,1024]{3,2,1,0:T(2,128)(2,1)S(1)}, u32[]{:S(2)}, u32[]{:S(2)}) %all-to-all-start) | async-done | bytes 524320 | tf_op jit(solution)/shard_map/all_to_all | solution.py:148
  68.6 4.9 %all-to-all-start.1 = ((bf16[128,1,2,1024]{3,2,1,0:T(2,128)(2,1)}), bf16[128,1,2,1024]{3,2,1,0:T(2,128)(2,1)S(1)}, u32[]{:S(2)}, u32[]{:S(2)}) async-start(bf16[128,1,2,1024]{3,2,1,0:T(2,128)(2,1)} %reshape.233), calls=%async_computation.1 | async-start | bytes 1048576 | tf_op jit(solution)/shard_map/all_to_all | solution.py:148
  73.5 3.4 %copy.96 = bf16[16,8,128,128]{3,2,1,0:T(8,128)(2,1)S(1)} copy(bf16[16,8,128,128]{3,1,2,0:T(8,128)(2,1)} %bitcast.133) | data formatting | bytes 8388608
  77.0 4.7 %copy.54 = bf16[128,8,16,128]{3,0,2,1:T(8,128)(2,1)} copy(bf16[128,8,16,128]{3,2,1,0:T(8,128)(2,1)S(1)} %bitcast.132) | data formatting | bytes 8388608 | tf_op jit(solution)/shard_map/reshape;squeeze | solution.py:53
  83.4 4.2 %all-to-all-done.1 = bf16[128,1,2,1024]{3,2,1,0:T(2,128)(2,1)S(1)} async-done(((bf16[128,1,2,1024]{3,2,1,0:T(2,128)(2,1)}), bf16[128,1,2,1024]{3,2,1,0:T(2,128)(2,1)S(1)}, u32[]{:S(2)}, u32[]{:S(2)}) %all-to-all-start.1) | async-done | bytes 524320 | tf_op jit(solution)/shard_map/all_to_all | solution.py:148
  87.6 135.8 %while.13 = (s32[]{:T(128)}, f32[8,2048]{1,0:T(8,128)S(1)}, f32[8,2048,128]{2,1,0:T(8,128)}, bf16[8,2048,128]{2,1,0:T(8,128)(2,1)}, bf16[8,1024,128]{1,2,0:T(8,1...) while((s32[]{:T(128)}, f32[8,2048]{1,0:T(8,128)S(1)}, ...), condition=%wide.region_6.7_spmd.clone, body=%wide.region_3.6_spmd.clone.sunk | while | flops 1097472000 | bytes 69581968 | solution.py:100
  88.4 3.2 %select_reduce_fusion.2 = (f32[2048]{0:T(1024)S(1)}, f32[2048,1024]{0,1:T(8,128)S(1)}) fusion(pred[128,8,16,128]{3,2,1,0:T(8,128)(4,1)S(1)} %bitcast.127, bf16[8,1024,128]{1,2,0:T(8,128)(2,1)} %get-tuple-element.229, s32[]{:T(128)S(6)} %copy.131, bf16[8,2048,128]{2,1,0:T(8,128)(2,1)} %get-tuple-element.228), kind=kOutput, calls=%fused_computation.2.clone.1 | convolution fusion | flops 543160320 | bytes 11281408 | tf_op jit(solution)/shard_map/while/body/eval_jaxpr/dot_general | solution.py:83
  91.6 3.2 %copy-done = f32[2048,1024]{0,1:T(8,128)} copy-done((f32[2048,1024]{0,1:T(8,128)}, f32[2048,1024]{0,1:T(8,128)S(1)}, u32[]{:S(2)}) %copy-start) | copy-done | bytes 8388632 | tf_op jit(solution)/shard_map/while
  94.8 2.5 fusion.81
  97.5 7.1 %fusion.82 = f32[8,2048,128]{2,1,0:T(8,128)} fusion(f32[8,2048,128]{2,1,0:T(8,128)} %get-tuple-element.216, s32[]{:T(128)S(6)} %copy.131, f32[2048,1024]{0,1:T(8,128)} %copy-done, pred[128,8,16,128]{3,2,1,0:T(8,128)(4,1)S(1)} %bitcast.129, f32[2048]{0:T(1024)S(1)} %broadcast_maximum_fusion.2, f32[2048]{0:T(1024)S(1)} %get-tuple-element.202, ...), kind=kOutput, calls=%fused_computation.8.clone.1 | convolution fusion | flops 545521664 | bytes 11813888 | tf_op jit(solution)/shard_map/while/body/eval_jaxpr/dot_general | solution.py:92
  105.3 3.2 %select_reduce_fusion.2 = (f32[2048]{0:T(1024)S(1)}, f32[2048,1024]{0,1:T(8,128)S(1)}) fusion(pred[128,8,16,128]{3,2,1,0:T(8,128)(4,1)S(1)} %bitcast.127, bf16[8,1024,128]{1,2,0:T(8,128)(2,1)} %get-tuple-element.229, s32[]{:T(128)S(6)} %copy.131, bf16[8,2048,128]{2,1,0:T(8,128)(2,1)} %get-tuple-element.228), kind=kOutput, calls=%fused_computation.2.clone.1 | convolution fusion | flops 543160320 | bytes 11281408 | tf_op jit(solution)/shard_map/while/body/eval_jaxpr/dot_general | solution.py:83
  108.5 3.2 %copy-done = f32[2048,1024]{0,1:T(8,128)} copy-done((f32[2048,1024]{0,1:T(8,128)}, f32[2048,1024]{0,1:T(8,128)S(1)}, u32[]{:S(2)}) %copy-start) | copy-done | bytes 8388632 | tf_op jit(solution)/shard_map/while
  111.7 2.5 fusion.81
  114.4 7.1 %fusion.82 = f32[8,2048,128]{2,1,0:T(8,128)} fusion(f32[8,2048,128]{2,1,0:T(8,128)} %get-tuple-element.216, s32[]{:T(128)S(6)} %copy.131, f32[2048,1024]{0,1:T(8,128)} %copy-done, pred[128,8,16,128]{3,2,1,0:T(8,128)(4,1)S(1)} %bitcast.129, f32[2048]{0:T(1024)S(1)} %broadcast_maximum_fusion.2, f32[2048]{0:T(1024)S(1)} %get-tuple-element.202, ...), kind=kOutput, calls=%fused_computation.8.clone.1 | convolution fusion | flops 545521664 | bytes 11813888 | tf_op jit(solution)/shard_map/while/body/eval_jaxpr/dot_general | solution.py:92
  122.4 3.2 %select_reduce_fusion.2 = (f32[2048]{0:T(1024)S(1)}, f32[2048,1024]{0,1:T(8,128)S(1)}) fusion(pred[128,8,16,128]{3,2,1,0:T(8,128)(4,1)S(1)} %bitcast.127, bf16[8,1024,128]{1,2,0:T(8,128)(2,1)} %get-tuple-element.229, s32[]{:T(128)S(6)} %copy.131, bf16[8,2048,128]{2,1,0:T(8,128)(2,1)} %get-tuple-element.228), kind=kOutput, calls=%fused_computation.2.clone.1 | convolution fusion | flops 543160320 | bytes 11281408 | tf_op jit(solution)/shard_map/while/body/eval_jaxpr/dot_general | solution.py:83
  125.5 3.2 %copy-done = f32[2048,1024]{0,1:T(8,128)} copy-done((f32[2048,1024]{0,1:T(8,128)}, f32[2048,1024]{0,1:T(8,128)S(1)}, u32[]{:S(2)}) %copy-start) | copy-done | bytes 8388632 | tf_op jit(solution)/shard_map/while
  128.7 2.5 fusion.81
  131.5 7.1 %fusion.82 = f32[8,2048,128]{2,1,0:T(8,128)} fusion(f32[8,2048,128]{2,1,0:T(8,128)} %get-tuple-element.216, s32[]{:T(128)S(6)} %copy.131, f32[2048,1024]{0,1:T(8,128)} %copy-done, pred[128,8,16,128]{3,2,1,0:T(8,128)(4,1)S(1)} %bitcast.129, f32[2048]{0:T(1024)S(1)} %broadcast_maximum_fusion.2, f32[2048]{0:T(1024)S(1)} %get-tuple-element.202, ...), kind=kOutput, calls=%fused_computation.8.clone.1 | convolution fusion | flops 545521664 | bytes 11813888 | tf_op jit(solution)/shard_map/while/body/eval_jaxpr/dot_general | solution.py:92
  139.3 3.2 %select_reduce_fusion.2 = (f32[2048]{0:T(1024)S(1)}, f32[2048,1024]{0,1:T(8,128)S(1)}) fusion(pred[128,8,16,128]{3,2,1,0:T(8,128)(4,1)S(1)} %bitcast.127, bf16[8,1024,128]{1,2,0:T(8,128)(2,1)} %get-tuple-element.229, s32[]{:T(128)S(6)} %copy.131, bf16[8,2048,128]{2,1,0:T(8,128)(2,1)} %get-tuple-element.228), kind=kOutput, calls=%fused_computation.2.clone.1 | convolution fusion | flops 543160320 | bytes 11281408 | tf_op jit(solution)/shard_map/while/body/eval_jaxpr/dot_general | solution.py:83
  142.5 3.2 %copy-done = f32[2048,1024]{0,1:T(8,128)} copy-done((f32[2048,1024]{0,1:T(8,128)}, f32[2048,1024]{0,1:T(8,128)S(1)}, u32[]{:S(2)}) %copy-start) | copy-done | bytes 8388632 | tf_op jit(solution)/shard_map/while
  145.7 2.5 fusion.81
  148.4 7.1 %fusion.82 = f32[8,2048,128]{2,1,0:T(8,128)} fusion(f32[8,2048,128]{2,1,0:T(8,128)} %get-tuple-element.216, s32[]{:T(128)S(6)} %copy.131, f32[2048,1024]{0,1:T(8,128)} %copy-done, pred[128,8,16,128]{3,2,1,0:T(8,128)(4,1)S(1)} %bitcast.129, f32[2048]{0:T(1024)S(1)} %broadcast_maximum_fusion.2, f32[2048]{0:T(1024)S(1)} %get-tuple-element.202, ...), kind=kOutput, calls=%fused_computation.8.clone.1 | convolution fusion | flops 545521664 | bytes 11813888 | tf_op jit(solution)/shard_map/while/body/eval_jaxpr/dot_general | solution.py:92
  156.3 3.2 %select_reduce_fusion.2 = (f32[2048]{0:T(1024)S(1)}, f32[2048,1024]{0,1:T(8,128)S(1)}) fusion(pred[128,8,16,128]{3,2,1,0:T(8,128)(4,1)S(1)} %bitcast.127, bf16[8,1024,128]{1,2,0:T(8,128)(2,1)} %get-tuple-element.229, s32[]{:T(128)S(6)} %copy.131, bf16[8,2048,128]{2,1,0:T(8,128)(2,1)} %get-tuple-element.228), kind=kOutput, calls=%fused_computation.2.clone.1 | convolution fusion | flops 543160320 | bytes 11281408 | tf_op jit(solution)/shard_map/while/body/eval_jaxpr/dot_general | solution.py:83
  159.5 3.2 %copy-done = f32[2048,1024]{0,1:T(8,128)} copy-done((f32[2048,1024]{0,1:T(8,128)}, f32[2048,1024]{0,1:T(8,128)S(1)}, u32[]{:S(2)}) %copy-start) | copy-done | bytes 8388632 | tf_op jit(solution)/shard_map/while
  162.7 2.5 fusion.81
  165.4 7.1 %fusion.82 = f32[8,2048,128]{2,1,0:T(8,128)} fusion(f32[8,2048,128]{2,1,0:T(8,128)} %get-tuple-element.216, s32[]{:T(128)S(6)} %copy.131, f32[2048,1024]{0,1:T(8,128)} %copy-done, pred[128,8,16,128]{3,2,1,0:T(8,128)(4,1)S(1)} %bitcast.129, f32[2048]{0:T(1024)S(1)} %broadcast_maximum_fusion.2, f32[2048]{0:T(1024)S(1)} %get-tuple-element.202, ...), kind=kOutput, calls=%fused_computation.8.clone.1 | convolution fusion | flops 545521664 | bytes 11813888 | tf_op jit(solution)/shard_map/while/body/eval_jaxpr/dot_general | solution.py:92
  173.2 3.2 %select_reduce_fusion.2 = (f32[2048]{0:T(1024)S(1)}, f32[2048,1024]{0,1:T(8,128)S(1)}) fusion(pred[128,8,16,128]{3,2,1,0:T(8,128)(4,1)S(1)} %bitcast.127, bf16[8,1024,128]{1,2,0:T(8,128)(2,1)} %get-tuple-element.229, s32[]{:T(128)S(6)} %copy.131, bf16[8,2048,128]{2,1,0:T(8,128)(2,1)} %get-tuple-element.228), kind=kOutput, calls=%fused_computation.2.clone.1 | convolution fusion | flops 543160320 | bytes 11281408 | tf_op jit(solution)/shard_map/while/body/eval_jaxpr/dot_general | solution.py:83
  176.4 3.2 %copy-done = f32[2048,1024]{0,1:T(8,128)} copy-done((f32[2048,1024]{0,1:T(8,128)}, f32[2048,1024]{0,1:T(8,128)S(1)}, u32[]{:S(2)}) %copy-start) | copy-done | bytes 8388632 | tf_op jit(solution)/shard_map/while
  179.6 2.5 fusion.81
  182.3 7.1 %fusion.82 = f32[8,2048,128]{2,1,0:T(8,128)} fusion(f32[8,2048,128]{2,1,0:T(8,128)} %get-tuple-element.216, s32[]{:T(128)S(6)} %copy.131, f32[2048,1024]{0,1:T(8,128)} %copy-done, pred[128,8,16,128]{3,2,1,0:T(8,128)(4,1)S(1)} %bitcast.129, f32[2048]{0:T(1024)S(1)} %broadcast_maximum_fusion.2, f32[2048]{0:T(1024)S(1)} %get-tuple-element.202, ...), kind=kOutput, calls=%fused_computation.8.clone.1 | convolution fusion | flops 545521664 | bytes 11813888 | tf_op jit(solution)/shard_map/while/body/eval_jaxpr/dot_general | solution.py:92
  190.2 3.2 %select_reduce_fusion.2 = (f32[2048]{0:T(1024)S(1)}, f32[2048,1024]{0,1:T(8,128)S(1)}) fusion(pred[128,8,16,128]{3,2,1,0:T(8,128)(4,1)S(1)} %bitcast.127, bf16[8,1024,128]{1,2,0:T(8,128)(2,1)} %get-tuple-element.229, s32[]{:T(128)S(6)} %copy.131, bf16[8,2048,128]{2,1,0:T(8,128)(2,1)} %get-tuple-element.228), kind=kOutput, calls=%fused_computation.2.clone.1 | convolution fusion | flops 543160320 | bytes 11281408 | tf_op jit(solution)/shard_map/while/body/eval_jaxpr/dot_general | solution.py:83
  193.4 3.2 %copy-done = f32[2048,1024]{0,1:T(8,128)} copy-done((f32[2048,1024]{0,1:T(8,128)}, f32[2048,1024]{0,1:T(8,128)S(1)}, u32[]{:S(2)}) %copy-start) | copy-done | bytes 8388632 | tf_op jit(solution)/shard_map/while
  196.6 2.5 fusion.81
  199.3 7.1 %fusion.82 = f32[8,2048,128]{2,1,0:T(8,128)} fusion(f32[8,2048,128]{2,1,0:T(8,128)} %get-tuple-element.216, s32[]{:T(128)S(6)} %copy.131, f32[2048,1024]{0,1:T(8,128)} %copy-done, pred[128,8,16,128]{3,2,1,0:T(8,128)(4,1)S(1)} %bitcast.129, f32[2048]{0:T(1024)S(1)} %broadcast_maximum_fusion.2, f32[2048]{0:T(1024)S(1)} %get-tuple-element.202, ...), kind=kOutput, calls=%fused_computation.8.clone.1 | convolution fusion | flops 545521664 | bytes 11813888 | tf_op jit(solution)/shard_map/while/body/eval_jaxpr/dot_general | solution.py:92
  207.2 3.2 %select_reduce_fusion.2 = (f32[2048]{0:T(1024)S(1)}, f32[2048,1024]{0,1:T(8,128)S(1)}) fusion(pred[128,8,16,128]{3,2,1,0:T(8,128)(4,1)S(1)} %bitcast.127, bf16[8,1024,128]{1,2,0:T(8,128)(2,1)} %get-tuple-element.229, s32[]{:T(128)S(6)} %copy.131, bf16[8,2048,128]{2,1,0:T(8,128)(2,1)} %get-tuple-element.228), kind=kOutput, calls=%fused_computation.2.clone.1 | convolution fusion | flops 543160320 | bytes 11281408 | tf_op jit(solution)/shard_map/while/body/eval_jaxpr/dot_general | solution.py:83
  210.4 3.2 %copy-done = f32[2048,1024]{0,1:T(8,128)} copy-done((f32[2048,1024]{0,1:T(8,128)}, f32[2048,1024]{0,1:T(8,128)S(1)}, u32[]{:S(2)}) %copy-start) | copy-done | bytes 8388632 | tf_op jit(solution)/shard_map/while
  213.6 2.5 fusion.81
  216.3 7.1 %fusion.82 = f32[8,2048,128]{2,1,0:T(8,128)} fusion(f32[8,2048,128]{2,1,0:T(8,128)} %get-tuple-element.216, s32[]{:T(128)S(6)} %copy.131, f32[2048,1024]{0,1:T(8,128)} %copy-done, pred[128,8,16,128]{3,2,1,0:T(8,128)(4,1)S(1)} %bitcast.129, f32[2048]{0:T(1024)S(1)} %broadcast_maximum_fusion.2, f32[2048]{0:T(1024)S(1)} %get-tuple-element.202, ...), kind=kOutput, calls=%fused_computation.8.clone.1 | convolution fusion | flops 545521664 | bytes 11813888 | tf_op jit(solution)/shard_map/while/body/eval_jaxpr/dot_general | solution.py:92
  223.4 5.5 %divide_convert_fusion = bf16[8,2048,128]{2,1,0:T(8,128)(2,1)S(1)} fusion(f32[8,2048,128]{2,1,0:T(8,128)} %get-tuple-element.43, f32[8,2048]{1,0:T(8,128)S(1)} %get-tuple-element.44), kind=kLoop, calls=%fused_computation.25 | loop fusion | flops 4194304 | bytes 12648448 | tf_op jit(solution)/shard_map/convert_element_type | solution.py:107
  228.9 4.6 %copy.119 = bf16[8,16,128,128]{3,1,0,2:T(8,128)(2,1)} copy(bf16[8,16,128,128]{3,2,1,0:T(8,128)(2,1)S(1)} %bitcast.130) | data formatting | bytes 8388608 | tf_op jit(solution)/shard_map/convert_element_type | solution.py:107
  233.5 7.3 %convert_element_type.131 = bf16[1,128,16384]{2,1,0:T(8,128)(2,1)} reshape(bf16[128,8,16,128]{3,2,1,0:T(8,128)(2,1)} %bitcast.131) | data formatting | bytes 8388608 | tf_op jit(solution)/shard_map/convert_element_type | solution.py:107
  (91 shorter events, 21.1 us)
Async XLA Ops:
  7.2 80.4 %all-gather.3.cloned.1.call-start = ((), (), s32[]{:S(2)}) async-start(), calls=%async_computation.4 | async-start | bytes 2359296 | tf_op jit(solution)/shard_map/all_gather | solution.py:65
  9.0 78.6 %all-gather.5.cloned.1.call-start = ((), (), s32[]{:S(2)}) async-start(), calls=%async_computation.5 | async-start | bytes 2359296 | tf_op jit(solution)/shard_map/all_gather | solution.py:76
  14.9 21.2 %all-to-all-start.2 = ((bf16[128,1,2,8]{3,2,1,0:T(2,128)(2,1)}), bf16[128,1,2,8]{3,2,1,0:T(2,128)(2,1)S(1)}, u32[]{:S(2)}, u32[]{:S(2)}) async-start(bf16[128,1,2,8]{3,2,1,0:T(2,128)(2,1)} %bitcast.28), calls=%async_computation.2 | async-start | bytes 131072 | tf_op jit(solution)/shard_map/all_to_all | solution.py:148
  36.2 14.0 %all-to-all-start.3 = ((bf16[128,1,2,8]{3,2,1,0:T(2,128)(2,1)}), bf16[128,1,2,8]{3,2,1,0:T(2,128)(2,1)S(1)}, u32[]{:S(2)}, u32[]{:S(2)}) async-start(bf16[128,1,2,8]{3,2,1,0:T(2,128)(2,1)} %bitcast.32), calls=%async_computation.3 | async-start | bytes 131072 | tf_op jit(solution)/shard_map/all_to_all | solution.py:148
  50.2 18.5 %all-to-all-start = ((bf16[128,1,2,1024]{3,2,1,0:T(2,128)(2,1)}), bf16[128,1,2,1024]{3,2,1,0:T(2,128)(2,1)S(1)}, u32[]{:S(2)}, u32[]{:S(2)}) async-start(bf16[128,1,2,1024]{3,2,1,0:T(2,128)(2,1)} %reshape.232), calls=%async_computation | async-start | bytes 1048576 | tf_op jit(solution)/shard_map/all_to_all | solution.py:148
  68.6 19.0 %all-to-all-start.1 = ((bf16[128,1,2,1024]{3,2,1,0:T(2,128)(2,1)}), bf16[128,1,2,1024]{3,2,1,0:T(2,128)(2,1)S(1)}, u32[]{:S(2)}, u32[]{:S(2)}) async-start(bf16[128,1,2,1024]{3,2,1,0:T(2,128)(2,1)} %reshape.233), calls=%async_computation.1 | async-start | bytes 1048576 | tf_op jit(solution)/shard_map/all_to_all | solution.py:148
  73.5 8.2 %copy-start.1 = (s32[1,4]{1,0:T(1,128)S(1)}, s32[1,4]{1,0:T(1,128)}, u32[]{:S(2)}) copy-start(s32[1,4]{1,0:T(1,128)} %param.10) | copy-start | bytes 52
  91.5 3.2 %copy-start = (f32[2048,1024]{0,1:T(8,128)}, f32[2048,1024]{0,1:T(8,128)S(1)}, u32[]{:S(2)}) copy-start(f32[2048,1024]{0,1:T(8,128)S(1)} %get-tuple-element.200) | copy-start | bytes 25165828 | tf_op jit(solution)/shard_map/while
  108.5 3.2 %copy-start = (f32[2048,1024]{0,1:T(8,128)}, f32[2048,1024]{0,1:T(8,128)S(1)}, u32[]{:S(2)}) copy-start(f32[2048,1024]{0,1:T(8,128)S(1)} %get-tuple-element.200) | copy-start | bytes 25165828 | tf_op jit(solution)/shard_map/while
  125.5 3.2 %copy-start = (f32[2048,1024]{0,1:T(8,128)}, f32[2048,1024]{0,1:T(8,128)S(1)}, u32[]{:S(2)}) copy-start(f32[2048,1024]{0,1:T(8,128)S(1)} %get-tuple-element.200) | copy-start | bytes 25165828 | tf_op jit(solution)/shard_map/while
  142.5 3.2 %copy-start = (f32[2048,1024]{0,1:T(8,128)}, f32[2048,1024]{0,1:T(8,128)S(1)}, u32[]{:S(2)}) copy-start(f32[2048,1024]{0,1:T(8,128)S(1)} %get-tuple-element.200) | copy-start | bytes 25165828 | tf_op jit(solution)/shard_map/while
  159.5 3.2 %copy-start = (f32[2048,1024]{0,1:T(8,128)}, f32[2048,1024]{0,1:T(8,128)S(1)}, u32[]{:S(2)}) copy-start(f32[2048,1024]{0,1:T(8,128)S(1)} %get-tuple-element.200) | copy-start | bytes 25165828 | tf_op jit(solution)/shard_map/while
  176.4 3.2 %copy-start = (f32[2048,1024]{0,1:T(8,128)}, f32[2048,1024]{0,1:T(8,128)S(1)}, u32[]{:S(2)}) copy-start(f32[2048,1024]{0,1:T(8,128)S(1)} %get-tuple-element.200) | copy-start | bytes 25165828 | tf_op jit(solution)/shard_map/while
  193.4 3.2 %copy-start = (f32[2048,1024]{0,1:T(8,128)}, f32[2048,1024]{0,1:T(8,128)S(1)}, u32[]{:S(2)}) copy-start(f32[2048,1024]{0,1:T(8,128)S(1)} %get-tuple-element.200) | copy-start | bytes 25165828 | tf_op jit(solution)/shard_map/while
  210.4 3.2 %copy-start = (f32[2048,1024]{0,1:T(8,128)}, f32[2048,1024]{0,1:T(8,128)S(1)}, u32[]{:S(2)}) copy-start(f32[2048,1024]{0,1:T(8,128)S(1)} %get-tuple-element.200) | copy-start | bytes 25165828 | tf_op jit(solution)/shard_map/while
Sparse Core Ops, SparseCore 0:
  9.7 31.0 all-gather.2
  42.4 32.6 all-gather.4
where the time goes:
time: 250 us; the launch traced here: 249 us
  matrix products  83.8 us (34%)
  local copies, waits for them, and re-layouts  64.8 us (26%)
  waiting for transfers between devices  31.8 us (13%)
  other arithmetic  29.1 us (12%)
  starting transfers between devices  25 us (10%)
  between operations  14.2 us (6%)
    dot_general x8, matrix products, head_pass(): jnp.dot(weights.astype(jnp.bfloat16).reshape(group_size * tokens, key_cou...  56.9 us
    all_to_all x4, waiting for transfers between devices, body(): lax.all_to_all(as_sent(merged), ('ctx', 'dec'), split_axis=0, concat_axis...  31.8 us
    while x16, local copies, waits for them, and re-layouts  25.5 us
    dot_general x8, matrix products, head_pass(): jnp.dot(query_block, key_block.T, preferred_element_type=jnp.float32)  25.3 us
    all_to_all x4, starting transfers between devices, body(): lax.all_to_all(as_sent(merged), ('ctx', 'dec'), split_axis=0, concat_axis...  24.9 us
    reduce_sum x8, other arithmetic, head_pass(): jnp.sum(weights, axis=-1).reshape(group_size * tokens)  19.9 us
    convert_element_type x2, local copies, waits for them, and re-layouts, body(): attended = finished.reshape(kv_heads, group_size, tokens, head_size).tran...  11.9 us
    unnamed x9, local copies, waits for them, and re-layouts  9.95 us
  transfers between devices with their start and end apart: 6, of which 4 were waited for; matrix products, arithmetic and copies ran while one was open for 9% of the time, Pallas kernels for 0%

commit v1 on v0

v1 whole, which is shorter than its diff:
```python
import functools
import math

import jax
import jax.numpy as jnp
from jax import lax
from jax.experimental import pallas as pl
from jax.experimental.pallas import tpu as pltpu
from jax.sharding import PartitionSpec as P

HD = 128
KVH = 8
GROUP = 16
PAGE = 8
CAP = 2
REQS = 4
TOK = 128
PAGES_DEV = 16
OWNERS = 16
BLOCKS = 5
WINDOW = BLOCKS * TOK
ROW = 2 * PAGE * HD + HD
STACK = 2
PARTS = ((0, 5), (5, 3))
EXP_SCALE = math.log2(math.e) / math.sqrt(HD)
INV_ROOT = 1.0 / math.sqrt(HD)
NT = (((1,), (1,)), ((), ()))
NN = (((1,), (0,)), ((), ()))
ANY = pl.BlockSpec(memory_space=pl.ANY)
SMEM = pl.BlockSpec(memory_space=pltpu.SMEM)
VMEM = pl.BlockSpec(memory_space=pltpu.VMEM)


def iota(shape, axis):
    return lax.broadcasted_iota(jnp.int32, shape, axis)


def pack_kernel(owners, keys, values, out):
    row, col = iota((HD, HD), 0), iota((HD, HD), 1)
    common = row & col
    parity = jnp.zeros((HD, HD), jnp.int32)
    for bit in range(7):
        parity = parity + ((common >> bit) & 1)
    signs = (1 - 2 * (parity & 1)).astype(jnp.float32).astype(jnp.bfloat16)
    position = iota((1, TOK), 1)
    page, within = position // PAGE, position % PAGE
    slot = jnp.zeros((1, TOK), jnp.int32)
    for p in range(PAGES_DEV):
        rank = jnp.int32(0)
        for q in range(p):
            rank = rank + (owners[q] == owners[p]).astype(jnp.int32)
        slot = jnp.where(page == p, owners[p] * CAP + rank, slot)
    slots = OWNERS * CAP
    place = iota((PAGE * slots, TOK), 0)
    select = jnp.where((place % slots == slot) & (place // slots == within), 1.0, 0.0).astype(jnp.bfloat16)
    any_row = jnp.where(iota((slots, TOK), 0) == slot, 1.0, 0.0).astype(jnp.bfloat16)
    lane, in_page = iota((TOK, HD), 1), iota((TOK, HD), 0) % PAGE
    for h in range(KVH):
        scales = jnp.zeros((TOK, HD), jnp.float32)
        for which, rows in enumerate((keys, values)):
            rotated = (
                lax.dot_general(rows[0, :, h * HD : (h + 1) * HD], signs, NN, preferred_element_type=jnp.float32)
                * INV_ROOT
            )
            scale = (jnp.max(jnp.abs(rotated), axis=-1, keepdims=True) + 1e-06).astype(jnp.bfloat16)
            scale = scale.astype(jnp.float32)
            codes = (rotated / scale).astype(jnp.bfloat16)
            placed = lax.dot_general(select, codes, NN, preferred_element_type=jnp.float32).astype(jnp.bfloat16)
            for i in range(PAGE):
                at = (which * PAGE + i) * HD
                out[h, :, at : at + HD] = placed[i * slots : (i + 1) * slots]
            scales = jnp.where(lane == which * PAGE + in_page, scale, scales)
        out[h, :, 2 * PAGE * HD :] = lax.dot_general(
            any_row, scales.astype(jnp.bfloat16), NN, preferred_element_type=jnp.float32
        ).astype(jnp.bfloat16)


def pack(owners, keys, values):
    return pl.pallas_call(
        pack_kernel,
        in_specs=[SMEM, VMEM, VMEM],
        out_specs=VMEM,
        out_shape=jax.ShapeDtypeStruct((KVH, OWNERS * CAP, ROW), jnp.bfloat16),
        compiler_params=pltpu.CompilerParams(vmem_limit_bytes=24 * 2**20),
        cost_estimate=pl.CostEstimate(flops=2 * 10**8, bytes_accessed=2 * 10**6, transcendentals=0),
        name="pack",
    )(owners, keys, values)


def attend_kernel(first, heads, where, queries, own, near, far, swapped, *rest):
    out, q_buf, o_buf, k_buf, v_buf, bias, q_sem, kv_sem, o_sem = rest[-9:]
    head_width = GROUP * HD

    def query_copy(h):
        at = pl.ds(pl.multiple_of(h * head_width, head_width), head_width)
        from_at = pl.ds(pl.multiple_of((first + h) * head_width, head_width), head_width)
        return pltpu.make_async_copy(queries.at[0, :, from_at], q_buf.at[:, at], q_sem.at[h])

    def out_copy(h):
        at = pl.ds(pl.multiple_of(h * head_width, head_width), head_width)
        to_at = pl.ds(pl.multiple_of((first + h) * head_width, head_width), head_width)
        return pltpu.make_async_copy(o_buf.at[:, at], out.at[0, :, to_at], o_sem.at[h])

    blocks = (far, swapped.at[0], near, swapped.at[1], own)
    kv_copies = []
    for b, block in enumerate(blocks):
        for which, buf in enumerate((k_buf, v_buf)):
            kv_copies.append(
                pltpu.make_async_copy(block.at[which], buf.at[pl.ds(b * TOK, TOK)], kv_sem.at[2 * b + which])
            )
    for copy in kv_copies:
        copy.start()
    for h in range(heads):
        query_copy(h).start()

    ctx = where[0]
    core = lax.rem(ctx, 2)
    query_pos = ctx * TOK + iota((TOK, TOK), 0)
    start = jnp.zeros((TOK, TOK), jnp.int32)
    end = jnp.int32(0)
    for r in range(REQS):
        end = end + where[1 + r]
        start = jnp.where(query_pos >= end, end, start)
    back = (4, jnp.where(core == 0, 3, 1), 2, jnp.where(core == 0, 1, 3), 0)
    for b in range(BLOCKS):
        key_pos = (ctx - back[b]) * TOK + iota((TOK, TOK), 1)
        kept = (key_pos >= start) & (key_pos <= query_pos)
        bias[b * TOK : (b + 1) * TOK, :] = jnp.where(kept, 0.0, -1e30).astype(jnp.bfloat16).T
    eye = jnp.where(iota((TOK, TOK), 0) == iota((TOK, TOK), 1), 1.0, 0.0).astype(jnp.bfloat16)
    eyes = jnp.concatenate([eye] * STACK, 0)
    ones = jnp.ones((WINDOW, HD), jnp.bfloat16)
    for copy in kv_copies:
        copy.wait()

    def one_head(h, carry):
        query_copy(h).wait()
        lanes = pl.ds(pl.multiple_of(h * HD, HD), HD)
        key_side = jnp.concatenate([k_buf[:, lanes], bias[...]], 1)
        value_side = jnp.concatenate([v_buf[:, lanes], ones], 1)

        def head_lanes(g):
            return pl.ds(pl.multiple_of(h * head_width + g * HD, HD), HD)

        def score(g0):
            rows = jnp.concatenate([q_buf[:, head_lanes(g0 + g)] for g in range(STACK)], 0)
            return lax.dot_general(
                jnp.concatenate([rows, eyes], 1), key_side, NT, preferred_element_type=jnp.float32
            )

        def finish(g0, scores):
            top = jnp.max(scores, axis=-1, keepdims=True)
            weights = jnp.exp2((scores - top) * EXP_SCALE).astype(jnp.bfloat16)
            mixed = lax.dot_general(weights, value_side, NN, preferred_element_type=jnp.float32)
            result = (mixed[:, :HD] / mixed[:, HD:]).astype(jnp.bfloat16)
            for g in range(STACK):
                o_buf[:, head_lanes(g0 + g)] = result[g * TOK : (g + 1) * TOK]

        scores = score(0)
        for g0 in range(0, GROUP, STACK):
            following = score(g0 + STACK) if g0 + STACK < GROUP else None
            finish(g0, scores)
            scores = following
        out_copy(h).start()
        return carry

    lax.fori_loop(0, heads, one_head, 0)
    for h in range(heads):
        out_copy(h).wait()


def attend(first, heads, where, queries, own, near, far, swapped, partial):
    more = () if partial is None else (partial,)
    scores = GROUP * TOK * WINDOW * heads
    return pl.pallas_call(
        functools.partial(attend_kernel, first, heads),
        in_specs=[SMEM] + [ANY] * (5 + len(more)),
        out_specs=ANY,
        out_shape=jax.ShapeDtypeStruct(queries.shape, jnp.bfloat16),
        scratch_shapes=[
            pltpu.VMEM((TOK, heads * GROUP * HD), jnp.bfloat16),
            pltpu.VMEM((TOK, heads * GROUP * HD), jnp.bfloat16),
            pltpu.VMEM((WINDOW, heads * HD), jnp.bfloat16),
            pltpu.VMEM((WINDOW, heads * HD), jnp.bfloat16),
            pltpu.VMEM((WINDOW, TOK), jnp.bfloat16),
            pltpu.SemaphoreType.DMA((heads,)),
            pltpu.SemaphoreType.DMA((2 * BLOCKS,)),
            pltpu.SemaphoreType.DMA((heads,)),
        ],
        input_output_aliases={6: 0} if more else {},
        compiler_params=pltpu.CompilerParams(vmem_limit_bytes=32 * 2**20),
        cost_estimate=pl.CostEstimate(
            flops=scores * HD * 6, bytes_accessed=2 * heads * GROUP * TOK * HD * 2, transcendentals=scores
        ),
        name=f"attend{first}",
    )(where, queries, own, near, far, swapped, *more)


def body(queries, keys, values, lengths, owners):
    ctx_index = lax.axis_index("ctx")
    ctx_count = lax.axis_size("ctx")
    where = jnp.concatenate([ctx_index.astype(jnp.int32).reshape(1), lengths[0]])

    def chips_on(block, chips):
        step = 2 * chips
        return lax.ppermute(block, "ctx", [(i, i + step) for i in range(ctx_count - step)])

    owns, nears, fars = [], [], []
    for first, heads in PARTS:
        lanes = slice(first * HD, (first + heads) * HD)
        own = jnp.concatenate([keys[:, :, lanes], values[:, :, lanes]], 0)
        owns.append(own)
        nears.append(chips_on(own, 1))
        fars.append(chips_on(own, 2))

    message = pack(owners.reshape(PAGES_DEV), keys, values)
    message = message.reshape(KVH * OWNERS, CAP, ROW)
    received = lax.all_to_all(message, ("ctx", "dec"), split_axis=0, concat_axis=0, tiled=True)

    attended = None
    for (first, heads), own, near, far in zip(PARTS, owns, nears, fars):
        handed = jnp.where(ctx_index % 2 == 0, own, far)
        swapped = lax.ppermute(jnp.stack([handed, near]), "ctx", [(i, i ^ 1) for i in range(ctx_count)])
        attended = attend(first, heads, where, queries, own, near, far, swapped, attended)

    half = PAGE * HD
    cache_keys = received[:, None, :, :half]
    cache_values = received[:, None, :, half : 2 * half]
    key_scales = received[:, None, :, 2 * half : 2 * half + PAGE]
    value_scales = received[:, None, :, 2 * half + PAGE : 2 * half + 2 * PAGE]
    return (attended, cache_keys, cache_values, key_scales, value_scales)


def solution(mesh):
    placed = (
        P("dec", "ctx", None),
        P("dec", "ctx", None),
        P("dec", "ctx", None),
        P("dec", None),
        P("dec", "ctx", None),
    )
    return jax.shard_map(
        body,
        mesh=mesh,
        in_specs=placed,
        out_specs=(
            P("dec", "ctx", None),
            P(None, "ctx", "dec", None),
            P(None, "ctx", "dec", None),
            P(None, "ctx", "dec", None),
            P(None, "ctx", "dec", None),
        ),
        check_vma=False,
    )
```

time: 250 us -> 76.3 us (0.31)
  matrix products: 83.8 us -> 0 us
  local copies, waits for them, and re-layouts: 64.8 us -> 10.6 us
  other arithmetic: 29.1 us -> 1.18 us
  Pallas kernels: 0 us -> 27.1 us
  waiting for transfers between devices: 31.8 us -> 10.9 us
  between operations: 14.2 us -> 0.87 us
    dot_general x22 -> x0, matrix products: 83.8 us -> none  [the longest x8 56.9 us: head_pass(): jnp.dot(weights.astype(jnp.bfloat16).reshape(group_size * tokens, key_cou...]
    all_to_all x4 -> x1, waiting for transfers between devices: 31.8 us -> 0.01 us  [body(): lax.all_to_all(message, ('ctx', 'dec'), split_axis=0, concat_axis=0, tile...]
    pallas_call x0 -> x3, Pallas kernels: none -> 27.1 us  [the longest x2 24.1 us: attend(): pl.pallas_call(functools.partial(attend_kernel, first, heads), in_specs=[...]
    while x16 -> x0, local copies, waits for them, and re-layouts: 25.5 us -> none
    reduce_sum x11 -> x0, other arithmetic: 21 us -> none  [the longest x8 19.9 us: head_pass(): jnp.sum(weights, axis=-1).reshape(group_size * tokens)]
    ppermute x0 -> x6, starting transfers between devices: none -> 17.6 us  [the longest x4 14.9 us: chips_on(): lax.ppermute(block, 'ctx', [(i, i + step) for i in range(ctx_count - step)])]
    all_to_all x4 -> x1, starting transfers between devices: 24.9 us -> 7.66 us  [body(): lax.all_to_all(message, ('ctx', 'dec'), split_axis=0, concat_axis=0, tile...]
    convert_element_type x6 -> x0, local copies, waits for them, and re-layouts: 12.4 us -> none  [the longest x2 11.9 us: body(): attended = finished.reshape(kv_heads, group_size, tokens, head_size).tran...]
  transfers between devices with their start and end apart: 6 -> 7, of which waited for: 4 -> 2; matrix products, arithmetic and copies ran while one was open for 9% -> 2% of each run, Pallas kernels for 0% -> 36%
where the time goes in v1:
time: 76.3 us; the launch traced here: 75.9 us
  Pallas kernels  27.1 us (36%)
  starting transfers between devices  25.2 us (33%)
  waiting for transfers between devices  10.9 us (14%)
  local copies, waits for them, and re-layouts  10.6 us (14%)
  other arithmetic  1.18 us (2%)
  between operations  0.87 us (1%)
    pallas_call x2, Pallas kernels, attend(): pl.pallas_call(functools.partial(attend_kernel, first, heads), in_specs=[...  24.1 us
    ppermute x4, starting transfers between devices, chips_on(): lax.ppermute(block, 'ctx', [(i, i + step) for i in range(ctx_count - step)])  14.9 us
    ppermute x4, waiting for transfers between devices, chips_on(): lax.ppermute(block, 'ctx', [(i, i + step) for i in range(ctx_count - step)])  10.9 us
    all_to_all x1, starting transfers between devices, body(): lax.all_to_all(message, ('ctx', 'dec'), split_axis=0, concat_axis=0, tile...  7.66 us
    unnamed x14, local copies, waits for them, and re-layouts  6.22 us
    pallas_call x1, Pallas kernels, pack(): pl.pallas_call(pack_kernel, in_specs=[SMEM, VMEM, VMEM], out_specs=VMEM,...  3.02 us
    ppermute x2, starting transfers between devices, body(): lax.ppermute(jnp.stack([handed, near]), 'ctx', [(i, i ^ 1) for i in range...  2.69 us
    slice x4, local copies, waits for them, and re-layouts, body(): own = jnp.concatenate([keys[:, :, lanes], values[:, :, lanes]], 0)  1.94 us
  transfers between devices with their start and end apart: 7, of which 2 were waited for; matrix products, arithmetic and copies ran while one was open for 2% of the time, Pallas kernels for 36%

profile of v1, /device:TPU:1, one launch (start us, length us, event | category | flops | bytes accessed | tf_op | source)
XLA Modules:
  0.0 75.9 jit_solution(3800793550056005475)
XLA Ops:
  0.6 0.0 copy-start.2
  0.6 0.0 copy-start.1
  0.7 1.0 %slice.26 = bf16[1,128,640]{2,1,0:T(8,128)(2,1)S(1)} slice(bf16[1,128,1024]{2,1,0:T(8,128)(2,1)} %keys.1), slice={[0:1], [0:128], [0:640]} | slice | bytes 327680 | tf_op jit(solution)/shard_map/slice | solution.py:210
  1.6 0.9 %slice.27 = bf16[1,128,640]{2,1,0:T(8,128)(2,1)S(1)} slice(bf16[1,128,1024]{2,1,0:T(8,128)(2,1)} %values.1), slice={[0:1], [0:128], [0:640]} | slice | bytes 327680 | tf_op jit(solution)/shard_map/slice | solution.py:210
  2.6 5.7 %collective-permute-start.4 = (bf16[2,128,640]{2,1,0:T(8,128)(2,1)S(1)}, bf16[2,128,640]{2,1,0:T(8,128)(2,1)S(1)}, u32[]{:S(2)}, u32[]{:S(2)}) collective-permute-start(bf16[2,128,640]{2,1,0:T(8,128)(2,1)S(1)} %pad_maximum_fusion.2.own), channel_id=1, source_target_pairs={{0,64},{16,80},{32,96},{48,112},{1,65},{17,81},{33,97},{49,113},{2... | collective-permute-start | bytes 983048 | tf_op jit(solution)/shard_map/ppermute | solution.py:205
  8.3 2.3 %collective-permute-start.3 = (bf16[2,128,640]{2,1,0:T(8,128)(2,1)S(1)}, bf16[2,128,640]{2,1,0:T(8,128)(2,1)S(1)}, u32[]{:S(2)}, u32[]{:S(2)}) collective-permute-start(bf16[2,128,640]{2,1,0:T(8,128)(2,1)S(1)} %pad_maximum_fusion.2.own), channel_id=1, source_target_pairs={{0,32},{16,48},{32,64},{48,80},{64,96},{80,112},{1,33},{17,49},{33... | collective-permute-start | bytes 983048 | tf_op jit(solution)/shard_map/ppermute | solution.py:205
  10.6 0.0 copy-done.2
  10.7 0.0 copy-done.1
  10.7 0.0 copy-start.3
  10.7 4.0 %collective-permute-done.4.far = bf16[2,128,640]{2,1,0:T(8,128)(2,1)S(1)} collective-permute-done((bf16[2,128,640]{2,1,0:T(8,128)(2,1)S(1)}, bf16[2,128,640]{2,1,0:T(8,128)(2,1)S(1)}, u32[]{:S(2)}, u32[]{:S(2)}) %collective-permute-start.4) | collective-permute-done | bytes 327712 | tf_op jit(solution)/shard_map/ppermute | solution.py:205
  14.7 7.0 %collective-permute-done.3.near = bf16[2,128,640]{2,1,0:T(8,128)(2,1)S(1)} collective-permute-done((bf16[2,128,640]{2,1,0:T(8,128)(2,1)S(1)}, bf16[2,128,640]{2,1,0:T(8,128)(2,1)S(1)}, u32[]{:S(2)}, u32[]{:S(2)}) %collective-permute-start.3) | collective-permute-done | bytes 327712 | tf_op jit(solution)/shard_map/ppermute | solution.py:205
  21.7 0.9 %pad_maximum_fusion = bf16[2,2,128,640]{3,2,1,0:T(8,128)(2,1)} fusion(bf16[1,2,128,640]{3,2,1,0:T(8,128)(2,1)S(1)} %bitcast.18, bf16[1,2,128,640]{3,2,1,0:T(8,128)(2,1)S(1)} %select_bitcast_fusion), kind=kLoop, calls=%fused_computation | loop fusion | flops 327680 | bytes 1310720 | tf_op jit(solution)/shard_map/stack | solution.py:222
  22.6 1.5 %collective-permute-start.5 = (bf16[2,2,128,640]{3,2,1,0:T(8,128)(2,1)}, bf16[2,2,128,640]{3,2,1,0:T(8,128)(2,1)}, u32[]{:S(2)}, u32[]{:S(2)}) collective-permute-start(bf16[2,2,128,640]{3,2,1,0:T(8,128)(2,1)} %pad_maximum_fusion), channel_id=1, source_target_pairs={{0,16},{16,0},{32,48},{48,32},{64,80},{80,64},{96,112},{112,96},{1... | collective-permute-start | bytes 1966088 | tf_op jit(solution)/shard_map/ppermute | solution.py:222
  24.2 5.6 %collective-permute-start.1 = (bf16[2,128,384]{2,1,0:T(8,128)(2,1)S(1)}, bf16[2,128,384]{2,1,0:T(8,128)(2,1)S(1)}, u32[]{:S(2)}, u32[]{:S(2)}) collective-permute-start(bf16[2,128,384]{2,1,0:T(8,128)(2,1)S(1)} %pad_maximum_fusion.3.own), channel_id=1, source_target_pairs={{0,64},{16,80},{32,96},{48,112},{1,65},{17,81},{33,97},{49,113},{2... | collective-permute-start | bytes 589832 | tf_op jit(solution)/shard_map/ppermute | solution.py:205
  29.8 1.3 %collective-permute-start = (bf16[2,128,384]{2,1,0:T(8,128)(2,1)S(1)}, bf16[2,128,384]{2,1,0:T(8,128)(2,1)S(1)}, u32[]{:S(2)}, u32[]{:S(2)}) collective-permute-start(bf16[2,128,384]{2,1,0:T(8,128)(2,1)S(1)} %pad_maximum_fusion.3.own), channel_id=1, source_target_pairs={{0,32},{16,48},{32,64},{48,80},{64,96},{80,112},{1,33},{17,49},{33... | collective-permute-start | bytes 589832 | tf_op jit(solution)/shard_map/ppermute | solution.py:205
  31.1 0.0 copy-done.3
  31.1 3.0 %pack.1 = bf16[8,32,2176]{2,1,0:T(8,128)(2,1)S(1)} custom-call(s32[16]{0:T(128)S(1)} %bitcast.19, bf16[1,128,1024]{2,1,0:T(8,128)(2,1)S(1)} %copy-done.2, bf16[1,128,1024]{2,1,0:T(8,128)(2,1)S(1)} %copy-done.1), custom_call_target="tpu_custom_call" | custom-call | flops 200000000 | bytes 2000000 | tf_op jit(solution)/shard_map/pack/pallas_call | solution.py:79
  34.1 1.3 %reshape.21 = bf16[128,2,2176]{2,1,0:T(2,128)(2,1)} reshape(bf16[8,32,2176]{2,1,0:T(8,128)(2,1)S(1)} %pack.1) | data formatting | bytes 2228224 | tf_op jit(solution)/shard_map/reshape | solution.py:216
  35.4 0.0 copy-start.4
  35.4 7.7 %all-to-all-start = ((bf16[128,2,2176]{2,1,0:T(2,128)(2,1)}), bf16[128,2,2176]{2,1,0:T(2,128)(2,1)S(1)}, u32[]{:S(2)}, u32[]{:S(2)}) async-start(bf16[128,2,2176]{2,1,0:T(2,128)(2,1)} %reshape.21), calls=%async_computation | async-start | bytes 2228224 | tf_op jit(solution)/shard_map/all_to_all | solution.py:217
  43.0 0.0 copy-done.4
  43.1 0.1 pad_add_fusion.where
  43.1 0.0 collective-permute-done.1.far
  43.2 0.0 collective-permute-done.near
  43.2 1.1 %collective-permute-start.2 = (bf16[2,2,128,384]{3,2,1,0:T(8,128)(2,1)S(1)}, bf16[2,2,128,384]{3,2,1,0:T(8,128)(2,1)S(1)}, u32[]{:S(2)}, u32[]{:S(2)}) collective-permute-start(bf16[2,2,128,384]{3,2,1,0:T(8,128)(2,1)S(1)} %pad_maximum_fusion.1), channel_id=1, source_target_pairs={{0,16},{16,0},{32,48},{48,32},{64,80},{80,64},{96,112},{112,96},{1... | collective-permute-start | bytes 1179656 | tf_op jit(solution)/shard_map/ppermute | solution.py:222
  44.4 0.0 collective-permute-done.5.swapped
  44.4 0.0 copy-start
  44.4 2.2 %copy-done = bf16[1,128,16384]{2,1,0:T(8,128)(2,1)S(1)} copy-done((bf16[1,128,16384]{2,1,0:T(8,128)(2,1)S(1)}, bf16[1,128,16384]{2,1,0:T(8,128)(2,1)}, u32[]{:S(2)}) %copy-start) | copy-done | bytes 4194328
  46.6 14.5 %attend0.1.rest_0_ = bf16[1,128,16384]{2,1,0:T(8,128)(2,1)} custom-call(s32[5]{0:T(128)S(1)} %pad_add_fusion.where, bf16[1,128,16384]{2,1,0:T(8,128)(2,1)S(1)} %copy-done, bf16[2,128,640]{2,1,0:T(8,128)(2,1)S(1)} %pad_maximum_fusion.2.own, bf16[2,128,640]{2,1,0:T(8,128)(2,1)S(1)} %collective-permute-done.3.near, ...), custom_call_target="tpu_custom_call" | custom-call | flops 5033164800 | bytes 5242880 | tf_op jit(solution)/shard_map/attend0/pallas_call | solution.py:174
  61.1 0.0 collective-permute-done.2.swapped
  61.1 9.6 %attend5.1 = bf16[1,128,16384]{2,1,0:T(8,128)(2,1)} custom-call(s32[5]{0:T(128)S(1)} %pad_add_fusion.where, bf16[1,128,16384]{2,1,0:T(8,128)(2,1)S(1)} %copy-done, bf16[2,128,384]{2,1,0:T(8,128)(2,1)S(1)} %pad_maximum_fusion.3.own, bf16[2,128,384]{2,1,0:T(8,128)(2,1)S(1)} %collective-permute-done.near, ...), custom_call_target="tpu_custom_call", output_to_operand_aliasing={{}: (6, {})} | custom-call | flops 3019898880 | bytes 3145728 | tf_op jit(solution)/shard_map/attend5/pallas_call | solution.py:174
  70.7 0.0 all-to-all-done
  70.7 0.7 fusion
  71.5 0.3 copy_bitcast_fusion
  71.8 1.3 %copy.19 = bf16[128,1,2,1024]{3,2,1,0:T(2,128)(2,1)} copy(bf16[128,1,2,1024]{3,0,2,1:T(8,128)(2,1)S(1)} %get-tuple-element.20) | data formatting | bytes 1048576
  73.1 1.3 %copy.20 = bf16[128,1,2,1024]{3,2,1,0:T(2,128)(2,1)} copy(bf16[128,1,2,1024]{3,0,2,1:T(8,128)(2,1)S(1)} %get-tuple-element.19) | data formatting | bytes 1048576
  74.4 0.1 slice_bitcast_fusion
  74.6 0.7 copy.21
  75.2 0.7 copy.22
  (7 shorter events, 0.2 us)
Async XLA Ops:
  0.6 10.0 %copy-start.2 = (bf16[1,128,1024]{2,1,0:T(8,128)(2,1)S(1)}, bf16[1,128,1024]{2,1,0:T(8,128)(2,1)}, u32[]{:S(2)}) copy-start(bf16[1,128,1024]{2,1,0:T(8,128)(2,1)} %keys.1) | copy-start | bytes 786436
  0.6 10.0 %copy-start.1 = (bf16[1,128,1024]{2,1,0:T(8,128)(2,1)S(1)}, bf16[1,128,1024]{2,1,0:T(8,128)(2,1)}, u32[]{:S(2)}) copy-start(bf16[1,128,1024]{2,1,0:T(8,128)(2,1)} %values.1) | copy-start | bytes 786436
  2.6 12.1 %collective-permute-start.4 = (bf16[2,128,640]{2,1,0:T(8,128)(2,1)S(1)}, bf16[2,128,640]{2,1,0:T(8,128)(2,1)S(1)}, u32[]{:S(2)}, u32[]{:S(2)}) collective-permute-start(bf16[2,128,640]{2,1,0:T(8,128)(2,1)S(1)} %pad_maximum_fusion.2.own), channel_id=1, source_target_pairs={{0,64},{16,80},{32,96},{48,112},{1,65},{17,81},{33,97},{49,113},{2... | collective-permute-start | bytes 983048 | tf_op jit(solution)/shard_map/ppermute | solution.py:205
  8.3 13.4 %collective-permute-start.3 = (bf16[2,128,640]{2,1,0:T(8,128)(2,1)S(1)}, bf16[2,128,640]{2,1,0:T(8,128)(2,1)S(1)}, u32[]{:S(2)}, u32[]{:S(2)}) collective-permute-start(bf16[2,128,640]{2,1,0:T(8,128)(2,1)S(1)} %pad_maximum_fusion.2.own), channel_id=1, source_target_pairs={{0,32},{16,48},{32,64},{48,80},{64,96},{80,112},{1,33},{17,49},{33... | collective-permute-start | bytes 983048 | tf_op jit(solution)/shard_map/ppermute | solution.py:205
  10.7 20.4 %copy-start.3 = (s32[1,16,1]{1,2,0:T(1,128)S(1)}, s32[1,16,1]{1,2,0:T(1,128)}, u32[]{:S(2)}) copy-start(s32[1,16,1]{1,2,0:T(1,128)} %param.9) | copy-start | bytes 196
  22.6 21.8 %collective-permute-start.5 = (bf16[2,2,128,640]{3,2,1,0:T(8,128)(2,1)}, bf16[2,2,128,640]{3,2,1,0:T(8,128)(2,1)}, u32[]{:S(2)}, u32[]{:S(2)}) collective-permute-start(bf16[2,2,128,640]{3,2,1,0:T(8,128)(2,1)} %pad_maximum_fusion), channel_id=1, source_target_pairs={{0,16},{16,0},{32,48},{48,32},{64,80},{80,64},{96,112},{112,96},{1... | collective-permute-start | bytes 1966088 | tf_op jit(solution)/shard_map/ppermute | solution.py:222
  24.2 18.9 %collective-permute-start.1 = (bf16[2,128,384]{2,1,0:T(8,128)(2,1)S(1)}, bf16[2,128,384]{2,1,0:T(8,128)(2,1)S(1)}, u32[]{:S(2)}, u32[]{:S(2)}) collective-permute-start(bf16[2,128,384]{2,1,0:T(8,128)(2,1)S(1)} %pad_maximum_fusion.3.own), channel_id=1, source_target_pairs={{0,64},{16,80},{32,96},{48,112},{1,65},{17,81},{33,97},{49,113},{2... | collective-permute-start | bytes 589832 | tf_op jit(solution)/shard_map/ppermute | solution.py:205
  29.8 13.4 %collective-permute-start = (bf16[2,128,384]{2,1,0:T(8,128)(2,1)S(1)}, bf16[2,128,384]{2,1,0:T(8,128)(2,1)S(1)}, u32[]{:S(2)}, u32[]{:S(2)}) collective-permute-start(bf16[2,128,384]{2,1,0:T(8,128)(2,1)S(1)} %pad_maximum_fusion.3.own), channel_id=1, source_target_pairs={{0,32},{16,48},{32,64},{48,80},{64,96},{80,112},{1,33},{17,49},{33... | collective-permute-start | bytes 589832 | tf_op jit(solution)/shard_map/ppermute | solution.py:205
  35.4 7.7 %copy-start.4 = (s32[1,4]{1,0:T(1,128)S(1)}, s32[1,4]{1,0:T(1,128)}, u32[]{:S(2)}) copy-start(s32[1,4]{1,0:T(1,128)} %param.8) | copy-start | bytes 52
  35.4 35.4 %all-to-all-start = ((bf16[128,2,2176]{2,1,0:T(2,128)(2,1)}), bf16[128,2,2176]{2,1,0:T(2,128)(2,1)S(1)}, u32[]{:S(2)}, u32[]{:S(2)}) async-start(bf16[128,2,2176]{2,1,0:T(2,128)(2,1)} %reshape.21), calls=%async_computation | async-start | bytes 2228224 | tf_op jit(solution)/shard_map/all_to_all | solution.py:217
  43.2 17.8 %collective-permute-start.2 = (bf16[2,2,128,384]{3,2,1,0:T(8,128)(2,1)S(1)}, bf16[2,2,128,384]{3,2,1,0:T(8,128)(2,1)S(1)}, u32[]{:S(2)}, u32[]{:S(2)}) collective-permute-start(bf16[2,2,128,384]{3,2,1,0:T(8,128)(2,1)S(1)} %pad_maximum_fusion.1), channel_id=1, source_target_pairs={{0,16},{16,0},{32,48},{48,32},{64,80},{80,64},{96,112},{112,96},{1... | collective-permute-start | bytes 1179656 | tf_op jit(solution)/shard_map/ppermute | solution.py:222
  44.4 2.2 %copy-start = (bf16[1,128,16384]{2,1,0:T(8,128)(2,1)S(1)}, bf16[1,128,16384]{2,1,0:T(8,128)(2,1)}, u32[]{:S(2)}) copy-start(bf16[1,128,16384]{2,1,0:T(8,128)(2,1)} %queries.3) | copy-start | bytes 12582916

commit v2 on v1

v2 whole, which is shorter than its diff:
```python
import functools
import math

import jax
import jax.numpy as jnp
from jax import lax
from jax.experimental import pallas as pl
from jax.experimental.pallas import tpu as pltpu
from jax.sharding import PartitionSpec as P

HD = 128
KVH = 8
GROUP = 16
PAGE = 8
CAP = 2
REQS = 4
TOK = 128
PAGES_DEV = 16
OWNERS = 16
BLOCKS = 5
WINDOW = BLOCKS * TOK
ROW = 2 * PAGE * HD + HD
STACK = 8
STACK_TOP = 4
HEAD_WIDTH = GROUP * HD
SUM_LEAST = 2.0**-100
SUM_MOST = 2.0**100
PARTS = ((0, 8),)
EXP_SCALE = math.log2(math.e) / math.sqrt(HD)
INV_ROOT = 1.0 / math.sqrt(HD)
NT = (((1,), (1,)), ((), ()))
NN = (((1,), (0,)), ((), ()))
CHEAP = pl.CostEstimate(flops=1000, bytes_accessed=1000, transcendentals=0)
HBM = pl.BlockSpec(memory_space=pltpu.HBM)
SMEM = pl.BlockSpec(memory_space=pltpu.SMEM)
VMEM = pl.BlockSpec(memory_space=pltpu.VMEM)


def iota(shape, axis):
    return lax.broadcasted_iota(jnp.int32, shape, axis)


def pack_kernel(owners, keys, values, out):
    row, col = iota((HD, HD), 0), iota((HD, HD), 1)
    common = row & col
    parity = jnp.zeros((HD, HD), jnp.int32)
    for bit in range(7):
        parity = parity + ((common >> bit) & 1)
    signs = (1 - 2 * (parity & 1)).astype(jnp.float32).astype(jnp.bfloat16)
    position = iota((1, TOK), 1)
    page, within = position // PAGE, position % PAGE
    slot = jnp.zeros((1, TOK), jnp.int32)
    for p in range(PAGES_DEV):
        rank = jnp.int32(0)
        for q in range(p):
            rank = rank + (owners[q] == owners[p]).astype(jnp.int32)
        slot = jnp.where(page == p, owners[p] * CAP + rank, slot)
    slots = OWNERS * CAP
    place = iota((PAGE * slots, TOK), 0)
    select = jnp.where((place % slots == slot) & (place // slots == within), 1.0, 0.0).astype(jnp.bfloat16)
    any_row = jnp.where(iota((slots, TOK), 0) == slot, 1.0, 0.0).astype(jnp.bfloat16)
    lane, in_page = iota((TOK, HD), 1), iota((TOK, HD), 0) % PAGE
    for h in range(KVH):
        scales = jnp.zeros((TOK, HD), jnp.float32)
        for which, rows in enumerate((keys, values)):
            rotated = (
                lax.dot_general(rows[0, :, h * HD : (h + 1) * HD], signs, NN, preferred_element_type=jnp.float32)
                * INV_ROOT
            )
            scale = (jnp.max(jnp.abs(rotated), axis=-1, keepdims=True) + 1e-06).astype(jnp.bfloat16)
            scale = scale.astype(jnp.float32)
            codes = (rotated / scale).astype(jnp.bfloat16)
            placed = lax.dot_general(select, codes, NN, preferred_element_type=jnp.float32).astype(jnp.bfloat16)
            for i in range(PAGE):
                at = (which * PAGE + i) * HD
                out[h, :, at : at + HD] = placed[i * slots : (i + 1) * slots]
            scales = jnp.where(lane == which * PAGE + in_page, scale, scales)
        out[h, :, 2 * PAGE * HD :] = lax.dot_general(
            any_row, scales.astype(jnp.bfloat16), NN, preferred_element_type=jnp.float32
        ).astype(jnp.bfloat16)


def pack(owners, keys, values):
    return pl.pallas_call(
        pack_kernel,
        in_specs=[SMEM, VMEM, VMEM],
        out_specs=VMEM,
        out_shape=jax.ShapeDtypeStruct((KVH, OWNERS * CAP, ROW), jnp.bfloat16),
        compiler_params=pltpu.CompilerParams(vmem_limit_bytes=24 * 2**20),
        cost_estimate=CHEAP,
        name="pack",
    )(owners, keys, values)


def unpack_kernel(received, cache_keys, cache_values, key_scales, value_scales, sem):
    half = PAGE * HD
    copies = [
        pltpu.make_async_copy(received.at[:, :, pl.ds(0, half)], cache_keys.at[:, 0], sem.at[0]),
        pltpu.make_async_copy(received.at[:, :, pl.ds(half, half)], cache_values.at[:, 0], sem.at[1]),
    ]
    for copy in copies:
        copy.start()
    for slot in range(CAP):
        turned = received[:, slot, 2 * half :].T
        key_scales[slot] = turned[:PAGE]
        value_scales[slot] = turned[PAGE : 2 * PAGE]
    for copy in copies:
        copy.wait()


def unpack(received):
    sources = received.shape[0]
    cache = jax.ShapeDtypeStruct((sources, 1, CAP, PAGE * HD), jnp.bfloat16)
    scales = jax.ShapeDtypeStruct((CAP, PAGE, sources), jnp.bfloat16)
    cache_keys, cache_values, key_scales, value_scales = pl.pallas_call(
        unpack_kernel,
        in_specs=[VMEM],
        out_specs=[HBM, HBM, VMEM, VMEM],
        out_shape=[cache, cache, scales, scales],
        scratch_shapes=[pltpu.SemaphoreType.DMA((2,))],
        cost_estimate=CHEAP,
        name="unpack",
    )(received)
    return (
        cache_keys,
        cache_values,
        key_scales.transpose(2, 0, 1)[:, None],
        value_scales.transpose(2, 0, 1)[:, None],
    )


def attend_kernel(first, heads, where, queries, keys, values, near_keys, near_values, far_keys, far_values, swapped, *rest):
    out, q_buf, o_buf, bias, sums, q_sem, o_sem = rest[-7:]
    key_blocks = (far_keys, swapped.at[0], near_keys, swapped.at[1], keys)
    value_blocks = (far_values, swapped.at[2], near_values, swapped.at[3], values)

    def query_copy(h):
        at = pl.ds(pl.multiple_of(h * HEAD_WIDTH, HEAD_WIDTH), HEAD_WIDTH)
        from_at = pl.ds(pl.multiple_of((first + h) * HEAD_WIDTH, HEAD_WIDTH), HEAD_WIDTH)
        return pltpu.make_async_copy(queries.at[0, :, from_at], q_buf.at[:, at], q_sem.at[h])

    def out_copy(h, g0):
        width = STACK * HD
        at = pl.ds(pl.multiple_of(h * HEAD_WIDTH + g0 * HD, width), width)
        to_at = pl.ds(pl.multiple_of((first + h) * HEAD_WIDTH + g0 * HD, width), width)
        return pltpu.make_async_copy(o_buf.at[:, at], out.at[0, :, to_at], o_sem.at[h])

    for h in range(heads):
        query_copy(h).start()

    ctx = where[0]
    core = lax.rem(ctx, 2)
    query_pos = ctx * TOK + iota((TOK, TOK), 1)
    start = jnp.zeros((TOK, TOK), jnp.int32)
    end = jnp.int32(0)
    for r in range(REQS):
        end = end + where[1 + r]
        start = jnp.where(query_pos >= end, end, start)
    back = (4, jnp.where(core == 0, 3, 1), 2, jnp.where(core == 0, 1, 3), 0)
    for b in range(BLOCKS):
        key_pos = (ctx - back[b]) * TOK + iota((TOK, TOK), 0)
        kept = (key_pos >= start) & (key_pos <= query_pos)
        bias[b * TOK : (b + 1) * TOK, :] = jnp.where(kept, 0.0, -1e30)
    sums[0] = jnp.ones((8, STACK * TOK), jnp.float32)
    sums[1] = jnp.ones((8, STACK * TOK), jnp.float32)
    ones = jnp.ones((16, WINDOW), jnp.bfloat16)
    def one_head(h, stack, with_top):
        lanes = pl.ds(pl.multiple_of((first + h) * HD, HD), HD)
        key_rows = jnp.concatenate([block[0, :, lanes] if len(block.shape) == 3 else block[:, lanes] for block in key_blocks], 0)
        value_rows = jnp.concatenate([block[0, :, lanes] if len(block.shape) == 3 else block[:, lanes] for block in value_blocks], 0)
        value_side = jnp.concatenate([value_rows.T, ones], 0)
        mask = jnp.concatenate([bias[...]] * stack, 1)

        def head_lanes(h, g):
            return pl.ds(pl.multiple_of(h * HEAD_WIDTH + g * HD, HD), HD)

        def score(g0):
            rows = jnp.concatenate([q_buf[:, head_lanes(h, g0 + g)] for g in range(stack)], 0)
            return lax.dot_general(key_rows, rows, NT, preferred_element_type=jnp.float32)

        def finish(g0, scores):
            if with_top:
                masked = scores + mask
                exponent = (masked - jnp.max(masked, axis=0, keepdims=True)) * EXP_SCALE
            else:
                exponent = scores * EXP_SCALE + mask
            weights = jnp.exp2(exponent).astype(jnp.bfloat16)
            mixed = lax.dot_general(value_side, weights, NN, preferred_element_type=jnp.float32)
            if not with_top:
                total = mixed[HD : HD + 8]
                sums[0] = jnp.minimum(sums[0], total)
                sums[1] = jnp.maximum(sums[1], total)
            result = (mixed[:HD] * (1.0 / mixed[HD : HD + 1])).astype(jnp.bfloat16)
            for g in range(stack):
                o_buf[:, head_lanes(h, g0 + g)] = result[:, g * TOK : (g + 1) * TOK].T
            if (g0 + stack) % STACK == 0:
                out_copy(h, g0 + stack - STACK).start()

        scores = score(0)
        for g0 in range(0, GROUP, stack):
            following = score(g0 + stack) if g0 + stack < GROUP else None
            finish(g0, scores)
            scores = following

    def first_pass(h, carry):
        query_copy(h).wait()
        one_head(h, STACK, False)
        return carry

    def wait_out(h, carry):
        for g0 in range(0, GROUP, STACK):
            out_copy(h, g0).wait()
        return carry

    lax.fori_loop(0, heads, first_pass, 0)
    lax.fori_loop(0, heads, wait_out, 0)

    in_range = (jnp.min(sums[0]) > SUM_LEAST) & (jnp.max(sums[1]) < SUM_MOST)

    @pl.when(jnp.logical_not(in_range))
    def _():
        def second_pass(h, carry):
            one_head(h, STACK_TOP, True)
            return wait_out(h, carry)

        lax.fori_loop(0, heads, second_pass, 0)


def attend(first, heads, where, queries, *operands, partial=None):
    more = () if partial is None else (partial,)
    return pl.pallas_call(
        functools.partial(attend_kernel, first, heads),
        in_specs=[SMEM, HBM] + [VMEM] * len(operands) + [HBM] * len(more),
        out_specs=HBM,
        out_shape=jax.ShapeDtypeStruct(queries.shape, jnp.bfloat16),
        scratch_shapes=[
            pltpu.VMEM((TOK, heads * HEAD_WIDTH), jnp.bfloat16),
            pltpu.VMEM((TOK, heads * HEAD_WIDTH), jnp.bfloat16),
            pltpu.VMEM((WINDOW, TOK), jnp.float32),
            pltpu.VMEM((2, 8, STACK * TOK), jnp.float32),
            pltpu.SemaphoreType.DMA((heads,)),
            pltpu.SemaphoreType.DMA((heads,)),
        ],
        input_output_aliases={2 + len(operands): 0} if more else {},
        compiler_params=pltpu.CompilerParams(vmem_limit_bytes=51 * 2**20),
        cost_estimate=CHEAP,
        name=f"attend{first}",
    )(where, queries, *operands, *more)


def body(queries, keys, values, lengths, owners):
    ctx_index = lax.axis_index("ctx")
    ctx_count = lax.axis_size("ctx")
    where = jnp.concatenate([ctx_index.astype(jnp.int32).reshape(1), lengths[0]])

    def chips_on(block, chips):
        step = 2 * chips
        return lax.ppermute(block, "ctx", [(i, (i + step) % ctx_count) for i in range(ctx_count)])

    near_keys, near_values = chips_on(keys, 1), chips_on(values, 1)
    far_keys, far_values = chips_on(keys, 2), chips_on(values, 2)

    message = pack(owners.reshape(PAGES_DEV), keys, values)
    message = message.reshape(KVH * OWNERS, CAP, ROW)
    received = lax.all_to_all(message, ("ctx", "dec"), split_axis=0, concat_axis=0, tiled=True)

    even = ctx_index % 2 == 0
    handed = [
        jnp.where(even, keys, far_keys),
        near_keys,
        jnp.where(even, values, far_values),
        near_values,
    ]
    swapped = lax.ppermute(jnp.concatenate(handed, 0), "ctx", [(i, i ^ 1) for i in range(ctx_count)])
    attended = None
    for first, heads in PARTS:
        attended = attend(
            first,
            heads,
            where,
            queries,
            keys,
            values,
            near_keys,
            near_values,
            far_keys,
            far_values,
            swapped,
            partial=attended,
        )
    attended, received = lax.optimization_barrier((attended, received))
    return (attended,) + unpack(received)


def solution(mesh):
    placed = (
        P("dec", "ctx", None),
        P("dec", "ctx", None),
        P("dec", "ctx", None),
        P("dec", None),
        P("dec", "ctx", None),
    )
    return jax.shard_map(
        body,
        mesh=mesh,
        in_specs=placed,
        out_specs=(
            P("dec", "ctx", None),
            P(None, "ctx", "dec", None),
            P(None, "ctx", "dec", None),
            P(None, "ctx", "dec", None),
            P(None, "ctx", "dec", None),
        ),
        check_vma=False,
    )
```

time: 76.3 us -> 85.8 us (1.12)
  the two profiles are of different devices: /device:TPU:1 before, /device:TPU:107 now
where the time goes in v2:
time: 85.8 us; the launch traced here: 85.5 us
  Pallas kernels  46.8 us (55%)
  starting transfers between devices  18.4 us (21%)
  waiting for transfers between devices  14.5 us (17%)
  local copies, waits for them, and re-layouts  4.83 us (6%)
    pallas_call x1, Pallas kernels, attend(): pl.pallas_call(functools.partial(attend_kernel, first, heads), in_specs=[...  40.9 us
    ppermute x4, waiting for transfers between devices, chips_on(): lax.ppermute(block, 'ctx', [(i, (i + step) % ctx_count) for i in range(ct...  12.3 us
    all_to_all x1, starting transfers between devices, body(): lax.all_to_all(message, ('ctx', 'dec'), split_axis=0, concat_axis=0, tile...  9.99 us
    ppermute x4, starting transfers between devices, chips_on(): lax.ppermute(block, 'ctx', [(i, (i + step) % ctx_count) for i in range(ct...  5.35 us
    unnamed x14, local copies, waits for them, and re-layouts  3.56 us
    ppermute x1, starting transfers between devices, body(): lax.ppermute(jnp.concatenate(handed, 0), 'ctx', [(i, i ^ 1) for i in rang...  3.04 us
    pallas_call x1, Pallas kernels, pack(): pl.pallas_call(pack_kernel, in_specs=[SMEM, VMEM, VMEM], out_specs=VMEM,...  3.01 us
    pallas_call x1, Pallas kernels, unpack(): pl.pallas_call(unpack_kernel, in_specs=[VMEM], out_specs=[HBM, HBM, VMEM,...  2.83 us
  transfers between devices with their start and end apart: 6, of which 2 were waited for; matrix products, arithmetic and copies ran while one was open for 2% of the time, Pallas kernels for 51%

profile of v2, /device:TPU:107, one launch (start us, length us, event | category | flops | bytes accessed | tf_op | source)
XLA Modules:
  0.0 85.5 jit_solution(10615732799431051049)
XLA Ops:
  0.6 2.1 %collective-permute-start.3 = (bf16[1,128,1024]{2,1,0:T(8,128)(2,1)}, bf16[1,128,1024]{2,1,0:T(8,128)(2,1)S(1)}, u32[]{:S(2)}, u32[]{:S(2)}) collective-permute-start(bf16[1,128,1024]{2,1,0:T(8,128)(2,1)} %values.3), channel_id=1, source_target_pairs={{0,64},{16,80},{32,96},{48,112},{64,0},{80,16},{96,32},{112,48},{1... | collective-permute-start | bytes 786440 | tf_op jit(solution)/shard_map/ppermute | solution.py:258
  2.7 1.0 %collective-permute-start.2 = (bf16[1,128,1024]{2,1,0:T(8,128)(2,1)}, bf16[1,128,1024]{2,1,0:T(8,128)(2,1)S(1)}, u32[]{:S(2)}, u32[]{:S(2)}) collective-permute-start(bf16[1,128,1024]{2,1,0:T(8,128)(2,1)} %keys.3), channel_id=1, source_target_pairs={{0,64},{16,80},{32,96},{48,112},{64,0},{80,16},{96,32},{112,48},{1... | collective-permute-start | bytes 786440 | tf_op jit(solution)/shard_map/ppermute | solution.py:258
  3.7 1.3 %collective-permute-start = (bf16[1,128,1024]{2,1,0:T(8,128)(2,1)}, bf16[1,128,1024]{2,1,0:T(8,128)(2,1)S(1)}, u32[]{:S(2)}, u32[]{:S(2)}) collective-permute-start(bf16[1,128,1024]{2,1,0:T(8,128)(2,1)} %keys.3), channel_id=1, source_target_pairs={{0,32},{16,48},{32,64},{48,80},{64,96},{80,112},{96,0},{112,16},{1... | collective-permute-start | bytes 786440 | tf_op jit(solution)/shard_map/ppermute | solution.py:258
  5.0 1.0 %collective-permute-start.1 = (bf16[1,128,1024]{2,1,0:T(8,128)(2,1)}, bf16[1,128,1024]{2,1,0:T(8,128)(2,1)S(1)}, u32[]{:S(2)}, u32[]{:S(2)}) collective-permute-start(bf16[1,128,1024]{2,1,0:T(8,128)(2,1)} %values.3), channel_id=1, source_target_pairs={{0,32},{16,48},{32,64},{48,80},{64,96},{80,112},{96,0},{112,16},{1... | collective-permute-start | bytes 786440 | tf_op jit(solution)/shard_map/ppermute | solution.py:258
  6.0 0.0 copy-start
  6.0 0.9 %copy-done = bf16[1,128,1024]{2,1,0:T(8,128)(2,1)S(1)} copy-done((bf16[1,128,1024]{2,1,0:T(8,128)(2,1)S(1)}, bf16[1,128,1024]{2,1,0:T(8,128)(2,1)}, u32[]{:S(2)}) %copy-start) | copy-done | bytes 262168
  6.9 0.0 copy-start.2
  6.9 0.9 %copy-done.2 = bf16[1,128,1024]{2,1,0:T(8,128)(2,1)S(1)} copy-done((bf16[1,128,1024]{2,1,0:T(8,128)(2,1)S(1)}, bf16[1,128,1024]{2,1,0:T(8,128)(2,1)}, u32[]{:S(2)}) %copy-start.2) | copy-done | bytes 262168
  7.9 0.0 copy-start.4
  7.9 0.7 copy-done.4
  8.5 3.0 %pack.1 = bf16[8,32,2176]{2,1,0:T(8,128)(2,1)S(1)} custom-call(s32[16]{0:T(128)S(1)} %bitcast.9, bf16[1,128,1024]{2,1,0:T(8,128)(2,1)S(1)} %copy-done, bf16[1,128,1024]{2,1,0:T(8,128)(2,1)S(1)} %copy-done.2), custom_call_target="tpu_custom_call" | custom-call | flops 1000 | bytes 1000 | tf_op jit(solution)/shard_map/pack/pallas_call | solution.py:84
  11.6 1.3 %reshape.21 = bf16[128,2,2176]{2,1,0:T(2,128)(2,1)} reshape(bf16[8,32,2176]{2,1,0:T(8,128)(2,1)S(1)} %pack.1) | data formatting | bytes 2228224 | tf_op jit(solution)/shard_map/reshape | solution.py:264
  12.8 0.0 copy-start.3
  12.8 0.0 copy-start.1
  12.8 10.0 %all-to-all-start = ((bf16[128,2,2176]{2,1,0:T(2,128)(2,1)}), bf16[128,2,2176]{2,1,0:T(2,128)(2,1)S(1)}, u32[]{:S(2)}, u32[]{:S(2)}) async-start(bf16[128,2,2176]{2,1,0:T(2,128)(2,1)} %reshape.21), calls=%async_computation | async-start | bytes 2228224 | tf_op jit(solution)/shard_map/all_to_all | solution.py:265
  22.8 0.0 collective-permute-done.3.far_values
  22.8 0.0 copy-done.3
  22.9 0.0 collective-permute-done.2.far_keys
  22.9 0.0 copy-done.1
  23.0 0.0 copy-start.6
  23.0 0.0 collective-permute-done.near_keys
  23.0 12.3 %collective-permute-done.1.near_values = bf16[1,128,1024]{2,1,0:T(8,128)(2,1)S(1)} collective-permute-done((bf16[1,128,1024]{2,1,0:T(8,128)(2,1)}, bf16[1,128,1024]{2,1,0:T(8,128)(2,1)S(1)}, u32[]{:S(2)}, u32[]{:S(2)}) %collective-permute-start.1) | collective-permute-done | bytes 262176 | tf_op jit(solution)/shard_map/ppermute | solution.py:258
  35.3 0.1 pad_maximum_fusion
  35.4 3.0 %collective-permute-start.4 = (bf16[4,128,1024]{2,1,0:T(8,128)(2,1)S(1)}, bf16[4,128,1024]{2,1,0:T(8,128)(2,1)S(1)}, u32[]{:S(2)}, u32[]{:S(2)}) collective-permute-start(bf16[4,128,1024]{2,1,0:T(8,128)(2,1)S(1)} %pad_maximum_fusion), channel_id=1, source_target_pairs={{0,16},{16,0},{32,48},{48,32},{64,80},{80,64},{96,112},{112,96},{1... | collective-permute-start | bytes 3145736 | tf_op jit(solution)/shard_map/ppermute | solution.py:274
  38.5 0.0 copy-done.6
  38.5 0.1 pad_add_fusion.where
  38.5 2.2 %collective-permute-done.4.swapped = bf16[4,128,1024]{2,1,0:T(8,128)(2,1)S(1)} collective-permute-done((bf16[4,128,1024]{2,1,0:T(8,128)(2,1)S(1)}, bf16[4,128,1024]{2,1,0:T(8,128)(2,1)S(1)}, u32[]{:S(2)}, u32[]{:S(2)}) %collective-permute-start.4) | collective-permute-done | bytes 1048608 | tf_op jit(solution)/shard_map/ppermute | solution.py:274
  40.8 40.9 %attend0.1 = bf16[1,128,16384]{2,1,0:T(8,128)(2,1)} custom-call(s32[5]{0:T(128)S(1)} %pad_add_fusion.where, bf16[1,128,16384]{2,1,0:T(8,128)(2,1)} %queries.1, bf16[1,128,1024]{2,1,0:T(8,128)(2,1)S(1)} %copy-done.1, bf16[1,128,1024]{2,1,0:T(8,128)(2,1)S(1)} %copy-done.3, bf16[1,128,1024]{2,1,0:T(8,128)(2,1)S(1)} %collective-permute-done.near_keys, ...), custom_call_target="tpu_custom_call" | custom-call | flops 1000 | bytes 1000 | tf_op jit(solution)/shard_map/attend0/pallas_call | solution.py:231
  81.7 0.0 all-to-all-done.received
  81.7 0.0 copy-start.5
  81.7 1.0 %copy-done.5 = bf16[128,2,2176]{2,1,0:T(2,128)(2,1)} copy-done((bf16[128,2,2176]{2,1,0:T(2,128)(2,1)}, bf16[128,2,2176]{2,1,0:T(2,128)(2,1)S(1)}, u32[]{:S(2)}) %copy-start.5) | copy-done | bytes 1114136
  82.7 2.8 %unpack.1 = (bf16[128,1,2,1024]{3,2,1,0:T(2,128)(2,1)}, bf16[128,1,2,1024]{3,2,1,0:T(2,128)(2,1)}, bf16[2,8,128]{2,1,0:T(8,128)(2,1)}, bf16[2,8,128]{2,1,0:T(8,128)(2,1)}) custom-call(bf16[128,2,2176]{2,1,0:T(2,128)(2,1)} %copy-done.5), custom_call_target="tpu_custom_call" | custom-call | flops 1000 | bytes 1000 | tf_op jit(solution)/shard_map/unpack/pallas_call | solution.py:115
  (2 shorter events, 0.1 us)
Async XLA Ops:
  0.6 22.2 %collective-permute-start.3 = (bf16[1,128,1024]{2,1,0:T(8,128)(2,1)}, bf16[1,128,1024]{2,1,0:T(8,128)(2,1)S(1)}, u32[]{:S(2)}, u32[]{:S(2)}) collective-permute-start(bf16[1,128,1024]{2,1,0:T(8,128)(2,1)} %values.3), channel_id=1, source_target_pairs={{0,64},{16,80},{32,96},{48,112},{64,0},{80,16},{96,32},{112,48},{1... | collective-permute-start | bytes 786440 | tf_op jit(solution)/shard_map/ppermute | solution.py:258
  2.7 20.2 %collective-permute-start.2 = (bf16[1,128,1024]{2,1,0:T(8,128)(2,1)}, bf16[1,128,1024]{2,1,0:T(8,128)(2,1)S(1)}, u32[]{:S(2)}, u32[]{:S(2)}) collective-permute-start(bf16[1,128,1024]{2,1,0:T(8,128)(2,1)} %keys.3), channel_id=1, source_target_pairs={{0,64},{16,80},{32,96},{48,112},{64,0},{80,16},{96,32},{112,48},{1... | collective-permute-start | bytes 786440 | tf_op jit(solution)/shard_map/ppermute | solution.py:258
  3.7 19.3 %collective-permute-start = (bf16[1,128,1024]{2,1,0:T(8,128)(2,1)}, bf16[1,128,1024]{2,1,0:T(8,128)(2,1)S(1)}, u32[]{:S(2)}, u32[]{:S(2)}) collective-permute-start(bf16[1,128,1024]{2,1,0:T(8,128)(2,1)} %keys.3), channel_id=1, source_target_pairs={{0,32},{16,48},{32,64},{48,80},{64,96},{80,112},{96,0},{112,16},{1... | collective-permute-start | bytes 786440 | tf_op jit(solution)/shard_map/ppermute | solution.py:258
  5.0 30.3 %collective-permute-start.1 = (bf16[1,128,1024]{2,1,0:T(8,128)(2,1)}, bf16[1,128,1024]{2,1,0:T(8,128)(2,1)S(1)}, u32[]{:S(2)}, u32[]{:S(2)}) collective-permute-start(bf16[1,128,1024]{2,1,0:T(8,128)(2,1)} %values.3), channel_id=1, source_target_pairs={{0,32},{16,48},{32,64},{48,80},{64,96},{80,112},{96,0},{112,16},{1... | collective-permute-start | bytes 786440 | tf_op jit(solution)/shard_map/ppermute | solution.py:258
  6.0 0.9 %copy-start = (bf16[1,128,1024]{2,1,0:T(8,128)(2,1)S(1)}, bf16[1,128,1024]{2,1,0:T(8,128)(2,1)}, u32[]{:S(2)}) copy-start(bf16[1,128,1024]{2,1,0:T(8,128)(2,1)} %keys.3) | copy-start | bytes 786436
  6.9 0.9 %copy-start.2 = (bf16[1,128,1024]{2,1,0:T(8,128)(2,1)S(1)}, bf16[1,128,1024]{2,1,0:T(8,128)(2,1)}, u32[]{:S(2)}) copy-start(bf16[1,128,1024]{2,1,0:T(8,128)(2,1)} %values.3) | copy-start | bytes 786436
  7.9 0.7 copy-start.4
  12.8 10.0 %copy-start.3 = (bf16[1,128,1024]{2,1,0:T(8,128)(2,1)S(1)}, bf16[1,128,1024]{2,1,0:T(8,128)(2,1)}, u32[]{:S(2)}) copy-start(bf16[1,128,1024]{2,1,0:T(8,128)(2,1)} %values.3) | copy-start | bytes 786436
  12.8 10.1 %copy-start.1 = (bf16[1,128,1024]{2,1,0:T(8,128)(2,1)S(1)}, bf16[1,128,1024]{2,1,0:T(8,128)(2,1)}, u32[]{:S(2)}) copy-start(bf16[1,128,1024]{2,1,0:T(8,128)(2,1)} %keys.3) | copy-start | bytes 786436
  12.8 68.9 %all-to-all-start = ((bf16[128,2,2176]{2,1,0:T(2,128)(2,1)}), bf16[128,2,2176]{2,1,0:T(2,128)(2,1)S(1)}, u32[]{:S(2)}, u32[]{:S(2)}) async-start(bf16[128,2,2176]{2,1,0:T(2,128)(2,1)} %reshape.21), calls=%async_computation | async-start | bytes 2228224 | tf_op jit(solution)/shard_map/all_to_all | solution.py:265
  23.0 15.5 %copy-start.6 = (s32[1,4]{1,0:T(1,128)S(1)}, s32[1,4]{1,0:T(1,128)}, u32[]{:S(2)}) copy-start(s32[1,4]{1,0:T(1,128)} %param.8) | copy-start | bytes 52
  35.4 5.3 %collective-permute-start.4 = (bf16[4,128,1024]{2,1,0:T(8,128)(2,1)S(1)}, bf16[4,128,1024]{2,1,0:T(8,128)(2,1)S(1)}, u32[]{:S(2)}, u32[]{:S(2)}) collective-permute-start(bf16[4,128,1024]{2,1,0:T(8,128)(2,1)S(1)} %pad_maximum_fusion), channel_id=1, source_target_pairs={{0,16},{16,0},{32,48},{48,32},{64,80},{80,64},{96,112},{112,96},{1... | collective-permute-start | bytes 3145736 | tf_op jit(solution)/shard_map/ppermute | solution.py:274
  81.7 1.0 %copy-start.5 = (bf16[128,2,2176]{2,1,0:T(2,128)(2,1)}, bf16[128,2,2176]{2,1,0:T(2,128)(2,1)S(1)}, u32[]{:S(2)}) copy-start(bf16[128,2,2176]{2,1,0:T(2,128)(2,1)S(1)} %all-to-all-done.received) | copy-start | bytes 3342340

commit v3 on v2

--- a/solution.py
+++ b/solution.py
@@ -31,6 +31,7 @@
 NT = (((1,), (1,)), ((), ()))
 NN = (((1,), (0,)), ((), ()))
 CHEAP = pl.CostEstimate(flops=1000, bytes_accessed=1000, transcendentals=0)
+ANY = pl.BlockSpec(memory_space=pl.ANY)
 HBM = pl.BlockSpec(memory_space=pltpu.HBM)
 SMEM = pl.BlockSpec(memory_space=pltpu.SMEM)
 VMEM = pl.BlockSpec(memory_space=pltpu.VMEM)
@@ -86,26 +87,35 @@
         in_specs=[SMEM, VMEM, VMEM],
         out_specs=VMEM,
         out_shape=jax.ShapeDtypeStruct((KVH, OWNERS * CAP, ROW), jnp.bfloat16),
-        compiler_params=pltpu.CompilerParams(vmem_limit_bytes=24 * 2**20),
+        compiler_params=pltpu.CompilerParams(vmem_limit_bytes=60 * 2**20),
         cost_estimate=CHEAP,
         name="pack",
     )(owners, keys, values)
 
 
-def unpack_kernel(received, cache_keys, cache_values, key_scales, value_scales, sem):
+def unpack_kernel(received, cache_keys, cache_values, key_scales, value_scales, buf, in_sem, out_sem):
     half = PAGE * HD
-    copies = [
-        pltpu.make_async_copy(received.at[:, :, pl.ds(0, half)], cache_keys.at[:, 0], sem.at[0]),
-        pltpu.make_async_copy(received.at[:, :, pl.ds(half, half)], cache_values.at[:, 0], sem.at[1]),
+    spans = ((2 * half, HD), (0, half), (half, half))
+    loads = [
+        pltpu.make_async_copy(received.at[:, :, pl.ds(at, width)], buf.at[:, :, pl.ds(at, width)], in_sem.at[n])
+        for n, (at, width) in enumerate(spans)
     ]
-    for copy in copies:
-        copy.start()
+    for load in loads:
+        load.start()
+    stores = [
+        pltpu.make_async_copy(buf.at[:, :, pl.ds(0, half)], cache_keys.at[:, 0], out_sem.at[0]),
+        pltpu.make_async_copy(buf.at[:, :, pl.ds(half, half)], cache_values.at[:, 0], out_sem.at[1]),
+    ]
+    for load, store in zip(loads[1:], stores):
+        load.wait()
+        store.start()
+    loads[0].wait()
     for slot in range(CAP):
-        turned = received[:, slot, 2 * half :].T
+        turned = buf[:, slot, 2 * half :].T
         key_scales[slot] = turned[:PAGE]
         value_scales[slot] = turned[PAGE : 2 * PAGE]
-    for copy in copies:
-        copy.wait()
+    for store in stores:
+        store.wait()
 
 
 def unpack(received):
@@ -114,10 +124,14 @@
     scales = jax.ShapeDtypeStruct((CAP, PAGE, sources), jnp.bfloat16)
     cache_keys, cache_values, key_scales, value_scales = pl.pallas_call(
         unpack_kernel,
-        in_specs=[VMEM],
+        in_specs=[ANY],
         out_specs=[HBM, HBM, VMEM, VMEM],
         out_shape=[cache, cache, scales, scales],
-        scratch_shapes=[pltpu.SemaphoreType.DMA((2,))],
+        scratch_shapes=[
+            pltpu.VMEM(received.shape, jnp.bfloat16),
+            pltpu.SemaphoreType.DMA((3,)),
+            pltpu.SemaphoreType.DMA((2,)),
+        ],
         cost_estimate=CHEAP,
         name="unpack",
     )(received)
@@ -129,11 +143,8 @@
     )
 
 
-def attend_kernel(first, heads, where, queries, keys, values, near_keys, near_values, far_keys, far_values, swapped, *rest):
+def attend_kernel(first, heads, where, queries, *rest):
     out, q_buf, o_buf, bias, sums, q_sem, o_sem = rest[-7:]
-    key_blocks = (far_keys, swapped.at[0], near_keys, swapped.at[1], keys)
-    value_blocks = (far_values, swapped.at[2], near_values, swapped.at[3], values)
-
     def query_copy(h):
         at = pl.ds(pl.multiple_of(h * HEAD_WIDTH, HEAD_WIDTH), HEAD_WIDTH)
         from_at = pl.ds(pl.multiple_of((first + h) * HEAD_WIDTH, HEAD_WIDTH), HEAD_WIDTH)
@@ -157,6 +168,7 @@
         end = end + where[1 + r]
         start = jnp.where(query_pos >= end, end, start)
     back = (4, jnp.where(core == 0, 3, 1), 2, jnp.where(core == 0, 1, 3), 0)
+    even = jnp.full((TOK, HD), core, jnp.int32) == 0
     for b in range(BLOCKS):
         key_pos = (ctx - back[b]) * TOK + iota((TOK, TOK), 0)
         kept = (key_pos >= start) & (key_pos <= query_pos)
@@ -164,10 +176,14 @@
     sums[0] = jnp.ones((8, STACK * TOK), jnp.float32)
     sums[1] = jnp.ones((8, STACK * TOK), jnp.float32)
     ones = jnp.ones((16, WINDOW), jnp.bfloat16)
+    def window(arrays, lanes):
+        own, beside, near, near_beside, far, far_beside = (array[0, :, lanes] for array in arrays)
+        third = jnp.where(even, far_beside, beside)
+        return jnp.concatenate([far, third, near, near_beside, own], 0)
+
     def one_head(h, stack, with_top):
         lanes = pl.ds(pl.multiple_of((first + h) * HD, HD), HD)
-        key_rows = jnp.concatenate([block[0, :, lanes] if len(block.shape) == 3 else block[:, lanes] for block in key_blocks], 0)
-        value_rows = jnp.concatenate([block[0, :, lanes] if len(block.shape) == 3 else block[:, lanes] for block in value_blocks], 0)
+        key_rows, value_rows = window(rest[0:12:2], lanes), window(rest[1:12:2], lanes)
         value_side = jnp.concatenate([value_rows.T, ones], 0)
         mask = jnp.concatenate([bias[...]] * stack, 1)
 
@@ -243,7 +259,7 @@
         ],
         input_output_aliases={2 + len(operands): 0} if more else {},
         compiler_params=pltpu.CompilerParams(vmem_limit_bytes=51 * 2**20),
-        cost_estimate=CHEAP,
+        cost_estimate=pl.CostEstimate(flops=8000000000, bytes_accessed=1000, transcendentals=0),
         name=f"attend{first}",
     )(where, queries, *operands, *more)
 
@@ -257,36 +273,31 @@
         step = 2 * chips
         return lax.ppermute(block, "ctx", [(i, (i + step) % ctx_count) for i in range(ctx_count)])
 
-    near_keys, near_values = chips_on(keys, 1), chips_on(values, 1)
-    far_keys, far_values = chips_on(keys, 2), chips_on(values, 2)
+    def swap(block):
+        return lax.ppermute(block, "ctx", [(i, i ^ 1) for i in range(ctx_count)])
+
+    near_values = chips_on(values, 1)
+    ahead_keys = chips_on(keys, -1)
+    near_keys = chips_on(keys, 1)
+    beside = (swap(keys), swap(values))
 
     message = pack(owners.reshape(PAGES_DEV), keys, values)
     message = message.reshape(KVH * OWNERS, CAP, ROW)
+    near_values, ahead_keys, beside, message = lax.optimization_barrier(
+        (near_values, ahead_keys, beside, message)
+    )
+    far_values = chips_on(near_values, 1)
+    far_keys = chips_on(ahead_keys, -1)
     received = lax.all_to_all(message, ("ctx", "dec"), split_axis=0, concat_axis=0, tiled=True)
 
-    even = ctx_index % 2 == 0
-    handed = [
-        jnp.where(even, keys, far_keys),
-        near_keys,
-        jnp.where(even, values, far_values),
-        near_values,
-    ]
-    swapped = lax.ppermute(jnp.concatenate(handed, 0), "ctx", [(i, i ^ 1) for i in range(ctx_count)])
+    near = (near_keys, near_values)
+    far = (far_keys, far_values)
+    near_beside = (swap(near_keys), swap(near_values))
+    far_beside = (swap(far_keys), swap(far_values))
     attended = None
     for first, heads in PARTS:
         attended = attend(
-            first,
-            heads,
-            where,
-            queries,
-            keys,
-            values,
-            near_keys,
-            near_values,
-            far_keys,
-            far_values,
-            swapped,
-            partial=attended,
+            first, heads, where, queries, keys, values, *beside, *near, *near_beside, *far, *far_beside, partial=attended
         )
     attended, received = lax.optimization_barrier((attended, received))
     return (attended,) + unpack(received)

time: 85.8 us -> 74.9 us (0.87)
  the two profiles are of different devices: /device:TPU:107 before, /device:TPU:1 now
where the time goes in v3:
time: 74.9 us; the launch traced here: 74.7 us
  Pallas kernels  48.6 us (65%)
  starting transfers between devices  20.7 us (28%)
  local copies, waits for them, and re-layouts  3.01 us (4%)
  waiting for transfers between devices  1.61 us (2%)
    pallas_call x1, Pallas kernels, attend(): pl.pallas_call(functools.partial(attend_kernel, first, heads), in_specs=[...  41.4 us
    all_to_all x1, starting transfers between devices, body(): lax.all_to_all(message, ('ctx', 'dec'), split_axis=0, concat_axis=0, tile...  11.6 us
    ppermute x5, starting transfers between devices, chips_on(): lax.ppermute(block, 'ctx', [(i, (i + step) % ctx_count) for i in range(ct...  5.44 us
    pallas_call x1, Pallas kernels, pack(): pl.pallas_call(pack_kernel, in_specs=[SMEM, VMEM, VMEM], out_specs=VMEM,...  4.5 us
    ppermute x6, starting transfers between devices, swap(): return lax.ppermute(block, 'ctx', [(i, i ^ 1) for i in range(ctx_count)])  3.67 us
    pallas_call x1, Pallas kernels, unpack(): pl.pallas_call(unpack_kernel, in_specs=[ANY], out_specs=[HBM, HBM, VMEM,...  2.69 us
    reshape x1, local copies, waits for them, and re-layouts, body(): message = message.reshape(KVH * OWNERS, CAP, ROW)  2.29 us
    ppermute x6, waiting for transfers between devices, swap(): return lax.ppermute(block, 'ctx', [(i, i ^ 1) for i in range(ctx_count)])  1.59 us
  transfers between devices with their start and end apart: 12, of which 3 were waited for; matrix products, arithmetic and copies ran while one was open for 3% of the time, Pallas kernels for 61%

profile of v3, /device:TPU:1, one launch (start us, length us, event | category | flops | bytes accessed | tf_op | source)
XLA Modules:
  0.0 74.7 jit_solution(13963488959490098405)
XLA Ops:
  0.6 1.5 %collective-permute-start.3 = (bf16[1,128,1024]{2,1,0:T(8,128)(2,1)}, bf16[1,128,1024]{2,1,0:T(8,128)(2,1)S(1)}, u32[]{:S(2)}, u32[]{:S(2)}) collective-permute-start(bf16[1,128,1024]{2,1,0:T(8,128)(2,1)} %rest_1_.1), channel_id=1, source_target_pairs={{0,16},{16,0},{32,48},{48,32},{64,80},{80,64},{96,112},{112,96},{1... | collective-permute-start | bytes 786440 | tf_op jit(solution)/shard_map/ppermute | solution.py:277
  2.1 1.4 %collective-permute-start = (bf16[1,128,1024]{2,1,0:T(8,128)(2,1)}, bf16[1,128,1024]{2,1,0:T(8,128)(2,1)S(1)}, u32[]{:S(2)}, u32[]{:S(2)}) collective-permute-start(bf16[1,128,1024]{2,1,0:T(8,128)(2,1)} %rest_1_.1), channel_id=1, source_target_pairs={{0,32},{16,48},{32,64},{48,80},{64,96},{80,112},{96,0},{112,16},{1... | collective-permute-start | bytes 786440 | tf_op jit(solution)/shard_map/ppermute | solution.py:274
  3.5 0.3 collective-permute-start.2
  3.9 1.3 %collective-permute-start.1 = (bf16[1,128,1024]{2,1,0:T(8,128)(2,1)}, bf16[1,128,1024]{2,1,0:T(8,128)(2,1)S(1)}, u32[]{:S(2)}, u32[]{:S(2)}) collective-permute-start(bf16[1,128,1024]{2,1,0:T(8,128)(2,1)} %rest_0_.1), channel_id=1, source_target_pairs={{0,96},{16,112},{32,0},{48,16},{64,32},{80,48},{96,64},{112,80},{1... | collective-permute-start | bytes 786440 | tf_op jit(solution)/shard_map/ppermute | solution.py:274
  5.2 0.2 collective-permute-start.4
  5.3 4.5 %pack.1 = bf16[8,32,2176]{2,1,0:T(8,128)(2,1)} custom-call(s32[16]{0:T(128)} %bitcast.9, bf16[1,128,1024]{2,1,0:T(8,128)(2,1)} %rest_0_.1, bf16[1,128,1024]{2,1,0:T(8,128)(2,1)} %rest_1_.1), custom_call_target="tpu_custom_call" | custom-call | flops 1000 | bytes 1000 | tf_op jit(solution)/shard_map/pack/pallas_call | solution.py:85
  9.8 2.3 %reshape.21 = bf16[128,2,2176]{2,1,0:T(2,128)(2,1)} reshape(bf16[8,32,2176]{2,1,0:T(8,128)(2,1)} %pack.1) | data formatting | bytes 2228224 | tf_op jit(solution)/shard_map/reshape | solution.py:285
  12.1 0.0 copy-start.3
  12.1 0.0 copy-start
  12.1 0.0 copy-start.1
  12.1 0.0 collective-permute-done.3.rest_3_
  12.2 0.0 collective-permute-done.rest_5_
  12.2 0.0 collective-permute-done.2.rest_2_
  12.2 0.0 collective-permute-done.1
  12.2 2.6 %collective-permute-start.7 = (bf16[1,128,1024]{2,1,0:T(8,128)(2,1)S(1)}, bf16[1,128,1024]{2,1,0:T(8,128)(2,1)S(1)}, u32[]{:S(2)}, u32[]{:S(2)}) collective-permute-start(bf16[1,128,1024]{2,1,0:T(8,128)(2,1)S(1)} %collective-permute-done.1), channel_id=1, source_target_pairs={{0,96},{16,112},{32,0},{48,16},{64,32},{80,48},{96,64},{112,80},{1... | collective-permute-start | bytes 786440 | tf_op jit(solution)/shard_map/ppermute | solution.py:274
  14.8 0.0 collective-permute-start.8
  14.8 11.6 %all-to-all-start = ((bf16[128,2,2176]{2,1,0:T(2,128)(2,1)}), bf16[128,2,2176]{2,1,0:T(2,128)(2,1)}, u32[]{:S(2)}, u32[]{:S(2)}) async-start(bf16[128,2,2176]{2,1,0:T(2,128)(2,1)} %reshape.21), calls=%async_computation | async-start | bytes 2228224 | tf_op jit(solution)/shard_map/all_to_all | solution.py:291
  26.3 1.2 %collective-permute-start.6 = (bf16[1,128,1024]{2,1,0:T(8,128)(2,1)S(1)}, bf16[1,128,1024]{2,1,0:T(8,128)(2,1)S(1)}, u32[]{:S(2)}, u32[]{:S(2)}) collective-permute-start(bf16[1,128,1024]{2,1,0:T(8,128)(2,1)S(1)} %collective-permute-done.rest_5_), channel_id=1, source_target_pairs={{0,16},{16,0},{32,48},{48,32},{64,80},{80,64},{96,112},{112,96},{1... | collective-permute-start | bytes 786440 | tf_op jit(solution)/shard_map/ppermute | solution.py:277
  27.6 0.0 collective-permute-done.4.rest_4_
  27.6 0.1 collective-permute-start.5
  27.7 0.0 collective-permute-done.7.rest_8_
  27.7 0.4 collective-permute-start.9
  28.1 0.0 collective-permute-done.8.rest_9_
  28.1 0.1 collective-permute-start.10
  28.2 0.0 copy-done.3
  28.2 0.1 pad_add_fusion.where
  28.3 0.8 %collective-permute-done.5.rest_6_ = bf16[1,128,1024]{2,1,0:T(8,128)(2,1)S(1)} collective-permute-done((bf16[1,128,1024]{2,1,0:T(8,128)(2,1)S(1)}, bf16[1,128,1024]{2,1,0:T(8,128)(2,1)S(1)}, u32[]{:S(2)}, u32[]{:S(2)}) %collective-permute-start.5) | collective-permute-done | bytes 262176 | tf_op jit(solution)/shard_map/ppermute | solution.py:277
  29.1 0.0 collective-permute-done.6.rest_7_
  29.1 0.4 collective-permute-done.9.rest_10_
  29.5 0.4 collective-permute-done.10.rest_11_
  29.8 0.0 copy-start.2
  29.8 0.7 copy-done.2
  30.5 0.0 copy-done
  30.5 0.0 copy-done.1
  30.6 41.4 %attend0.1 = bf16[1,128,16384]{2,1,0:T(8,128)(2,1)} custom-call(s32[5]{0:T(128)S(1)} %pad_add_fusion.where, bf16[1,128,16384]{2,1,0:T(8,128)(2,1)} %queries.1, bf16[1,128,1024]{2,1,0:T(8,128)(2,1)S(1)} %copy-done, bf16[1,128,1024]{2,1,0:T(8,128)(2,1)S(1)} %copy-done.1, bf16[1,128,1024]{2,1,0:T(8,128)(2,1)S(1)} %collective-permute-done.2.rest_2_, ...), custom_call_target="tpu_custom_call" | custom-call | flops 8000000000 | bytes 1000 | tf_op jit(solution)/shard_map/attend0/pallas_call | solution.py:247
  72.0 0.0 all-to-all-done.received
  72.0 2.7 %unpack.1 = (bf16[128,1,2,1024]{3,2,1,0:T(2,128)(2,1)}, bf16[128,1,2,1024]{3,2,1,0:T(2,128)(2,1)}, bf16[2,8,128]{2,1,0:T(8,128)(2,1)}, bf16[2,8,128]{2,1,0:T(8,128)(2,1)}) custom-call(bf16[128,2,2176]{2,1,0:T(2,128)(2,1)} %all-to-all-done.received), custom_call_target="tpu_custom_call" | custom-call | flops 1000 | bytes 1000 | tf_op jit(solution)/shard_map/unpack/pallas_call | solution.py:125
Async XLA Ops:
  0.6 11.5 %collective-permute-start.3 = (bf16[1,128,1024]{2,1,0:T(8,128)(2,1)}, bf16[1,128,1024]{2,1,0:T(8,128)(2,1)S(1)}, u32[]{:S(2)}, u32[]{:S(2)}) collective-permute-start(bf16[1,128,1024]{2,1,0:T(8,128)(2,1)} %rest_1_.1), channel_id=1, source_target_pairs={{0,16},{16,0},{32,48},{48,32},{64,80},{80,64},{96,112},{112,96},{1... | collective-permute-start | bytes 786440 | tf_op jit(solution)/shard_map/ppermute | solution.py:277
  2.1 10.0 %collective-permute-start = (bf16[1,128,1024]{2,1,0:T(8,128)(2,1)}, bf16[1,128,1024]{2,1,0:T(8,128)(2,1)S(1)}, u32[]{:S(2)}, u32[]{:S(2)}) collective-permute-start(bf16[1,128,1024]{2,1,0:T(8,128)(2,1)} %rest_1_.1), channel_id=1, source_target_pairs={{0,32},{16,48},{32,64},{48,80},{64,96},{80,112},{96,0},{112,16},{1... | collective-permute-start | bytes 786440 | tf_op jit(solution)/shard_map/ppermute | solution.py:274
  3.5 8.6 %collective-permute-start.2 = (bf16[1,128,1024]{2,1,0:T(8,128)(2,1)}, bf16[1,128,1024]{2,1,0:T(8,128)(2,1)S(1)}, u32[]{:S(2)}, u32[]{:S(2)}) collective-permute-start(bf16[1,128,1024]{2,1,0:T(8,128)(2,1)} %rest_0_.1), channel_id=1, source_target_pairs={{0,16},{16,0},{32,48},{48,32},{64,80},{80,64},{96,112},{112,96},{1... | collective-permute-start | bytes 786440 | tf_op jit(solution)/shard_map/ppermute | solution.py:277
  3.9 8.3 %collective-permute-start.1 = (bf16[1,128,1024]{2,1,0:T(8,128)(2,1)}, bf16[1,128,1024]{2,1,0:T(8,128)(2,1)S(1)}, u32[]{:S(2)}, u32[]{:S(2)}) collective-permute-start(bf16[1,128,1024]{2,1,0:T(8,128)(2,1)} %rest_0_.1), channel_id=1, source_target_pairs={{0,96},{16,112},{32,0},{48,16},{64,32},{80,48},{96,64},{112,80},{1... | collective-permute-start | bytes 786440 | tf_op jit(solution)/shard_map/ppermute | solution.py:274
  5.2 22.4 %collective-permute-start.4 = (bf16[1,128,1024]{2,1,0:T(8,128)(2,1)}, bf16[1,128,1024]{2,1,0:T(8,128)(2,1)S(1)}, u32[]{:S(2)}, u32[]{:S(2)}) collective-permute-start(bf16[1,128,1024]{2,1,0:T(8,128)(2,1)} %rest_0_.1), channel_id=1, source_target_pairs={{0,32},{16,48},{32,64},{48,80},{64,96},{80,112},{96,0},{112,16},{1... | collective-permute-start | bytes 786440 | tf_op jit(solution)/shard_map/ppermute | solution.py:274
  12.1 16.0 %copy-start.3 = (s32[1,4]{1,0:T(1,128)S(1)}, s32[1,4]{1,0:T(1,128)}, u32[]{:S(2)}) copy-start(s32[1,4]{1,0:T(1,128)} %param.8) | copy-start | bytes 52
  12.1 18.4 %copy-start = (bf16[1,128,1024]{2,1,0:T(8,128)(2,1)S(1)}, bf16[1,128,1024]{2,1,0:T(8,128)(2,1)}, u32[]{:S(2)}) copy-start(bf16[1,128,1024]{2,1,0:T(8,128)(2,1)} %rest_0_.1) | copy-start | bytes 786436
  12.1 18.4 %copy-start.1 = (bf16[1,128,1024]{2,1,0:T(8,128)(2,1)S(1)}, bf16[1,128,1024]{2,1,0:T(8,128)(2,1)}, u32[]{:S(2)}) copy-start(bf16[1,128,1024]{2,1,0:T(8,128)(2,1)} %rest_1_.1) | copy-start | bytes 786436
  12.2 15.5 %collective-permute-start.7 = (bf16[1,128,1024]{2,1,0:T(8,128)(2,1)S(1)}, bf16[1,128,1024]{2,1,0:T(8,128)(2,1)S(1)}, u32[]{:S(2)}, u32[]{:S(2)}) collective-permute-start(bf16[1,128,1024]{2,1,0:T(8,128)(2,1)S(1)} %collective-permute-done.1), channel_id=1, source_target_pairs={{0,96},{16,112},{32,0},{48,16},{64,32},{80,48},{96,64},{112,80},{1... | collective-permute-start | bytes 786440 | tf_op jit(solution)/shard_map/ppermute | solution.py:274
  14.8 13.3 %collective-permute-start.8 = (bf16[1,128,1024]{2,1,0:T(8,128)(2,1)S(1)}, bf16[1,128,1024]{2,1,0:T(8,128)(2,1)S(1)}, u32[]{:S(2)}, u32[]{:S(2)}) collective-permute-start(bf16[1,128,1024]{2,1,0:T(8,128)(2,1)S(1)} %collective-permute-done.rest_5_), channel_id=1, source_target_pairs={{0,32},{16,48},{32,64},{48,80},{64,96},{80,112},{96,0},{112,16},{1... | collective-permute-start | bytes 786440 | tf_op jit(solution)/shard_map/ppermute | solution.py:274
  14.8 57.2 %all-to-all-start = ((bf16[128,2,2176]{2,1,0:T(2,128)(2,1)}), bf16[128,2,2176]{2,1,0:T(2,128)(2,1)}, u32[]{:S(2)}, u32[]{:S(2)}) async-start(bf16[128,2,2176]{2,1,0:T(2,128)(2,1)} %reshape.21), calls=%async_computation | async-start | bytes 2228224 | tf_op jit(solution)/shard_map/all_to_all | solution.py:291
  26.3 2.8 %collective-permute-start.6 = (bf16[1,128,1024]{2,1,0:T(8,128)(2,1)S(1)}, bf16[1,128,1024]{2,1,0:T(8,128)(2,1)S(1)}, u32[]{:S(2)}, u32[]{:S(2)}) collective-permute-start(bf16[1,128,1024]{2,1,0:T(8,128)(2,1)S(1)} %collective-permute-done.rest_5_), channel_id=1, source_target_pairs={{0,16},{16,0},{32,48},{48,32},{64,80},{80,64},{96,112},{112,96},{1... | collective-permute-start | bytes 786440 | tf_op jit(solution)/shard_map/ppermute | solution.py:277
  27.6 1.5 %collective-permute-start.5 = (bf16[1,128,1024]{2,1,0:T(8,128)(2,1)S(1)}, bf16[1,128,1024]{2,1,0:T(8,128)(2,1)S(1)}, u32[]{:S(2)}, u32[]{:S(2)}) collective-permute-start(bf16[1,128,1024]{2,1,0:T(8,128)(2,1)S(1)} %collective-permute-done.4.rest_4_), channel_id=1, source_target_pairs={{0,16},{16,0},{32,48},{48,32},{64,80},{80,64},{96,112},{112,96},{1... | collective-permute-start | bytes 786440 | tf_op jit(solution)/shard_map/ppermute | solution.py:277
  27.7 1.8 %collective-permute-start.9 = (bf16[1,128,1024]{2,1,0:T(8,128)(2,1)S(1)}, bf16[1,128,1024]{2,1,0:T(8,128)(2,1)S(1)}, u32[]{:S(2)}, u32[]{:S(2)}) collective-permute-start(bf16[1,128,1024]{2,1,0:T(8,128)(2,1)S(1)} %collective-permute-done.7.rest_8_), channel_id=1, source_target_pairs={{0,16},{16,0},{32,48},{48,32},{64,80},{80,64},{96,112},{112,96},{1... | collective-permute-start | bytes 786440 | tf_op jit(solution)/shard_map/ppermute | solution.py:277
  28.1 1.8 %collective-permute-start.10 = (bf16[1,128,1024]{2,1,0:T(8,128)(2,1)S(1)}, bf16[1,128,1024]{2,1,0:T(8,128)(2,1)S(1)}, u32[]{:S(2)}, u32[]{:S(2)}) collective-permute-start(bf16[1,128,1024]{2,1,0:T(8,128)(2,1)S(1)} %collective-permute-done.8.rest_9_), channel_id=1, source_target_pairs={{0,16},{16,0},{32,48},{48,32},{64,80},{80,64},{96,112},{112,96},{1... | collective-permute-start | bytes 786440 | tf_op jit(solution)/shard_map/ppermute | solution.py:277
  29.8 0.7 copy-start.2

commit v4 on v3

v4 whole, which is shorter than its diff:
```python
import functools
import math

import jax
import jax.numpy as jnp
from jax import lax
from jax.experimental import pallas as pl
from jax.experimental.pallas import tpu as pltpu
from jax.sharding import PartitionSpec as P

HD = 128
KVH = 8
GROUP = 16
PAGE = 8
CAP = 2
REQS = 4
TOK = 128
PAGES_DEV = 16
OWNERS = 16
BLOCKS = 5
WINDOW = BLOCKS * TOK
ROW = 2 * PAGE * HD + HD
STACK = 8
STACK_TOP = 4
HEAD_WIDTH = GROUP * HD
SUM_LEAST = 2.0**-100
SUM_MOST = 2.0**100
PARTS = ((0, 8),)
EXP_SCALE = math.log2(math.e) / math.sqrt(HD)
INV_ROOT = 1.0 / math.sqrt(HD)
NT = (((1,), (1,)), ((), ()))
NN = (((1,), (0,)), ((), ()))
CHEAP = pl.CostEstimate(flops=1000, bytes_accessed=1000, transcendentals=0)
HBM = pl.BlockSpec(memory_space=pltpu.HBM)
SMEM = pl.BlockSpec(memory_space=pltpu.SMEM)
VMEM = pl.BlockSpec(memory_space=pltpu.VMEM)


def iota(shape, axis):
    return lax.broadcasted_iota(jnp.int32, shape, axis)


def pack_kernel(owners, keys, values, out, held, sem):
    row, col = iota((HD, HD), 0), iota((HD, HD), 1)
    common = row & col
    parity = jnp.zeros((HD, HD), jnp.int32)
    for bit in range(7):
        parity = parity + ((common >> bit) & 1)
    signs = (1 - 2 * (parity & 1)).astype(jnp.float32).astype(jnp.bfloat16)
    position = iota((1, TOK), 1)
    page, within = position // PAGE, position % PAGE
    slot = jnp.zeros((1, TOK), jnp.int32)
    for p in range(PAGES_DEV):
        rank = jnp.int32(0)
        for q in range(p):
            rank = rank + (owners[q] == owners[p]).astype(jnp.int32)
        slot = jnp.where(page == p, owners[p] * CAP + rank, slot)
    slots = OWNERS * CAP
    place = iota((PAGE * slots, TOK), 0)
    select = jnp.where((place % slots == slot) & (place // slots == within), 1.0, 0.0).astype(jnp.bfloat16)
    any_row = jnp.where(iota((slots, TOK), 0) == slot, 1.0, 0.0).astype(jnp.bfloat16)
    lane, in_page = iota((TOK, HD), 1), iota((TOK, HD), 0) % PAGE
    def put(h, at, tile):
        held[h * OWNERS : (h + 1) * OWNERS, :, at : at + HD] = tile.reshape(OWNERS, CAP, HD).astype(jnp.bfloat16)

    def head_copy(h):
        rows = pl.ds(h * OWNERS, OWNERS)
        return pltpu.make_async_copy(held.at[rows], out.at[rows], sem.at[h])

    for h in range(KVH):
        scales = jnp.zeros((TOK, HD), jnp.float32)
        codes = []
        for which, rows in enumerate((keys, values)):
            rotated = (
                lax.dot_general(rows[0, :, h * HD : (h + 1) * HD], signs, NN, preferred_element_type=jnp.float32)
                * INV_ROOT
            )
            scale = (jnp.max(jnp.abs(rotated), axis=-1, keepdims=True) + 1e-06).astype(jnp.bfloat16)
            scale = scale.astype(jnp.float32)
            codes.append((rotated * (1.0 / scale)).astype(jnp.bfloat16))
            scales = jnp.where(lane == which * PAGE + in_page, scale, scales)
        placed = lax.dot_general(select, jnp.concatenate(codes, 1), NN, preferred_element_type=jnp.float32)
        for which in range(2):
            for i in range(PAGE):
                put(h, (which * PAGE + i) * HD, placed[i * slots : (i + 1) * slots, which * HD : (which + 1) * HD])
        scales = lax.dot_general(any_row, scales.astype(jnp.bfloat16), NN, preferred_element_type=jnp.float32)
        put(h, 2 * PAGE * HD, scales)
        head_copy(h).start()
    for h in range(KVH):
        head_copy(h).wait()


def pack(owners, keys, values):
    shape = (KVH * OWNERS, CAP, ROW)
    return pl.pallas_call(
        pack_kernel,
        in_specs=[SMEM, VMEM, VMEM],
        out_specs=HBM,
        out_shape=jax.ShapeDtypeStruct(shape, jnp.bfloat16),
        scratch_shapes=[pltpu.VMEM(shape, jnp.bfloat16), pltpu.SemaphoreType.DMA((KVH,))],
        compiler_params=pltpu.CompilerParams(vmem_limit_bytes=60 * 2**20),
        cost_estimate=CHEAP,
        name="pack",
    )(owners, keys, values)


def unpack_kernel(received, cache_keys, cache_values, key_scales, value_scales, sem):
    half = PAGE * HD
    copies = [
        pltpu.make_async_copy(received.at[:, :, pl.ds(0, half)], cache_keys.at[:, 0], sem.at[0]),
        pltpu.make_async_copy(received.at[:, :, pl.ds(half, half)], cache_values.at[:, 0], sem.at[1]),
    ]
    for copy in copies:
        copy.start()
    for slot in range(CAP):
        turned = received[:, slot, 2 * half :].T
        key_scales[slot] = turned[:PAGE]
        value_scales[slot] = turned[PAGE : 2 * PAGE]
    for copy in copies:
        copy.wait()


def unpack(received):
    sources = received.shape[0]
    cache = jax.ShapeDtypeStruct((sources, 1, CAP, PAGE * HD), jnp.bfloat16)
    scales = jax.ShapeDtypeStruct((CAP, PAGE, sources), jnp.bfloat16)
    cache_keys, cache_values, key_scales, value_scales = pl.pallas_call(
        unpack_kernel,
        in_specs=[VMEM],
        out_specs=[HBM, HBM, VMEM, VMEM],
        out_shape=[cache, cache, scales, scales],
        scratch_shapes=[pltpu.SemaphoreType.DMA((2,))],
        compiler_params=pltpu.CompilerParams(vmem_limit_bytes=8 * 2**20),
        cost_estimate=CHEAP,
        name="unpack",
    )(received)
    return (
        cache_keys,
        cache_values,
        key_scales.transpose(2, 0, 1)[:, None],
        value_scales.transpose(2, 0, 1)[:, None],
    )


def mask_kernel(lengths, bias):
    ctx = lax.axis_index("ctx")
    core = lax.rem(ctx, 2)
    query_pos = ctx * TOK + iota((TOK, TOK), 1)
    start = jnp.zeros((TOK, TOK), jnp.int32)
    end = jnp.int32(0)
    for r in range(REQS):
        end = end + lengths[0, r]
        start = jnp.where(query_pos >= end, end, start)
    back = (4, jnp.where(core == 0, 3, 1), 2, jnp.where(core == 0, 1, 3), 0)
    for b in range(BLOCKS):
        key_pos = (ctx - back[b]) * TOK + iota((TOK, TOK), 0)
        kept = (key_pos >= start) & (key_pos <= query_pos)
        bias[b * TOK : (b + 1) * TOK, :] = jnp.where(kept, 0.0, -1e30)


def mask(lengths):
    return pl.pallas_call(
        mask_kernel,
        in_specs=[SMEM],
        out_specs=VMEM,
        out_shape=jax.ShapeDtypeStruct((WINDOW, TOK), jnp.float32),
        cost_estimate=pl.CostEstimate(flops=2000000000, bytes_accessed=1000, transcendentals=0),
        compiler_params=pltpu.CompilerParams(vmem_limit_bytes=8 * 2**20),
        name="mask",
    )(lengths)


def attend_kernel(first, heads, bias, queries, *rest):
    out, o_buf, sums, o_sem = rest[-4:]
    def out_copy(h, g0):
        width = STACK * HD
        at = pl.ds(pl.multiple_of(h * HEAD_WIDTH + g0 * HD, width), width)
        to_at = pl.ds(pl.multiple_of((first + h) * HEAD_WIDTH + g0 * HD, width), width)
        return pltpu.make_async_copy(o_buf.at[:, at], out.at[0, :, to_at], o_sem.at[h])

    even = jnp.full((TOK, HD), lax.rem(lax.axis_index("ctx"), 2), jnp.int32) == 0
    sums[0] = jnp.ones((8, STACK * TOK), jnp.float32)
    sums[1] = jnp.ones((8, STACK * TOK), jnp.float32)
    ones = jnp.ones((16, WINDOW), jnp.bfloat16)
    def window(arrays, lanes):
        own, beside, near, near_beside, far, far_beside = (array[0, :, lanes] for array in arrays)
        third = jnp.where(even, far_beside, beside)
        return jnp.concatenate([far, third, near, near_beside, own], 0)

    def one_head(h, stack, with_top):
        lanes = pl.ds(pl.multiple_of((first + h) * HD, HD), HD)
        key_rows, value_rows = window(rest[0:12:2], lanes), window(rest[1:12:2], lanes)
        value_side = jnp.concatenate([value_rows.T, ones], 0)
        mask = jnp.concatenate([bias[...]] * stack, 1)

        def head_lanes(h, g):
            return pl.ds(pl.multiple_of(h * HEAD_WIDTH + g * HD, HD), HD)

        def score(g0):
            rows = jnp.concatenate([queries[0, :, head_lanes(first + h, g0 + g)] for g in range(stack)], 0)
            return lax.dot_general(key_rows, rows, NT, preferred_element_type=jnp.float32)

        def finish(g0, scores):
            if with_top:
                masked = scores + mask
                exponent = (masked - jnp.max(masked, axis=0, keepdims=True)) * EXP_SCALE
            else:
                exponent = scores * EXP_SCALE + mask
            weights = jnp.exp2(exponent).astype(jnp.bfloat16)
            mixed = lax.dot_general(value_side, weights, NN, preferred_element_type=jnp.float32)
            if not with_top:
                total = mixed[HD : HD + 8]
                sums[0] = jnp.minimum(sums[0], total)
                sums[1] = jnp.maximum(sums[1], total)
            result = (mixed[:HD] * (1.0 / mixed[HD : HD + 1])).astype(jnp.bfloat16)
            for g in range(stack):
                o_buf[:, head_lanes(h, g0 + g)] = result[:, g * TOK : (g + 1) * TOK].T
            if (g0 + stack) % STACK == 0:
                out_copy(h, g0 + stack - STACK).start()

        scores = score(0)
        for g0 in range(0, GROUP, stack):
            following = score(g0 + stack) if g0 + stack < GROUP else None
            finish(g0, scores)
            scores = following

    def first_pass(h, carry):
        one_head(h, STACK, False)
        return carry

    def wait_out(h, carry):
        for g0 in range(0, GROUP, STACK):
            out_copy(h, g0).wait()
        return carry

    lax.fori_loop(0, heads, first_pass, 0)
    lax.fori_loop(0, heads, wait_out, 0)

    in_range = (jnp.min(sums[0]) > SUM_LEAST) & (jnp.max(sums[1]) < SUM_MOST)

    @pl.when(jnp.logical_not(in_range))
    def _():
        def second_pass(h, carry):
            one_head(h, STACK_TOP, True)
            return wait_out(h, carry)

        lax.fori_loop(0, heads, second_pass, 0)


def attend(first, heads, bias, queries, *operands, partial=None):
    more = () if partial is None else (partial,)
    return pl.pallas_call(
        functools.partial(attend_kernel, first, heads),
        in_specs=[VMEM, VMEM] + [VMEM] * len(operands) + [HBM] * len(more),
        out_specs=HBM,
        out_shape=jax.ShapeDtypeStruct(queries.shape, jnp.bfloat16),
        scratch_shapes=[
            pltpu.VMEM((TOK, heads * HEAD_WIDTH), jnp.bfloat16),
            pltpu.VMEM((2, 8, STACK * TOK), jnp.float32),
            pltpu.SemaphoreType.DMA((heads,)),
        ],
        input_output_aliases={2 + len(operands): 0} if more else {},
        compiler_params=pltpu.CompilerParams(vmem_limit_bytes=28 * 2**20),
        cost_estimate=pl.CostEstimate(flops=6000000000, bytes_accessed=1000, transcendentals=0),
        name=f"attend{first}",
    )(bias, queries, *operands, *more)


def body(queries, keys, values, lengths, owners):
    ctx_count = lax.axis_size("ctx")

    def chips_on(block, chips):
        step = 2 * chips
        return lax.ppermute(block, "ctx", [(i, (i + step) % ctx_count) for i in range(ctx_count)])

    def swap(block):
        return lax.ppermute(block, "ctx", [(i, i ^ 1) for i in range(ctx_count)])

    near_values = chips_on(values, 1)
    ahead_keys = chips_on(keys, -1)
    near_keys = chips_on(keys, 1)

    message = pack(owners.reshape(PAGES_DEV), keys, values)
    near_values, ahead_keys, message = lax.optimization_barrier((near_values, ahead_keys, message))
    lengths, message = lax.optimization_barrier((lengths, message))
    bias = mask(lengths)
    far_values = chips_on(near_values, 1)
    far_keys = chips_on(ahead_keys, -1)
    received = lax.all_to_all(message, ("ctx", "dec"), split_axis=0, concat_axis=0, tiled=True)

    near_keys, near_values, far_keys, far_values, own = lax.optimization_barrier(
        (near_keys, near_values, far_keys, far_values, (keys, values))
    )
    beside = (swap(own[0]), swap(own[1]))
    near = (near_keys, near_values)
    far = (far_keys, far_values)
    near_beside = (swap(near_keys), swap(near_values))
    far_beside = (swap(far_keys), swap(far_values))
    attended = None
    for first, heads in PARTS:
        attended = attend(
            first, heads, bias, queries, keys, values, *beside, *near, *near_beside, *far, *far_beside, partial=attended
        )
    attended, received = lax.optimization_barrier((attended, received))
    return (attended,) + unpack(received)


def solution(mesh):
    placed = (
        P("dec", "ctx", None),
        P("dec", "ctx", None),
        P("dec", "ctx", None),
        P("dec", None),
        P("dec", "ctx", None),
    )
    return jax.shard_map(
        body,
        mesh=mesh,
        in_specs=placed,
        out_specs=(
            P("dec", "ctx", None),
            P(None, "ctx", "dec", None),
            P(None, "ctx", "dec", None),
            P(None, "ctx", "dec", None),
            P(None, "ctx", "dec", None),
        ),
        check_vma=False,
    )
```

time: 74.9 us -> 70.3 us (0.939)
  Pallas kernels: 48.6 us -> 45.8 us
  local copies, waits for them, and re-layouts: 3.01 us -> 0.67 us
    reshape x1 -> x0, local copies, waits for them, and re-layouts: 2.29 us -> none  [body(): message = message.reshape(KVH * OWNERS, CAP, ROW)]
    pallas_call x1, Pallas kernels: 41.4 us -> 39.4 us  [attend(): pl.pallas_call(functools.partial(attend_kernel, first, heads), in_specs=[...]
    ppermute x5, waiting for transfers between devices: 0.01 us -> 1.81 us  [chips_on(): lax.ppermute(block, 'ctx', [(i, (i + step) % ctx_count) for i in range(ct...]
    ppermute x6, waiting for transfers between devices: 1.59 us -> 0.36 us  [swap(): return lax.ppermute(block, 'ctx', [(i, i ^ 1) for i in range(ctx_count)])]
    ppermute x6, starting transfers between devices: 3.67 us -> 2.54 us  [swap(): return lax.ppermute(block, 'ctx', [(i, i ^ 1) for i in range(ctx_count)])]
    pallas_call x2 -> x3, Pallas kernels: 7.2 us -> 6.39 us  [the longest x1 4.2 us: pack(): pl.pallas_call(pack_kernel, in_specs=[SMEM, VMEM, VMEM], out_specs=HBM, o...]
    ppermute x5, starting transfers between devices: 5.44 us -> 6.24 us  [chips_on(): lax.ppermute(block, 'ctx', [(i, (i + step) % ctx_count) for i in range(ct...]
  transfers between devices with their start and end apart: 12 -> 12, of which waited for: 3 -> 2; matrix products, arithmetic and copies ran while one was open for 3% -> 0% of each run, Pallas kernels for 61% -> 63%
where the time goes in v4:
time: 70.3 us; the launch traced here: 70.1 us
  Pallas kernels  45.8 us (65%)
  starting transfers between devices  20.7 us (29%)
  waiting for transfers between devices  2.17 us (3%)
  between operations  0.79 us (1%)
    pallas_call x1, Pallas kernels, attend(): pl.pallas_call(functools.partial(attend_kernel, first, heads), in_specs=[...  39.4 us
    all_to_all x1, starting transfers between devices, body(): lax.all_to_all(message, ('ctx', 'dec'), split_axis=0, concat_axis=0, tile...  11.9 us
    ppermute x5, starting transfers between devices, chips_on(): lax.ppermute(block, 'ctx', [(i, (i + step) % ctx_count) for i in range(ct...  6.24 us
    pallas_call x1, Pallas kernels, pack(): pl.pallas_call(pack_kernel, in_specs=[SMEM, VMEM, VMEM], out_specs=HBM, o...  4.2 us
    ppermute x6, starting transfers between devices, swap(): return lax.ppermute(block, 'ctx', [(i, i ^ 1) for i in range(ctx_count)])  2.54 us
    ppermute x5, waiting for transfers between devices, chips_on(): lax.ppermute(block, 'ctx', [(i, (i + step) % ctx_count) for i in range(ct...  1.81 us
    pallas_call x1, Pallas kernels, unpack(): pl.pallas_call(unpack_kernel, in_specs=[VMEM], out_specs=[HBM, HBM, VMEM,...  1.58 us
  transfers between devices with their start and end apart: 12, of which 2 were waited for; matrix products, arithmetic and copies ran while one was open for 0% of the time, Pallas kernels for 63%

profile of v4, /device:TPU:1, one launch (start us, length us, event | category | flops | bytes accessed | tf_op | source)
XLA Modules:
  0.0 70.1 jit_solution(6345724056177006150)
XLA Ops:
  0.6 2.2 %collective-permute-start = (bf16[1,128,1024]{2,1,0:T(8,128)(2,1)}, bf16[1,128,1024]{2,1,0:T(8,128)(2,1)S(1)}, u32[]{:S(2)}, u32[]{:S(2)}) collective-permute-start(bf16[1,128,1024]{2,1,0:T(8,128)(2,1)} %rest_1_.1), channel_id=1, source_target_pairs={{0,32},{16,48},{32,64},{48,80},{64,96},{80,112},{96,0},{112,16},{1... | collective-permute-start | bytes 786440 | tf_op jit(solution)/shard_map/ppermute | solution.py:274
  2.8 1.5 %collective-permute-start.1 = (bf16[1,128,1024]{2,1,0:T(8,128)(2,1)}, bf16[1,128,1024]{2,1,0:T(8,128)(2,1)S(1)}, u32[]{:S(2)}, u32[]{:S(2)}) collective-permute-start(bf16[1,128,1024]{2,1,0:T(8,128)(2,1)} %rest_0_.1), channel_id=1, source_target_pairs={{0,96},{16,112},{32,0},{48,16},{64,32},{80,48},{96,64},{112,80},{1... | collective-permute-start | bytes 786440 | tf_op jit(solution)/shard_map/ppermute | solution.py:274
  4.3 0.0 collective-permute-start.2
  4.4 4.2 %pack.1 = bf16[128,2,2176]{2,1,0:T(2,128)(2,1)} custom-call(s32[16]{0:T(128)} %bitcast.7, bf16[1,128,1024]{2,1,0:T(8,128)(2,1)} %rest_0_.1, bf16[1,128,1024]{2,1,0:T(8,128)(2,1)} %rest_1_.1), custom_call_target="tpu_custom_call" | custom-call | flops 1000 | bytes 1000 | tf_op jit(solution)/shard_map/pack/pallas_call | solution.py:95
  8.6 1.8 %collective-permute-done.rest_5_ = bf16[1,128,1024]{2,1,0:T(8,128)(2,1)S(1)} collective-permute-done((bf16[1,128,1024]{2,1,0:T(8,128)(2,1)}, bf16[1,128,1024]{2,1,0:T(8,128)(2,1)S(1)}, u32[]{:S(2)}, u32[]{:S(2)}) %collective-permute-start) | collective-permute-done | bytes 262176 | tf_op jit(solution)/shard_map/ppermute | solution.py:274
  10.4 0.0 collective-permute-done.1
  10.4 2.5 %collective-permute-start.3 = (bf16[1,128,1024]{2,1,0:T(8,128)(2,1)S(1)}, bf16[1,128,1024]{2,1,0:T(8,128)(2,1)S(1)}, u32[]{:S(2)}, u32[]{:S(2)}) collective-permute-start(bf16[1,128,1024]{2,1,0:T(8,128)(2,1)S(1)} %collective-permute-done.1), channel_id=1, source_target_pairs={{0,96},{16,112},{32,0},{48,16},{64,32},{80,48},{96,64},{112,80},{1... | collective-permute-start | bytes 786440 | tf_op jit(solution)/shard_map/ppermute | solution.py:274
  12.9 0.0 collective-permute-start.4
  12.9 11.9 %all-to-all-start = ((bf16[128,2,2176]{2,1,0:T(2,128)(2,1)}), bf16[128,2,2176]{2,1,0:T(2,128)(2,1)S(1)}, u32[]{:S(2)}, u32[]{:S(2)}) async-start(bf16[128,2,2176]{2,1,0:T(2,128)(2,1)} %pack.1), calls=%async_computation | async-start | bytes 2228224 | tf_op jit(solution)/shard_map/all_to_all | solution.py:289
  24.8 0.0 copy-start
  24.8 0.0 copy-start.1
  24.8 0.0 copy-start.2
  24.8 0.0 collective-permute-done.2.rest_4_
  24.9 0.0 collective-permute-done.3.rest_8_
  24.9 0.0 collective-permute-done.4.rest_9_
  24.9 1.1 %collective-permute-start.5 = (bf16[1,128,1024]{2,1,0:T(8,128)(2,1)}, bf16[1,128,1024]{2,1,0:T(8,128)(2,1)S(1)}, u32[]{:S(2)}, u32[]{:S(2)}) collective-permute-start(bf16[1,128,1024]{2,1,0:T(8,128)(2,1)} %rest_0_.1), channel_id=1, source_target_pairs={{0,16},{16,0},{32,48},{48,32},{64,80},{80,64},{96,112},{112,96},{1... | collective-permute-start | bytes 786440 | tf_op jit(solution)/shard_map/ppermute | solution.py:277
  26.0 0.1 collective-permute-start.6
  26.1 0.4 collective-permute-start.7
  26.5 0.1 collective-permute-start.8
  26.6 0.4 collective-permute-start.9
  27.0 0.4 collective-permute-done.5.rest_2_
  27.4 0.4 collective-permute-start.10
  27.8 0.0 copy-start.3
  27.8 0.7 copy-done.3
  28.4 0.6 mask.1.bias
  29.0 0.0 collective-permute-done.6.rest_3_
  29.1 0.0 collective-permute-done.7.rest_6_
  29.1 0.0 collective-permute-done.8.rest_7_
  29.1 0.0 collective-permute-done.9.rest_10_
  29.1 0.0 collective-permute-done.10.rest_11_
  29.1 0.0 copy-done
  29.1 0.0 copy-done.1
  29.1 0.0 copy-done.2
  29.1 39.4 %attend0.1 = bf16[1,128,16384]{2,1,0:T(8,128)(2,1)} custom-call(f32[640,128]{1,0:T(8,128)S(1)} %mask.1.bias, bf16[1,128,16384]{2,1,0:T(8,128)(2,1)S(1)} %copy-done.2, bf16[1,128,1024]{2,1,0:T(8,128)(2,1)S(1)} %copy-done, bf16[1,128,1024]{2,1,0:T(8,128)(2,1)S(1)} %copy-done.1, bf16[1,128,1024]{2,1,0:T(8,128)(2,1)S(1)} %collective-permute-done.5.rest_2_, ...), custom_call_target="tpu_custom_call" | custom-call | flops 6000000000 | bytes 1000 | tf_op jit(solution)/shard_map/attend0/pallas_call | solution.py:252
  68.5 0.0 all-to-all-done.received
  68.5 1.6 %unpack.1 = (bf16[128,1,2,1024]{3,2,1,0:T(2,128)(2,1)}, bf16[128,1,2,1024]{3,2,1,0:T(2,128)(2,1)}, bf16[2,8,128]{2,1,0:T(8,128)(2,1)}, bf16[2,8,128]{2,1,0:T(8,128)(2,1)}) custom-call(bf16[128,2,2176]{2,1,0:T(2,128)(2,1)S(1)} %all-to-all-done.received), custom_call_target="tpu_custom_call" | custom-call | flops 1000 | bytes 1000 | tf_op jit(solution)/shard_map/unpack/pallas_call | solution.py:127
Async XLA Ops:
  0.6 9.7 %collective-permute-start = (bf16[1,128,1024]{2,1,0:T(8,128)(2,1)}, bf16[1,128,1024]{2,1,0:T(8,128)(2,1)S(1)}, u32[]{:S(2)}, u32[]{:S(2)}) collective-permute-start(bf16[1,128,1024]{2,1,0:T(8,128)(2,1)} %rest_1_.1), channel_id=1, source_target_pairs={{0,32},{16,48},{32,64},{48,80},{64,96},{80,112},{96,0},{112,16},{1... | collective-permute-start | bytes 786440 | tf_op jit(solution)/shard_map/ppermute | solution.py:274
  2.8 7.5 %collective-permute-start.1 = (bf16[1,128,1024]{2,1,0:T(8,128)(2,1)}, bf16[1,128,1024]{2,1,0:T(8,128)(2,1)S(1)}, u32[]{:S(2)}, u32[]{:S(2)}) collective-permute-start(bf16[1,128,1024]{2,1,0:T(8,128)(2,1)} %rest_0_.1), channel_id=1, source_target_pairs={{0,96},{16,112},{32,0},{48,16},{64,32},{80,48},{96,64},{112,80},{1... | collective-permute-start | bytes 786440 | tf_op jit(solution)/shard_map/ppermute | solution.py:274
  4.3 20.5 %collective-permute-start.2 = (bf16[1,128,1024]{2,1,0:T(8,128)(2,1)}, bf16[1,128,1024]{2,1,0:T(8,128)(2,1)S(1)}, u32[]{:S(2)}, u32[]{:S(2)}) collective-permute-start(bf16[1,128,1024]{2,1,0:T(8,128)(2,1)} %rest_0_.1), channel_id=1, source_target_pairs={{0,32},{16,48},{32,64},{48,80},{64,96},{80,112},{96,0},{112,16},{1... | collective-permute-start | bytes 786440 | tf_op jit(solution)/shard_map/ppermute | solution.py:274
  10.4 14.5 %collective-permute-start.3 = (bf16[1,128,1024]{2,1,0:T(8,128)(2,1)S(1)}, bf16[1,128,1024]{2,1,0:T(8,128)(2,1)S(1)}, u32[]{:S(2)}, u32[]{:S(2)}) collective-permute-start(bf16[1,128,1024]{2,1,0:T(8,128)(2,1)S(1)} %collective-permute-done.1), channel_id=1, source_target_pairs={{0,96},{16,112},{32,0},{48,16},{64,32},{80,48},{96,64},{112,80},{1... | collective-permute-start | bytes 786440 | tf_op jit(solution)/shard_map/ppermute | solution.py:274
  12.9 12.0 %collective-permute-start.4 = (bf16[1,128,1024]{2,1,0:T(8,128)(2,1)S(1)}, bf16[1,128,1024]{2,1,0:T(8,128)(2,1)S(1)}, u32[]{:S(2)}, u32[]{:S(2)}) collective-permute-start(bf16[1,128,1024]{2,1,0:T(8,128)(2,1)S(1)} %collective-permute-done.rest_5_), channel_id=1, source_target_pairs={{0,32},{16,48},{32,64},{48,80},{64,96},{80,112},{96,0},{112,16},{1... | collective-permute-start | bytes 786440 | tf_op jit(solution)/shard_map/ppermute | solution.py:274
  12.9 55.6 %all-to-all-start = ((bf16[128,2,2176]{2,1,0:T(2,128)(2,1)}), bf16[128,2,2176]{2,1,0:T(2,128)(2,1)S(1)}, u32[]{:S(2)}, u32[]{:S(2)}) async-start(bf16[128,2,2176]{2,1,0:T(2,128)(2,1)} %pack.1), calls=%async_computation | async-start | bytes 2228224 | tf_op jit(solution)/shard_map/all_to_all | solution.py:289
  24.8 4.3 %copy-start = (bf16[1,128,1024]{2,1,0:T(8,128)(2,1)S(1)}, bf16[1,128,1024]{2,1,0:T(8,128)(2,1)}, u32[]{:S(2)}) copy-start(bf16[1,128,1024]{2,1,0:T(8,128)(2,1)} %rest_0_.1) | copy-start | bytes 786436
  24.8 4.3 %copy-start.1 = (bf16[1,128,1024]{2,1,0:T(8,128)(2,1)S(1)}, bf16[1,128,1024]{2,1,0:T(8,128)(2,1)}, u32[]{:S(2)}) copy-start(bf16[1,128,1024]{2,1,0:T(8,128)(2,1)} %rest_1_.1) | copy-start | bytes 786436
  24.8 4.3 %copy-start.2 = (bf16[1,128,16384]{2,1,0:T(8,128)(2,1)S(1)}, bf16[1,128,16384]{2,1,0:T(8,128)(2,1)}, u32[]{:S(2)}) copy-start(bf16[1,128,16384]{2,1,0:T(8,128)(2,1)} %queries.1) | copy-start | bytes 12582916
  24.9 2.5 %collective-permute-start.5 = (bf16[1,128,1024]{2,1,0:T(8,128)(2,1)}, bf16[1,128,1024]{2,1,0:T(8,128)(2,1)S(1)}, u32[]{:S(2)}, u32[]{:S(2)}) collective-permute-start(bf16[1,128,1024]{2,1,0:T(8,128)(2,1)} %rest_0_.1), channel_id=1, source_target_pairs={{0,16},{16,0},{32,48},{48,32},{64,80},{80,64},{96,112},{112,96},{1... | collective-permute-start | bytes 786440 | tf_op jit(solution)/shard_map/ppermute | solution.py:277
  26.0 3.0 %collective-permute-start.6 = (bf16[1,128,1024]{2,1,0:T(8,128)(2,1)}, bf16[1,128,1024]{2,1,0:T(8,128)(2,1)S(1)}, u32[]{:S(2)}, u32[]{:S(2)}) collective-permute-start(bf16[1,128,1024]{2,1,0:T(8,128)(2,1)} %rest_1_.1), channel_id=1, source_target_pairs={{0,16},{16,0},{32,48},{48,32},{64,80},{80,64},{96,112},{112,96},{1... | collective-permute-start | bytes 786440 | tf_op jit(solution)/shard_map/ppermute | solution.py:277
  26.1 2.9 %collective-permute-start.7 = (bf16[1,128,1024]{2,1,0:T(8,128)(2,1)S(1)}, bf16[1,128,1024]{2,1,0:T(8,128)(2,1)S(1)}, u32[]{:S(2)}, u32[]{:S(2)}) collective-permute-start(bf16[1,128,1024]{2,1,0:T(8,128)(2,1)S(1)} %collective-permute-done.2.rest_4_), channel_id=1, source_target_pairs={{0,16},{16,0},{32,48},{48,32},{64,80},{80,64},{96,112},{112,96},{1... | collective-permute-start | bytes 786440 | tf_op jit(solution)/shard_map/ppermute | solution.py:277
  26.5 2.5 %collective-permute-start.8 = (bf16[1,128,1024]{2,1,0:T(8,128)(2,1)S(1)}, bf16[1,128,1024]{2,1,0:T(8,128)(2,1)S(1)}, u32[]{:S(2)}, u32[]{:S(2)}) collective-permute-start(bf16[1,128,1024]{2,1,0:T(8,128)(2,1)S(1)} %collective-permute-done.rest_5_), channel_id=1, source_target_pairs={{0,16},{16,0},{32,48},{48,32},{64,80},{80,64},{96,112},{112,96},{1... | collective-permute-start | bytes 786440 | tf_op jit(solution)/shard_map/ppermute | solution.py:277
  26.6 2.4 %collective-permute-start.9 = (bf16[1,128,1024]{2,1,0:T(8,128)(2,1)S(1)}, bf16[1,128,1024]{2,1,0:T(8,128)(2,1)S(1)}, u32[]{:S(2)}, u32[]{:S(2)}) collective-permute-start(bf16[1,128,1024]{2,1,0:T(8,128)(2,1)S(1)} %collective-permute-done.3.rest_8_), channel_id=1, source_target_pairs={{0,16},{16,0},{32,48},{48,32},{64,80},{80,64},{96,112},{112,96},{1... | collective-permute-start | bytes 786440 | tf_op jit(solution)/shard_map/ppermute | solution.py:277
  27.4 1.7 %collective-permute-start.10 = (bf16[1,128,1024]{2,1,0:T(8,128)(2,1)S(1)}, bf16[1,128,1024]{2,1,0:T(8,128)(2,1)S(1)}, u32[]{:S(2)}, u32[]{:S(2)}) collective-permute-start(bf16[1,128,1024]{2,1,0:T(8,128)(2,1)S(1)} %collective-permute-done.4.rest_9_), channel_id=1, source_target_pairs={{0,16},{16,0},{32,48},{48,32},{64,80},{80,64},{96,112},{112,96},{1... | collective-permute-start | bytes 786440 | tf_op jit(solution)/shard_map/ppermute | solution.py:277
  27.8 0.7 copy-start.3

commit v5 on v4

--- a/solution.py
+++ b/solution.py
@@ -104,18 +104,22 @@
     )(owners, keys, values)
 
 
-def unpack_kernel(received, cache_keys, cache_values, key_scales, value_scales, sem):
+def unpack_kernel(received, cache_keys, cache_values, key_scales, value_scales, held, sem):
     half = PAGE * HD
     copies = [
         pltpu.make_async_copy(received.at[:, :, pl.ds(0, half)], cache_keys.at[:, 0], sem.at[0]),
         pltpu.make_async_copy(received.at[:, :, pl.ds(half, half)], cache_values.at[:, 0], sem.at[1]),
+        pltpu.make_async_copy(held.at[0], key_scales, sem.at[2]),
+        pltpu.make_async_copy(held.at[1], value_scales, sem.at[3]),
     ]
-    for copy in copies:
-        copy.start()
+    copies[0].start()
+    copies[1].start()
     for slot in range(CAP):
         turned = received[:, slot, 2 * half :].T
-        key_scales[slot] = turned[:PAGE]
-        value_scales[slot] = turned[PAGE : 2 * PAGE]
+        held[0, slot] = turned[:PAGE]
+        held[1, slot] = turned[PAGE : 2 * PAGE]
+    copies[2].start()
+    copies[3].start()
     for copy in copies:
         copy.wait()
 
@@ -127,9 +131,9 @@
     cache_keys, cache_values, key_scales, value_scales = pl.pallas_call(
         unpack_kernel,
         in_specs=[VMEM],
-        out_specs=[HBM, HBM, VMEM, VMEM],
+        out_specs=[HBM] * 4,
         out_shape=[cache, cache, scales, scales],
-        scratch_shapes=[pltpu.SemaphoreType.DMA((2,))],
+        scratch_shapes=[pltpu.VMEM((2, CAP, PAGE, sources), jnp.bfloat16), pltpu.SemaphoreType.DMA((4,))],
         compiler_params=pltpu.CompilerParams(vmem_limit_bytes=8 * 2**20),
         cost_estimate=CHEAP,
         name="unpack",

time: 70.3 us -> 69.7 us (level)
  transfers between devices with their start and end apart: 12 -> 12, of which waited for: 2 -> 2; matrix products, arithmetic and copies ran while one was open for 0% -> 0% of each run, Pallas kernels for 63% -> 64%
where the time goes in v5:
time: 69.7 us; the launch traced here: 69.5 us
  Pallas kernels  45.2 us (65%)
  starting transfers between devices  20.7 us (30%)
  waiting for transfers between devices  2.17 us (3%)
  between operations  0.79 us (1%)
    pallas_call x1, Pallas kernels, attend(): pl.pallas_call(functools.partial(attend_kernel, first, heads), in_specs=[...  39.4 us
    all_to_all x1, starting transfers between devices, body(): lax.all_to_all(message, ('ctx', 'dec'), split_axis=0, concat_axis=0, tile...  11.9 us
    ppermute x5, starting transfers between devices, chips_on(): lax.ppermute(block, 'ctx', [(i, (i + step) % ctx_count) for i in range(ct...  6.24 us
    pallas_call x1, Pallas kernels, pack(): pl.pallas_call(pack_kernel, in_specs=[SMEM, VMEM, VMEM], out_specs=HBM, o...  4.2 us
    ppermute x6, starting transfers between devices, swap(): return lax.ppermute(block, 'ctx', [(i, i ^ 1) for i in range(ctx_count)])  2.54 us
    ppermute x5, waiting for transfers between devices, chips_on(): lax.ppermute(block, 'ctx', [(i, (i + step) % ctx_count) for i in range(ct...  1.81 us
  transfers between devices with their start and end apart: 12, of which 2 were waited for; matrix products, arithmetic and copies ran while one was open for 0% of the time, Pallas kernels for 64%

profile of v5, /device:TPU:1, one launch (start us, length us, event | category | flops | bytes accessed | tf_op | source)
XLA Modules:
  0.0 69.5 jit_solution(2768996438025188847)
XLA Ops:
  0.6 2.2 %collective-permute-start = (bf16[1,128,1024]{2,1,0:T(8,128)(2,1)}, bf16[1,128,1024]{2,1,0:T(8,128)(2,1)S(1)}, u32[]{:S(2)}, u32[]{:S(2)}) collective-permute-start(bf16[1,128,1024]{2,1,0:T(8,128)(2,1)} %rest_1_.1), channel_id=1, source_target_pairs={{0,32},{16,48},{32,64},{48,80},{64,96},{80,112},{96,0},{112,16},{1... | collective-permute-start | bytes 786440 | tf_op jit(solution)/shard_map/ppermute | solution.py:278
  2.8 1.5 %collective-permute-start.1 = (bf16[1,128,1024]{2,1,0:T(8,128)(2,1)}, bf16[1,128,1024]{2,1,0:T(8,128)(2,1)S(1)}, u32[]{:S(2)}, u32[]{:S(2)}) collective-permute-start(bf16[1,128,1024]{2,1,0:T(8,128)(2,1)} %rest_0_.1), channel_id=1, source_target_pairs={{0,96},{16,112},{32,0},{48,16},{64,32},{80,48},{96,64},{112,80},{1... | collective-permute-start | bytes 786440 | tf_op jit(solution)/shard_map/ppermute | solution.py:278
  4.3 0.0 collective-permute-start.2
  4.4 4.2 %pack.1 = bf16[128,2,2176]{2,1,0:T(2,128)(2,1)} custom-call(s32[16]{0:T(128)} %bitcast.7, bf16[1,128,1024]{2,1,0:T(8,128)(2,1)} %rest_0_.1, bf16[1,128,1024]{2,1,0:T(8,128)(2,1)} %rest_1_.1), custom_call_target="tpu_custom_call" | custom-call | flops 1000 | bytes 1000 | tf_op jit(solution)/shard_map/pack/pallas_call | solution.py:95
  8.6 1.8 %collective-permute-done.rest_5_ = bf16[1,128,1024]{2,1,0:T(8,128)(2,1)S(1)} collective-permute-done((bf16[1,128,1024]{2,1,0:T(8,128)(2,1)}, bf16[1,128,1024]{2,1,0:T(8,128)(2,1)S(1)}, u32[]{:S(2)}, u32[]{:S(2)}) %collective-permute-start) | collective-permute-done | bytes 262176 | tf_op jit(solution)/shard_map/ppermute | solution.py:278
  10.4 0.0 collective-permute-done.1
  10.4 2.5 %collective-permute-start.3 = (bf16[1,128,1024]{2,1,0:T(8,128)(2,1)S(1)}, bf16[1,128,1024]{2,1,0:T(8,128)(2,1)S(1)}, u32[]{:S(2)}, u32[]{:S(2)}) collective-permute-start(bf16[1,128,1024]{2,1,0:T(8,128)(2,1)S(1)} %collective-permute-done.1), channel_id=1, source_target_pairs={{0,96},{16,112},{32,0},{48,16},{64,32},{80,48},{96,64},{112,80},{1... | collective-permute-start | bytes 786440 | tf_op jit(solution)/shard_map/ppermute | solution.py:278
  12.9 0.0 collective-permute-start.4
  12.9 11.9 %all-to-all-start = ((bf16[128,2,2176]{2,1,0:T(2,128)(2,1)}), bf16[128,2,2176]{2,1,0:T(2,128)(2,1)S(1)}, u32[]{:S(2)}, u32[]{:S(2)}) async-start(bf16[128,2,2176]{2,1,0:T(2,128)(2,1)} %pack.1), calls=%async_computation | async-start | bytes 2228224 | tf_op jit(solution)/shard_map/all_to_all | solution.py:293
  24.8 0.0 copy-start
  24.8 0.0 copy-start.1
  24.8 0.0 copy-start.2
  24.8 0.0 collective-permute-done.2.rest_4_
  24.9 0.0 collective-permute-done.3.rest_8_
  24.9 0.0 collective-permute-done.4.rest_9_
  24.9 1.1 %collective-permute-start.5 = (bf16[1,128,1024]{2,1,0:T(8,128)(2,1)}, bf16[1,128,1024]{2,1,0:T(8,128)(2,1)S(1)}, u32[]{:S(2)}, u32[]{:S(2)}) collective-permute-start(bf16[1,128,1024]{2,1,0:T(8,128)(2,1)} %rest_0_.1), channel_id=1, source_target_pairs={{0,16},{16,0},{32,48},{48,32},{64,80},{80,64},{96,112},{112,96},{1... | collective-permute-start | bytes 786440 | tf_op jit(solution)/shard_map/ppermute | solution.py:281
  26.0 0.1 collective-permute-start.6
  26.1 0.4 collective-permute-start.7
  26.5 0.1 collective-permute-start.8
  26.6 0.4 collective-permute-start.9
  27.0 0.4 collective-permute-done.5.rest_2_
  27.4 0.4 collective-permute-start.10
  27.8 0.0 copy-start.3
  27.8 0.7 copy-done.3
  28.4 0.6 mask.1.bias
  29.0 0.0 collective-permute-done.6.rest_3_
  29.1 0.0 collective-permute-done.7.rest_6_
  29.1 0.0 collective-permute-done.8.rest_7_
  29.1 0.0 collective-permute-done.9.rest_10_
  29.1 0.0 collective-permute-done.10.rest_11_
  29.1 0.0 copy-done
  29.1 0.0 copy-done.1
  29.1 0.0 copy-done.2
  29.1 39.4 %attend0.1 = bf16[1,128,16384]{2,1,0:T(8,128)(2,1)} custom-call(f32[640,128]{1,0:T(8,128)S(1)} %mask.1.bias, bf16[1,128,16384]{2,1,0:T(8,128)(2,1)S(1)} %copy-done.2, bf16[1,128,1024]{2,1,0:T(8,128)(2,1)S(1)} %copy-done, bf16[1,128,1024]{2,1,0:T(8,128)(2,1)S(1)} %copy-done.1, bf16[1,128,1024]{2,1,0:T(8,128)(2,1)S(1)} %collective-permute-done.5.rest_2_, ...), custom_call_target="tpu_custom_call" | custom-call | flops 6000000000 | bytes 1000 | tf_op jit(solution)/shard_map/attend0/pallas_call | solution.py:256
  68.5 0.0 all-to-all-done.received
  68.5 1.0 %unpack.1 = (bf16[128,1,2,1024]{3,2,1,0:T(2,128)(2,1)}, bf16[128,1,2,1024]{3,2,1,0:T(2,128)(2,1)}, bf16[2,8,128]{2,1,0:T(8,128)(2,1)}, bf16[2,8,128]{2,1,0:T(8,128)(2,1)}) custom-call(bf16[128,2,2176]{2,1,0:T(2,128)(2,1)S(1)} %all-to-all-done.received), custom_call_target="tpu_custom_call" | custom-call | flops 1000 | bytes 1000 | tf_op jit(solution)/shard_map/unpack/pallas_call | solution.py:131
Async XLA Ops:
  0.6 9.7 %collective-permute-start = (bf16[1,128,1024]{2,1,0:T(8,128)(2,1)}, bf16[1,128,1024]{2,1,0:T(8,128)(2,1)S(1)}, u32[]{:S(2)}, u32[]{:S(2)}) collective-permute-start(bf16[1,128,1024]{2,1,0:T(8,128)(2,1)} %rest_1_.1), channel_id=1, source_target_pairs={{0,32},{16,48},{32,64},{48,80},{64,96},{80,112},{96,0},{112,16},{1... | collective-permute-start | bytes 786440 | tf_op jit(solution)/shard_map/ppermute | solution.py:278
  2.8 7.5 %collective-permute-start.1 = (bf16[1,128,1024]{2,1,0:T(8,128)(2,1)}, bf16[1,128,1024]{2,1,0:T(8,128)(2,1)S(1)}, u32[]{:S(2)}, u32[]{:S(2)}) collective-permute-start(bf16[1,128,1024]{2,1,0:T(8,128)(2,1)} %rest_0_.1), channel_id=1, source_target_pairs={{0,96},{16,112},{32,0},{48,16},{64,32},{80,48},{96,64},{112,80},{1... | collective-permute-start | bytes 786440 | tf_op jit(solution)/shard_map/ppermute | solution.py:278
  4.3 20.5 %collective-permute-start.2 = (bf16[1,128,1024]{2,1,0:T(8,128)(2,1)}, bf16[1,128,1024]{2,1,0:T(8,128)(2,1)S(1)}, u32[]{:S(2)}, u32[]{:S(2)}) collective-permute-start(bf16[1,128,1024]{2,1,0:T(8,128)(2,1)} %rest_0_.1), channel_id=1, source_target_pairs={{0,32},{16,48},{32,64},{48,80},{64,96},{80,112},{96,0},{112,16},{1... | collective-permute-start | bytes 786440 | tf_op jit(solution)/shard_map/ppermute | solution.py:278
  10.4 14.5 %collective-permute-start.3 = (bf16[1,128,1024]{2,1,0:T(8,128)(2,1)S(1)}, bf16[1,128,1024]{2,1,0:T(8,128)(2,1)S(1)}, u32[]{:S(2)}, u32[]{:S(2)}) collective-permute-start(bf16[1,128,1024]{2,1,0:T(8,128)(2,1)S(1)} %collective-permute-done.1), channel_id=1, source_target_pairs={{0,96},{16,112},{32,0},{48,16},{64,32},{80,48},{96,64},{112,80},{1... | collective-permute-start | bytes 786440 | tf_op jit(solution)/shard_map/ppermute | solution.py:278
  12.9 12.0 %collective-permute-start.4 = (bf16[1,128,1024]{2,1,0:T(8,128)(2,1)S(1)}, bf16[1,128,1024]{2,1,0:T(8,128)(2,1)S(1)}, u32[]{:S(2)}, u32[]{:S(2)}) collective-permute-start(bf16[1,128,1024]{2,1,0:T(8,128)(2,1)S(1)} %collective-permute-done.rest_5_), channel_id=1, source_target_pairs={{0,32},{16,48},{32,64},{48,80},{64,96},{80,112},{96,0},{112,16},{1... | collective-permute-start | bytes 786440 | tf_op jit(solution)/shard_map/ppermute | solution.py:278
  12.9 55.6 %all-to-all-start = ((bf16[128,2,2176]{2,1,0:T(2,128)(2,1)}), bf16[128,2,2176]{2,1,0:T(2,128)(2,1)S(1)}, u32[]{:S(2)}, u32[]{:S(2)}) async-start(bf16[128,2,2176]{2,1,0:T(2,128)(2,1)} %pack.1), calls=%async_computation | async-start | bytes 2228224 | tf_op jit(solution)/shard_map/all_to_all | solution.py:293
  24.8 4.3 %copy-start = (bf16[1,128,1024]{2,1,0:T(8,128)(2,1)S(1)}, bf16[1,128,1024]{2,1,0:T(8,128)(2,1)}, u32[]{:S(2)}) copy-start(bf16[1,128,1024]{2,1,0:T(8,128)(2,1)} %rest_0_.1) | copy-start | bytes 786436
  24.8 4.3 %copy-start.1 = (bf16[1,128,1024]{2,1,0:T(8,128)(2,1)S(1)}, bf16[1,128,1024]{2,1,0:T(8,128)(2,1)}, u32[]{:S(2)}) copy-start(bf16[1,128,1024]{2,1,0:T(8,128)(2,1)} %rest_1_.1) | copy-start | bytes 786436
  24.8 4.3 %copy-start.2 = (bf16[1,128,16384]{2,1,0:T(8,128)(2,1)S(1)}, bf16[1,128,16384]{2,1,0:T(8,128)(2,1)}, u32[]{:S(2)}) copy-start(bf16[1,128,16384]{2,1,0:T(8,128)(2,1)} %queries.1) | copy-start | bytes 12582916
  24.9 2.5 %collective-permute-start.5 = (bf16[1,128,1024]{2,1,0:T(8,128)(2,1)}, bf16[1,128,1024]{2,1,0:T(8,128)(2,1)S(1)}, u32[]{:S(2)}, u32[]{:S(2)}) collective-permute-start(bf16[1,128,1024]{2,1,0:T(8,128)(2,1)} %rest_0_.1), channel_id=1, source_target_pairs={{0,16},{16,0},{32,48},{48,32},{64,80},{80,64},{96,112},{112,96},{1... | collective-permute-start | bytes 786440 | tf_op jit(solution)/shard_map/ppermute | solution.py:281
  26.0 3.0 %collective-permute-start.6 = (bf16[1,128,1024]{2,1,0:T(8,128)(2,1)}, bf16[1,128,1024]{2,1,0:T(8,128)(2,1)S(1)}, u32[]{:S(2)}, u32[]{:S(2)}) collective-permute-start(bf16[1,128,1024]{2,1,0:T(8,128)(2,1)} %rest_1_.1), channel_id=1, source_target_pairs={{0,16},{16,0},{32,48},{48,32},{64,80},{80,64},{96,112},{112,96},{1... | collective-permute-start | bytes 786440 | tf_op jit(solution)/shard_map/ppermute | solution.py:281
  26.1 2.9 %collective-permute-start.7 = (bf16[1,128,1024]{2,1,0:T(8,128)(2,1)S(1)}, bf16[1,128,1024]{2,1,0:T(8,128)(2,1)S(1)}, u32[]{:S(2)}, u32[]{:S(2)}) collective-permute-start(bf16[1,128,1024]{2,1,0:T(8,128)(2,1)S(1)} %collective-permute-done.2.rest_4_), channel_id=1, source_target_pairs={{0,16},{16,0},{32,48},{48,32},{64,80},{80,64},{96,112},{112,96},{1... | collective-permute-start | bytes 786440 | tf_op jit(solution)/shard_map/ppermute | solution.py:281
  26.5 2.5 %collective-permute-start.8 = (bf16[1,128,1024]{2,1,0:T(8,128)(2,1)S(1)}, bf16[1,128,1024]{2,1,0:T(8,128)(2,1)S(1)}, u32[]{:S(2)}, u32[]{:S(2)}) collective-permute-start(bf16[1,128,1024]{2,1,0:T(8,128)(2,1)S(1)} %collective-permute-done.rest_5_), channel_id=1, source_target_pairs={{0,16},{16,0},{32,48},{48,32},{64,80},{80,64},{96,112},{112,96},{1... | collective-permute-start | bytes 786440 | tf_op jit(solution)/shard_map/ppermute | solution.py:281
  26.6 2.4 %collective-permute-start.9 = (bf16[1,128,1024]{2,1,0:T(8,128)(2,1)S(1)}, bf16[1,128,1024]{2,1,0:T(8,128)(2,1)S(1)}, u32[]{:S(2)}, u32[]{:S(2)}) collective-permute-start(bf16[1,128,1024]{2,1,0:T(8,128)(2,1)S(1)} %collective-permute-done.3.rest_8_), channel_id=1, source_target_pairs={{0,16},{16,0},{32,48},{48,32},{64,80},{80,64},{96,112},{112,96},{1... | collective-permute-start | bytes 786440 | tf_op jit(solution)/shard_map/ppermute | solution.py:281
  27.4 1.7 %collective-permute-start.10 = (bf16[1,128,1024]{2,1,0:T(8,128)(2,1)S(1)}, bf16[1,128,1024]{2,1,0:T(8,128)(2,1)S(1)}, u32[]{:S(2)}, u32[]{:S(2)}) collective-permute-start(bf16[1,128,1024]{2,1,0:T(8,128)(2,1)S(1)} %collective-permute-done.4.rest_9_), channel_id=1, source_target_pairs={{0,16},{16,0},{32,48},{48,32},{64,80},{80,64},{96,112},{112,96},{1... | collective-permute-start | bytes 786440 | tf_op jit(solution)/shard_map/ppermute | solution.py:281
  27.8 0.7 copy-start.3

commit v6 on v5

--- a/solution.py
+++ b/solution.py
@@ -175,12 +175,20 @@
 
 
 def attend_kernel(first, heads, bias, queries, *rest):
-    out, o_buf, sums, o_sem = rest[-4:]
+    out, q_buf, o_buf, sums, q_sem, o_sem = rest[-6:]
+    def query_copy(h):
+        at = pl.ds(pl.multiple_of(h * HEAD_WIDTH, HEAD_WIDTH), HEAD_WIDTH)
+        from_at = pl.ds(pl.multiple_of((first + h) * HEAD_WIDTH, HEAD_WIDTH), HEAD_WIDTH)
+        return pltpu.make_async_copy(queries.at[0, :, from_at], q_buf.at[:, at], q_sem.at[h])
+
     def out_copy(h, g0):
         width = STACK * HD
         at = pl.ds(pl.multiple_of(h * HEAD_WIDTH + g0 * HD, width), width)
         to_at = pl.ds(pl.multiple_of((first + h) * HEAD_WIDTH + g0 * HD, width), width)
         return pltpu.make_async_copy(o_buf.at[:, at], out.at[0, :, to_at], o_sem.at[h])
+
+    for h in range(heads):
+        query_copy(h).start()
 
     even = jnp.full((TOK, HD), lax.rem(lax.axis_index("ctx"), 2), jnp.int32) == 0
     sums[0] = jnp.ones((8, STACK * TOK), jnp.float32)
@@ -201,7 +209,7 @@
             return pl.ds(pl.multiple_of(h * HEAD_WIDTH + g * HD, HD), HD)
 
         def score(g0):
-            rows = jnp.concatenate([queries[0, :, head_lanes(first + h, g0 + g)] for g in range(stack)], 0)
+            rows = jnp.concatenate([q_buf[:, head_lanes(h, g0 + g)] for g in range(stack)], 0)
             return lax.dot_general(key_rows, rows, NT, preferred_element_type=jnp.float32)
 
         def finish(g0, scores):
@@ -229,6 +237,7 @@
             scores = following
 
     def first_pass(h, carry):
+        query_copy(h).wait()
         one_head(h, STACK, False)
         return carry
 
@@ -255,16 +264,18 @@
     more = () if partial is None else (partial,)
     return pl.pallas_call(
         functools.partial(attend_kernel, first, heads),
-        in_specs=[VMEM, VMEM] + [VMEM] * len(operands) + [HBM] * len(more),
+        in_specs=[VMEM, HBM] + [VMEM] * len(operands) + [HBM] * len(more),
         out_specs=HBM,
         out_shape=jax.ShapeDtypeStruct(queries.shape, jnp.bfloat16),
         scratch_shapes=[
             pltpu.VMEM((TOK, heads * HEAD_WIDTH), jnp.bfloat16),
+            pltpu.VMEM((TOK, heads * HEAD_WIDTH), jnp.bfloat16),
             pltpu.VMEM((2, 8, STACK * TOK), jnp.float32),
+            pltpu.SemaphoreType.DMA((heads,)),
             pltpu.SemaphoreType.DMA((heads,)),
         ],
         input_output_aliases={2 + len(operands): 0} if more else {},
-        compiler_params=pltpu.CompilerParams(vmem_limit_bytes=28 * 2**20),
+        compiler_params=pltpu.CompilerParams(vmem_limit_bytes=50 * 2**20),
         cost_estimate=pl.CostEstimate(flops=6000000000, bytes_accessed=1000, transcendentals=0),
         name=f"attend{first}",
     )(bias, queries, *operands, *more)
@@ -285,9 +296,9 @@
     near_keys = chips_on(keys, 1)
 
     message = pack(owners.reshape(PAGES_DEV), keys, values)
-    near_values, ahead_keys, message = lax.optimization_barrier((near_values, ahead_keys, message))
     lengths, message = lax.optimization_barrier((lengths, message))
     bias = mask(lengths)
+    near_values, ahead_keys, message, bias = lax.optimization_barrier((near_values, ahead_keys, message, bias))
     far_values = chips_on(near_values, 1)
     far_keys = chips_on(ahead_keys, -1)
     received = lax.all_to_all(message, ("ctx", "dec"), split_axis=0, concat_axis=0, tiled=True)

time: 69.7 us -> 70.7 us (1.014)
  Pallas kernels: 45.2 us -> 46.3 us
    ppermute x5, waiting for transfers between devices: 1.81 us -> 0.53 us  [chips_on(): lax.ppermute(block, 'ctx', [(i, (i + step) % ctx_count) for i in range(ct...]
    ppermute x6, waiting for transfers between devices: 0.36 us -> 1.64 us  [swap(): return lax.ppermute(block, 'ctx', [(i, i ^ 1) for i in range(ctx_count)])]
    pallas_call x1, Pallas kernels: 39.4 us -> 40.4 us  [attend(): pl.pallas_call(functools.partial(attend_kernel, first, heads), in_specs=[...]
  transfers between devices with their start and end apart: 12 -> 12, of which waited for: 2 -> 6; matrix products, arithmetic and copies ran while one was open for 0% -> 0% of each run, Pallas kernels for 64% -> 64%
where the time goes in v6:
time: 70.7 us; the launch traced here: 70.5 us
  Pallas kernels  46.3 us (65%)
  starting transfers between devices  20.7 us (29%)
  waiting for transfers between devices  2.17 us (3%)
  between operations  0.72 us (1%)
    pallas_call x1, Pallas kernels, attend(): pl.pallas_call(functools.partial(attend_kernel, first, heads), in_specs=[...  40.4 us
    all_to_all x1, starting transfers between devices, body(): lax.all_to_all(message, ('ctx', 'dec'), split_axis=0, concat_axis=0, tile...  11.9 us
    ppermute x5, starting transfers between devices, chips_on(): lax.ppermute(block, 'ctx', [(i, (i + step) % ctx_count) for i in range(ct...  6.24 us
    pallas_call x1, Pallas kernels, pack(): pl.pallas_call(pack_kernel, in_specs=[SMEM, VMEM, VMEM], out_specs=HBM, o...  4.21 us
    ppermute x6, starting transfers between devices, swap(): return lax.ppermute(block, 'ctx', [(i, i ^ 1) for i in range(ctx_count)])  2.54 us
    ppermute x6, waiting for transfers between devices, swap(): return lax.ppermute(block, 'ctx', [(i, i ^ 1) for i in range(ctx_count)])  1.64 us
  transfers between devices with their start and end apart: 12, of which 6 were waited for; matrix products, arithmetic and copies ran while one was open for 0% of the time, Pallas kernels for 64%

profile of v6, /device:TPU:1, one launch (start us, length us, event | category | flops | bytes accessed | tf_op | source)
XLA Modules:
  0.0 70.5 jit_solution(12923800744746193834)
XLA Ops:
  0.6 2.2 %collective-permute-start = (bf16[1,128,1024]{2,1,0:T(8,128)(2,1)}, bf16[1,128,1024]{2,1,0:T(8,128)(2,1)S(1)}, u32[]{:S(2)}, u32[]{:S(2)}) collective-permute-start(bf16[1,128,1024]{2,1,0:T(8,128)(2,1)} %rest_1_.1), channel_id=1, source_target_pairs={{0,32},{16,48},{32,64},{48,80},{64,96},{80,112},{96,0},{112,16},{1... | collective-permute-start | bytes 786440 | tf_op jit(solution)/shard_map/ppermute | solution.py:289
  2.8 1.5 %collective-permute-start.1 = (bf16[1,128,1024]{2,1,0:T(8,128)(2,1)}, bf16[1,128,1024]{2,1,0:T(8,128)(2,1)S(1)}, u32[]{:S(2)}, u32[]{:S(2)}) collective-permute-start(bf16[1,128,1024]{2,1,0:T(8,128)(2,1)} %rest_0_.1), channel_id=1, source_target_pairs={{0,96},{16,112},{32,0},{48,16},{64,32},{80,48},{96,64},{112,80},{1... | collective-permute-start | bytes 786440 | tf_op jit(solution)/shard_map/ppermute | solution.py:289
  4.3 0.0 collective-permute-start.2
  4.4 4.2 %pack.1 = bf16[128,2,2176]{2,1,0:T(2,128)(2,1)} custom-call(s32[16]{0:T(128)} %bitcast.7, bf16[1,128,1024]{2,1,0:T(8,128)(2,1)} %rest_0_.1, bf16[1,128,1024]{2,1,0:T(8,128)(2,1)} %rest_1_.1), custom_call_target="tpu_custom_call" | custom-call | flops 1000 | bytes 1000 | tf_op jit(solution)/shard_map/pack/pallas_call | solution.py:95
  8.6 0.0 copy-start.2
  8.6 0.6 copy-done.2
  9.2 0.0 copy-start
  9.2 0.0 copy-start.1
  9.2 0.6 mask.1.bias
  9.8 0.5 collective-permute-done.rest_5_
  10.4 0.0 collective-permute-done.1
  10.4 2.5 %collective-permute-start.3 = (bf16[1,128,1024]{2,1,0:T(8,128)(2,1)S(1)}, bf16[1,128,1024]{2,1,0:T(8,128)(2,1)S(1)}, u32[]{:S(2)}, u32[]{:S(2)}) collective-permute-start(bf16[1,128,1024]{2,1,0:T(8,128)(2,1)S(1)} %collective-permute-done.1), channel_id=1, source_target_pairs={{0,96},{16,112},{32,0},{48,16},{64,32},{80,48},{96,64},{112,80},{1... | collective-permute-start | bytes 786440 | tf_op jit(solution)/shard_map/ppermute | solution.py:289
  12.9 0.0 collective-permute-start.4
  12.9 11.9 %all-to-all-start = ((bf16[128,2,2176]{2,1,0:T(2,128)(2,1)}), bf16[128,2,2176]{2,1,0:T(2,128)(2,1)S(1)}, u32[]{:S(2)}, u32[]{:S(2)}) async-start(bf16[128,2,2176]{2,1,0:T(2,128)(2,1)} %pack.1), calls=%async_computation | async-start | bytes 2228224 | tf_op jit(solution)/shard_map/all_to_all | solution.py:304
  24.8 0.0 collective-permute-done.2.rest_4_
  24.8 0.0 collective-permute-done.3.rest_8_
  24.8 0.0 collective-permute-done.4.rest_9_
  24.8 0.0 copy-done
  24.9 1.1 %collective-permute-start.5 = (bf16[1,128,1024]{2,1,0:T(8,128)(2,1)S(1)}, bf16[1,128,1024]{2,1,0:T(8,128)(2,1)S(1)}, u32[]{:S(2)}, u32[]{:S(2)}) collective-permute-start(bf16[1,128,1024]{2,1,0:T(8,128)(2,1)S(1)} %copy-done), channel_id=1, source_target_pairs={{0,16},{16,0},{32,48},{48,32},{64,80},{80,64},{96,112},{112,96},{1... | collective-permute-start | bytes 786440 | tf_op jit(solution)/shard_map/ppermute | solution.py:292
  26.0 0.0 copy-done.1
  26.0 0.1 collective-permute-start.6
  26.1 0.4 collective-permute-start.7
  26.5 0.1 collective-permute-start.8
  26.6 0.4 collective-permute-start.9
  27.0 0.1 collective-permute-done.5.rest_2_
  27.2 0.4 collective-permute-start.10
  27.5 0.0 collective-permute-done.6.rest_3_
  27.5 0.4 collective-permute-done.7.rest_6_
  27.9 0.4 collective-permute-done.8.rest_7_
  28.3 0.4 collective-permute-done.9.rest_10_
  28.7 0.4 collective-permute-done.10.rest_11_
  29.0 40.4 %attend0.1 = bf16[1,128,16384]{2,1,0:T(8,128)(2,1)} custom-call(f32[640,128]{1,0:T(8,128)S(1)} %mask.1.bias, bf16[1,128,16384]{2,1,0:T(8,128)(2,1)} %queries.1, bf16[1,128,1024]{2,1,0:T(8,128)(2,1)S(1)} %copy-done, bf16[1,128,1024]{2,1,0:T(8,128)(2,1)S(1)} %copy-done.1, bf16[1,128,1024]{2,1,0:T(8,128)(2,1)S(1)} %collective-permute-done.5.rest_2_, ...), custom_call_target="tpu_custom_call" | custom-call | flops 6000000000 | bytes 1000 | tf_op jit(solution)/shard_map/attend0/pallas_call | solution.py:265
  69.5 0.0 all-to-all-done.received
  69.5 1.0 %unpack.1 = (bf16[128,1,2,1024]{3,2,1,0:T(2,128)(2,1)}, bf16[128,1,2,1024]{3,2,1,0:T(2,128)(2,1)}, bf16[2,8,128]{2,1,0:T(8,128)(2,1)}, bf16[2,8,128]{2,1,0:T(8,128)(2,1)}) custom-call(bf16[128,2,2176]{2,1,0:T(2,128)(2,1)S(1)} %all-to-all-done.received), custom_call_target="tpu_custom_call" | custom-call | flops 1000 | bytes 1000 | tf_op jit(solution)/shard_map/unpack/pallas_call | solution.py:131
Async XLA Ops:
  0.6 9.7 %collective-permute-start = (bf16[1,128,1024]{2,1,0:T(8,128)(2,1)}, bf16[1,128,1024]{2,1,0:T(8,128)(2,1)S(1)}, u32[]{:S(2)}, u32[]{:S(2)}) collective-permute-start(bf16[1,128,1024]{2,1,0:T(8,128)(2,1)} %rest_1_.1), channel_id=1, source_target_pairs={{0,32},{16,48},{32,64},{48,80},{64,96},{80,112},{96,0},{112,16},{1... | collective-permute-start | bytes 786440 | tf_op jit(solution)/shard_map/ppermute | solution.py:289
  2.8 7.5 %collective-permute-start.1 = (bf16[1,128,1024]{2,1,0:T(8,128)(2,1)}, bf16[1,128,1024]{2,1,0:T(8,128)(2,1)S(1)}, u32[]{:S(2)}, u32[]{:S(2)}) collective-permute-start(bf16[1,128,1024]{2,1,0:T(8,128)(2,1)} %rest_0_.1), channel_id=1, source_target_pairs={{0,96},{16,112},{32,0},{48,16},{64,32},{80,48},{96,64},{112,80},{1... | collective-permute-start | bytes 786440 | tf_op jit(solution)/shard_map/ppermute | solution.py:289
  4.3 20.5 %collective-permute-start.2 = (bf16[1,128,1024]{2,1,0:T(8,128)(2,1)}, bf16[1,128,1024]{2,1,0:T(8,128)(2,1)S(1)}, u32[]{:S(2)}, u32[]{:S(2)}) collective-permute-start(bf16[1,128,1024]{2,1,0:T(8,128)(2,1)} %rest_0_.1), channel_id=1, source_target_pairs={{0,32},{16,48},{32,64},{48,80},{64,96},{80,112},{96,0},{112,16},{1... | collective-permute-start | bytes 786440 | tf_op jit(solution)/shard_map/ppermute | solution.py:289
  8.6 0.7 copy-start.2
  9.2 15.6 %copy-start = (bf16[1,128,1024]{2,1,0:T(8,128)(2,1)S(1)}, bf16[1,128,1024]{2,1,0:T(8,128)(2,1)}, u32[]{:S(2)}) copy-start(bf16[1,128,1024]{2,1,0:T(8,128)(2,1)} %rest_0_.1) | copy-start | bytes 786436
  9.2 16.8 %copy-start.1 = (bf16[1,128,1024]{2,1,0:T(8,128)(2,1)S(1)}, bf16[1,128,1024]{2,1,0:T(8,128)(2,1)}, u32[]{:S(2)}) copy-start(bf16[1,128,1024]{2,1,0:T(8,128)(2,1)} %rest_1_.1) | copy-start | bytes 786436
  10.4 14.5 %collective-permute-start.3 = (bf16[1,128,1024]{2,1,0:T(8,128)(2,1)S(1)}, bf16[1,128,1024]{2,1,0:T(8,128)(2,1)S(1)}, u32[]{:S(2)}, u32[]{:S(2)}) collective-permute-start(bf16[1,128,1024]{2,1,0:T(8,128)(2,1)S(1)} %collective-permute-done.1), channel_id=1, source_target_pairs={{0,96},{16,112},{32,0},{48,16},{64,32},{80,48},{96,64},{112,80},{1... | collective-permute-start | bytes 786440 | tf_op jit(solution)/shard_map/ppermute | solution.py:289
  12.9 12.0 %collective-permute-start.4 = (bf16[1,128,1024]{2,1,0:T(8,128)(2,1)S(1)}, bf16[1,128,1024]{2,1,0:T(8,128)(2,1)S(1)}, u32[]{:S(2)}, u32[]{:S(2)}) collective-permute-start(bf16[1,128,1024]{2,1,0:T(8,128)(2,1)S(1)} %collective-permute-done.rest_5_), channel_id=1, source_target_pairs={{0,32},{16,48},{32,64},{48,80},{64,96},{80,112},{96,0},{112,16},{1... | collective-permute-start | bytes 786440 | tf_op jit(solution)/shard_map/ppermute | solution.py:289
  12.9 56.6 %all-to-all-start = ((bf16[128,2,2176]{2,1,0:T(2,128)(2,1)}), bf16[128,2,2176]{2,1,0:T(2,128)(2,1)S(1)}, u32[]{:S(2)}, u32[]{:S(2)}) async-start(bf16[128,2,2176]{2,1,0:T(2,128)(2,1)} %pack.1), calls=%async_computation | async-start | bytes 2228224 | tf_op jit(solution)/shard_map/all_to_all | solution.py:304
  24.9 2.3 %collective-permute-start.5 = (bf16[1,128,1024]{2,1,0:T(8,128)(2,1)S(1)}, bf16[1,128,1024]{2,1,0:T(8,128)(2,1)S(1)}, u32[]{:S(2)}, u32[]{:S(2)}) collective-permute-start(bf16[1,128,1024]{2,1,0:T(8,128)(2,1)S(1)} %copy-done), channel_id=1, source_target_pairs={{0,16},{16,0},{32,48},{48,32},{64,80},{80,64},{96,112},{112,96},{1... | collective-permute-start | bytes 786440 | tf_op jit(solution)/shard_map/ppermute | solution.py:292
  26.0 1.5 %collective-permute-start.6 = (bf16[1,128,1024]{2,1,0:T(8,128)(2,1)S(1)}, bf16[1,128,1024]{2,1,0:T(8,128)(2,1)S(1)}, u32[]{:S(2)}, u32[]{:S(2)}) collective-permute-start(bf16[1,128,1024]{2,1,0:T(8,128)(2,1)S(1)} %copy-done.1), channel_id=1, source_target_pairs={{0,16},{16,0},{32,48},{48,32},{64,80},{80,64},{96,112},{112,96},{1... | collective-permute-start | bytes 786440 | tf_op jit(solution)/shard_map/ppermute | solution.py:292
  26.1 1.8 %collective-permute-start.7 = (bf16[1,128,1024]{2,1,0:T(8,128)(2,1)S(1)}, bf16[1,128,1024]{2,1,0:T(8,128)(2,1)S(1)}, u32[]{:S(2)}, u32[]{:S(2)}) collective-permute-start(bf16[1,128,1024]{2,1,0:T(8,128)(2,1)S(1)} %collective-permute-done.2.rest_4_), channel_id=1, source_target_pairs={{0,16},{16,0},{32,48},{48,32},{64,80},{80,64},{96,112},{112,96},{1... | collective-permute-start | bytes 786440 | tf_op jit(solution)/shard_map/ppermute | solution.py:292
  26.5 1.8 %collective-permute-start.8 = (bf16[1,128,1024]{2,1,0:T(8,128)(2,1)S(1)}, bf16[1,128,1024]{2,1,0:T(8,128)(2,1)S(1)}, u32[]{:S(2)}, u32[]{:S(2)}) collective-permute-start(bf16[1,128,1024]{2,1,0:T(8,128)(2,1)S(1)} %collective-permute-done.rest_5_), channel_id=1, source_target_pairs={{0,16},{16,0},{32,48},{48,32},{64,80},{80,64},{96,112},{112,96},{1... | collective-permute-start | bytes 786440 | tf_op jit(solution)/shard_map/ppermute | solution.py:292
  26.6 2.0 %collective-permute-start.9 = (bf16[1,128,1024]{2,1,0:T(8,128)(2,1)S(1)}, bf16[1,128,1024]{2,1,0:T(8,128)(2,1)S(1)}, u32[]{:S(2)}, u32[]{:S(2)}) collective-permute-start(bf16[1,128,1024]{2,1,0:T(8,128)(2,1)S(1)} %collective-permute-done.3.rest_8_), channel_id=1, source_target_pairs={{0,16},{16,0},{32,48},{48,32},{64,80},{80,64},{96,112},{112,96},{1... | collective-permute-start | bytes 786440 | tf_op jit(solution)/shard_map/ppermute | solution.py:292
  27.2 1.9 %collective-permute-start.10 = (bf16[1,128,1024]{2,1,0:T(8,128)(2,1)S(1)}, bf16[1,128,1024]{2,1,0:T(8,128)(2,1)S(1)}, u32[]{:S(2)}, u32[]{:S(2)}) collective-permute-start(bf16[1,128,1024]{2,1,0:T(8,128)(2,1)S(1)} %collective-permute-done.4.rest_9_), channel_id=1, source_target_pairs={{0,16},{16,0},{32,48},{48,32},{64,80},{80,64},{96,112},{112,96},{1... | collective-permute-start | bytes 786440 | tf_op jit(solution)/shard_map/ppermute | solution.py:292

commit v7 on v5

--- a/solution.py
+++ b/solution.py
@@ -285,11 +285,11 @@
     near_keys = chips_on(keys, 1)
 
     message = pack(owners.reshape(PAGES_DEV), keys, values)
-    near_values, ahead_keys, message = lax.optimization_barrier((near_values, ahead_keys, message))
-    lengths, message = lax.optimization_barrier((lengths, message))
+    near_values, message = lax.optimization_barrier((near_values, message))
+    far_values = chips_on(near_values, 1)
+    ahead_keys, lengths, message = lax.optimization_barrier((ahead_keys, lengths, message))
+    far_keys = chips_on(ahead_keys, -1)
     bias = mask(lengths)
-    far_values = chips_on(near_values, 1)
-    far_keys = chips_on(ahead_keys, -1)
     received = lax.all_to_all(message, ("ctx", "dec"), split_axis=0, concat_axis=0, tiled=True)
 
     near_keys, near_values, far_keys, far_values, own = lax.optimization_barrier(

time: 69.7 us -> 69.2 us (level)
  the two profiles are of different devices: /device:TPU:1 before, /device:TPU:0 now
where the time goes in v7:
time: 69.2 us; the launch traced here: 68.4 us
  Pallas kernels  45.2 us (65%)
  starting transfers between devices  18.2 us (26%)
  waiting for transfers between devices  3.56 us (5%)
  between operations  0.77 us (1%)
    pallas_call x1, Pallas kernels, attend(): pl.pallas_call(functools.partial(attend_kernel, first, heads), in_specs=[...  39.4 us
    all_to_all x1, starting transfers between devices, body(): lax.all_to_all(message, ('ctx', 'dec'), split_axis=0, concat_axis=0, tile...  11.1 us
    ppermute x5, starting transfers between devices, chips_on(): lax.ppermute(block, 'ctx', [(i, (i + step) % ctx_count) for i in range(ct...  5.81 us
    pallas_call x1, Pallas kernels, pack(): pl.pallas_call(pack_kernel, in_specs=[SMEM, VMEM, VMEM], out_specs=HBM, o...  4.2 us
    ppermute x5, waiting for transfers between devices, chips_on(): lax.ppermute(block, 'ctx', [(i, (i + step) % ctx_count) for i in range(ct...  2.7 us
  transfers between devices with their start and end apart: 12, of which 3 were waited for; matrix products, arithmetic and copies ran while one was open for 0% of the time, Pallas kernels for 65%

profile of v7, /device:TPU:0, one launch (start us, length us, event | category | flops | bytes accessed | tf_op | source)
XLA Modules:
  0.0 68.4 jit_solution(2768996438025188847)
XLA Ops:
  0.6 1.7 %collective-permute-start.1 = (bf16[1,128,1024]{2,1,0:T(8,128)(2,1)}, bf16[1,128,1024]{2,1,0:T(8,128)(2,1)S(1)}, u32[]{:S(2)}, u32[]{:S(2)}) collective-permute-start(bf16[1,128,1024]{2,1,0:T(8,128)(2,1)} %rest_1_.1), channel_id=1, source_target_pairs={{0,32},{16,48},{32,64},{48,80},{64,96},{80,112},{96,0},{112,16},{1... | collective-permute-start | bytes 786440 | tf_op jit(solution)/shard_map/ppermute | solution.py:278
  2.4 1.6 %collective-permute-start = (bf16[1,128,1024]{2,1,0:T(8,128)(2,1)}, bf16[1,128,1024]{2,1,0:T(8,128)(2,1)S(1)}, u32[]{:S(2)}, u32[]{:S(2)}) collective-permute-start(bf16[1,128,1024]{2,1,0:T(8,128)(2,1)} %rest_0_.1), channel_id=1, source_target_pairs={{0,96},{16,112},{32,0},{48,16},{64,32},{80,48},{96,64},{112,80},{1... | collective-permute-start | bytes 786440 | tf_op jit(solution)/shard_map/ppermute | solution.py:278
  3.9 0.4 collective-permute-start.2
  4.4 4.2 %pack.1 = bf16[128,2,2176]{2,1,0:T(2,128)(2,1)} custom-call(s32[16]{0:T(128)} %bitcast.7, bf16[1,128,1024]{2,1,0:T(8,128)(2,1)} %rest_0_.1, bf16[1,128,1024]{2,1,0:T(8,128)(2,1)} %rest_1_.1), custom_call_target="tpu_custom_call" | custom-call | flops 1000 | bytes 1000 | tf_op jit(solution)/shard_map/pack/pallas_call | solution.py:95
  8.6 2.7 %collective-permute-done.1.rest_5_ = bf16[1,128,1024]{2,1,0:T(8,128)(2,1)S(1)} collective-permute-done((bf16[1,128,1024]{2,1,0:T(8,128)(2,1)}, bf16[1,128,1024]{2,1,0:T(8,128)(2,1)S(1)}, u32[]{:S(2)}, u32[]{:S(2)}) %collective-permute-start.1) | collective-permute-done | bytes 262176 | tf_op jit(solution)/shard_map/ppermute | solution.py:278
  11.3 0.0 collective-permute-done
  11.3 2.1 %collective-permute-start.3 = (bf16[1,128,1024]{2,1,0:T(8,128)(2,1)S(1)}, bf16[1,128,1024]{2,1,0:T(8,128)(2,1)S(1)}, u32[]{:S(2)}, u32[]{:S(2)}) collective-permute-start(bf16[1,128,1024]{2,1,0:T(8,128)(2,1)S(1)} %collective-permute-done), channel_id=1, source_target_pairs={{0,96},{16,112},{32,0},{48,16},{64,32},{80,48},{96,64},{112,80},{1... | collective-permute-start | bytes 786440 | tf_op jit(solution)/shard_map/ppermute | solution.py:278
  13.3 0.0 collective-permute-start.4
  13.4 11.1 %all-to-all-start = ((bf16[128,2,2176]{2,1,0:T(2,128)(2,1)}), bf16[128,2,2176]{2,1,0:T(2,128)(2,1)S(1)}, u32[]{:S(2)}, u32[]{:S(2)}) async-start(bf16[128,2,2176]{2,1,0:T(2,128)(2,1)} %pack.1), calls=%async_computation | async-start | bytes 2228224 | tf_op jit(solution)/shard_map/all_to_all | solution.py:293
  24.5 0.0 copy-start
  24.5 0.0 copy-start.1
  24.5 0.0 copy-start.2
  24.5 0.0 collective-permute-done.2.rest_4_
  24.5 0.0 collective-permute-done.3.rest_8_
  24.5 0.0 collective-permute-done.4.rest_9_
  24.5 0.1 collective-permute-start.5
  24.6 0.5 collective-permute-start.6
  25.1 0.1 collective-permute-start.7
  25.2 0.4 collective-permute-start.8
  25.6 0.1 collective-permute-start.9
  25.7 0.6 collective-permute-done.5.rest_2_
  26.4 0.1 collective-permute-start.10
  26.5 0.0 copy-start.3
  26.5 0.7 copy-done.3
  27.1 0.6 mask.1.bias
  27.8 0.0 collective-permute-done.6.rest_3_
  27.8 0.0 collective-permute-done.7.rest_6_
  27.8 0.0 collective-permute-done.8.rest_7_
  27.8 0.0 collective-permute-done.9.rest_10_
  27.8 0.2 collective-permute-done.10.rest_11_
  28.0 0.0 copy-done
  28.0 0.0 copy-done.1
  28.0 0.0 copy-done.2
  28.0 39.4 %attend0.1 = bf16[1,128,16384]{2,1,0:T(8,128)(2,1)} custom-call(f32[640,128]{1,0:T(8,128)S(1)} %mask.1.bias, bf16[1,128,16384]{2,1,0:T(8,128)(2,1)S(1)} %copy-done.2, bf16[1,128,1024]{2,1,0:T(8,128)(2,1)S(1)} %copy-done, bf16[1,128,1024]{2,1,0:T(8,128)(2,1)S(1)} %copy-done.1, bf16[1,128,1024]{2,1,0:T(8,128)(2,1)S(1)} %collective-permute-done.5.rest_2_, ...), custom_call_target="tpu_custom_call" | custom-call | flops 6000000000 | bytes 1000 | tf_op jit(solution)/shard_map/attend0/pallas_call | solution.py:256
  67.4 0.0 all-to-all-done.received
  67.4 1.0 %unpack.1 = (bf16[128,1,2,1024]{3,2,1,0:T(2,128)(2,1)}, bf16[128,1,2,1024]{3,2,1,0:T(2,128)(2,1)}, bf16[2,8,128]{2,1,0:T(8,128)(2,1)}, bf16[2,8,128]{2,1,0:T(8,128)(2,1)}) custom-call(bf16[128,2,2176]{2,1,0:T(2,128)(2,1)S(1)} %all-to-all-done.received), custom_call_target="tpu_custom_call" | custom-call | flops 1000 | bytes 1000 | tf_op jit(solution)/shard_map/unpack/pallas_call | solution.py:131
Async XLA Ops:
  0.6 10.7 %collective-permute-start.1 = (bf16[1,128,1024]{2,1,0:T(8,128)(2,1)}, bf16[1,128,1024]{2,1,0:T(8,128)(2,1)S(1)}, u32[]{:S(2)}, u32[]{:S(2)}) collective-permute-start(bf16[1,128,1024]{2,1,0:T(8,128)(2,1)} %rest_1_.1), channel_id=1, source_target_pairs={{0,32},{16,48},{32,64},{48,80},{64,96},{80,112},{96,0},{112,16},{1... | collective-permute-start | bytes 786440 | tf_op jit(solution)/shard_map/ppermute | solution.py:278
  2.4 8.9 %collective-permute-start = (bf16[1,128,1024]{2,1,0:T(8,128)(2,1)}, bf16[1,128,1024]{2,1,0:T(8,128)(2,1)S(1)}, u32[]{:S(2)}, u32[]{:S(2)}) collective-permute-start(bf16[1,128,1024]{2,1,0:T(8,128)(2,1)} %rest_0_.1), channel_id=1, source_target_pairs={{0,96},{16,112},{32,0},{48,16},{64,32},{80,48},{96,64},{112,80},{1... | collective-permute-start | bytes 786440 | tf_op jit(solution)/shard_map/ppermute | solution.py:278
  3.9 20.6 %collective-permute-start.2 = (bf16[1,128,1024]{2,1,0:T(8,128)(2,1)}, bf16[1,128,1024]{2,1,0:T(8,128)(2,1)S(1)}, u32[]{:S(2)}, u32[]{:S(2)}) collective-permute-start(bf16[1,128,1024]{2,1,0:T(8,128)(2,1)} %rest_0_.1), channel_id=1, source_target_pairs={{0,32},{16,48},{32,64},{48,80},{64,96},{80,112},{96,0},{112,16},{1... | collective-permute-start | bytes 786440 | tf_op jit(solution)/shard_map/ppermute | solution.py:278
  11.3 13.2 %collective-permute-start.3 = (bf16[1,128,1024]{2,1,0:T(8,128)(2,1)S(1)}, bf16[1,128,1024]{2,1,0:T(8,128)(2,1)S(1)}, u32[]{:S(2)}, u32[]{:S(2)}) collective-permute-start(bf16[1,128,1024]{2,1,0:T(8,128)(2,1)S(1)} %collective-permute-done), channel_id=1, source_target_pairs={{0,96},{16,112},{32,0},{48,16},{64,32},{80,48},{96,64},{112,80},{1... | collective-permute-start | bytes 786440 | tf_op jit(solution)/shard_map/ppermute | solution.py:278
  13.3 11.2 %collective-permute-start.4 = (bf16[1,128,1024]{2,1,0:T(8,128)(2,1)S(1)}, bf16[1,128,1024]{2,1,0:T(8,128)(2,1)S(1)}, u32[]{:S(2)}, u32[]{:S(2)}) collective-permute-start(bf16[1,128,1024]{2,1,0:T(8,128)(2,1)S(1)} %collective-permute-done.1.rest_5_), channel_id=1, source_target_pairs={{0,32},{16,48},{32,64},{48,80},{64,96},{80,112},{96,0},{112,16},{1... | collective-permute-start | bytes 786440 | tf_op jit(solution)/shard_map/ppermute | solution.py:278
  13.4 54.1 %all-to-all-start = ((bf16[128,2,2176]{2,1,0:T(2,128)(2,1)}), bf16[128,2,2176]{2,1,0:T(2,128)(2,1)S(1)}, u32[]{:S(2)}, u32[]{:S(2)}) async-start(bf16[128,2,2176]{2,1,0:T(2,128)(2,1)} %pack.1), calls=%async_computation | async-start | bytes 2228224 | tf_op jit(solution)/shard_map/all_to_all | solution.py:293
  24.5 3.6 %copy-start = (bf16[1,128,1024]{2,1,0:T(8,128)(2,1)S(1)}, bf16[1,128,1024]{2,1,0:T(8,128)(2,1)}, u32[]{:S(2)}) copy-start(bf16[1,128,1024]{2,1,0:T(8,128)(2,1)} %rest_0_.1) | copy-start | bytes 786436
  24.5 3.6 %copy-start.1 = (bf16[1,128,1024]{2,1,0:T(8,128)(2,1)S(1)}, bf16[1,128,1024]{2,1,0:T(8,128)(2,1)}, u32[]{:S(2)}) copy-start(bf16[1,128,1024]{2,1,0:T(8,128)(2,1)} %rest_1_.1) | copy-start | bytes 786436
  24.5 3.5 %copy-start.2 = (bf16[1,128,16384]{2,1,0:T(8,128)(2,1)S(1)}, bf16[1,128,16384]{2,1,0:T(8,128)(2,1)}, u32[]{:S(2)}) copy-start(bf16[1,128,16384]{2,1,0:T(8,128)(2,1)} %queries.1) | copy-start | bytes 12582916
  24.5 1.8 %collective-permute-start.5 = (bf16[1,128,1024]{2,1,0:T(8,128)(2,1)}, bf16[1,128,1024]{2,1,0:T(8,128)(2,1)S(1)}, u32[]{:S(2)}, u32[]{:S(2)}) collective-permute-start(bf16[1,128,1024]{2,1,0:T(8,128)(2,1)} %rest_0_.1), channel_id=1, source_target_pairs={{0,16},{16,0},{32,48},{48,32},{64,80},{80,64},{96,112},{112,96},{1... | collective-permute-start | bytes 786440 | tf_op jit(solution)/shard_map/ppermute | solution.py:281
  24.6 3.1 %collective-permute-start.6 = (bf16[1,128,1024]{2,1,0:T(8,128)(2,1)}, bf16[1,128,1024]{2,1,0:T(8,128)(2,1)S(1)}, u32[]{:S(2)}, u32[]{:S(2)}) collective-permute-start(bf16[1,128,1024]{2,1,0:T(8,128)(2,1)} %rest_1_.1), channel_id=1, source_target_pairs={{0,16},{16,0},{32,48},{48,32},{64,80},{80,64},{96,112},{112,96},{1... | collective-permute-start | bytes 786440 | tf_op jit(solution)/shard_map/ppermute | solution.py:281
  25.1 2.7 %collective-permute-start.7 = (bf16[1,128,1024]{2,1,0:T(8,128)(2,1)S(1)}, bf16[1,128,1024]{2,1,0:T(8,128)(2,1)S(1)}, u32[]{:S(2)}, u32[]{:S(2)}) collective-permute-start(bf16[1,128,1024]{2,1,0:T(8,128)(2,1)S(1)} %collective-permute-done.2.rest_4_), channel_id=1, source_target_pairs={{0,16},{16,0},{32,48},{48,32},{64,80},{80,64},{96,112},{112,96},{1... | collective-permute-start | bytes 786440 | tf_op jit(solution)/shard_map/ppermute | solution.py:281
  25.2 2.6 %collective-permute-start.8 = (bf16[1,128,1024]{2,1,0:T(8,128)(2,1)S(1)}, bf16[1,128,1024]{2,1,0:T(8,128)(2,1)S(1)}, u32[]{:S(2)}, u32[]{:S(2)}) collective-permute-start(bf16[1,128,1024]{2,1,0:T(8,128)(2,1)S(1)} %collective-permute-done.1.rest_5_), channel_id=1, source_target_pairs={{0,16},{16,0},{32,48},{48,32},{64,80},{80,64},{96,112},{112,96},{1... | collective-permute-start | bytes 786440 | tf_op jit(solution)/shard_map/ppermute | solution.py:281
  25.6 2.2 %collective-permute-start.9 = (bf16[1,128,1024]{2,1,0:T(8,128)(2,1)S(1)}, bf16[1,128,1024]{2,1,0:T(8,128)(2,1)S(1)}, u32[]{:S(2)}, u32[]{:S(2)}) collective-permute-start(bf16[1,128,1024]{2,1,0:T(8,128)(2,1)S(1)} %collective-permute-done.3.rest_8_), channel_id=1, source_target_pairs={{0,16},{16,0},{32,48},{48,32},{64,80},{80,64},{96,112},{112,96},{1... | collective-permute-start | bytes 786440 | tf_op jit(solution)/shard_map/ppermute | solution.py:281
  26.4 1.7 %collective-permute-start.10 = (bf16[1,128,1024]{2,1,0:T(8,128)(2,1)S(1)}, bf16[1,128,1024]{2,1,0:T(8,128)(2,1)S(1)}, u32[]{:S(2)}, u32[]{:S(2)}) collective-permute-start(bf16[1,128,1024]{2,1,0:T(8,128)(2,1)S(1)} %collective-permute-done.4.rest_9_), channel_id=1, source_target_pairs={{0,16},{16,0},{32,48},{48,32},{64,80},{80,64},{96,112},{112,96},{1... | collective-permute-start | bytes 786440 | tf_op jit(solution)/shard_map/ppermute | solution.py:281
  26.5 0.7 copy-start.3
